TPU v7x, 256 devices: a whole 4x4x8 slice. The times are simulated.
256 devices in a mesh: col: 4 (over z_hi), row: 64 (over x, z_lo, y, core).
Axes of the slice: x: 4, y: 4, z: 8 (z_hi: 4, z_lo: 2; z = z_hi * 2 + z_lo), core: 2. Of those that a mesh axis runs over, the one named last changes fastest.
Arguments:
- tokens: bfloat16 [128, 16384], P(None, 'row'), may hold values from -6 to 6
- output_gradient: bfloat16 [128, 16384], P(None, 'row'), may hold values from -3 to 3
- gate_values: bfloat16 [16384, 26624], P('row', 'col'), may hold values from -0.125 to 0.125
- gate_scales: float32 [128, 208], P('row', 'col'), may hold values from 0.5 to 2
- up_values: bfloat16 [16384, 26624], P('row', 'col'), may hold values from -0.125 to 0.125
- up_scales: float32 [128, 208], P('row', 'col'), may hold values from 0.5 to 2
- down_values: bfloat16 [26624, 16384], P('col', 'row'), may hold values from -0.109375 to 0.109375
- down_scales: float32 [208, 128], P('col', 'row'), may hold values from 0.5 to 2
- gate_reduce_factor: bfloat16 [64, 16384], P(None, 'row'), may hold values from -0.09375 to 0.09375
- gate_expand: bfloat16 [64, 26624], P(None, ('col', 'row')), may hold values from -0.09375 to 0.09375
- up_reduce_factor: bfloat16 [64, 16384], P(None, 'row'), may hold values from -0.09375 to 0.09375
- up_expand: bfloat16 [64, 26624], P(None, ('col', 'row')), may hold values from -0.09375 to 0.09375
- down_reduce: bfloat16 [64, 26624], P(None, ('col', 'row')), may hold values from -0.09375 to 0.09375
- down_expand: bfloat16 [64, 16384], P(None, 'row'), may hold values from -0.046875 to 0.046875
Outputs:
- input_gradient: bfloat16 [128, 16384], P('col', 'row')
- gate_reduce_gradient: float32 [64, 16384], P(None, 'row')
- gate_expand_gradient: float32 [64, 26624], P(None, ('col', 'row'))
- up_reduce_gradient: float32 [64, 16384], P(None, 'row')
- up_expand_gradient: float32 [64, 26624], P(None, ('col', 'row'))
- down_reduce_gradient: float32 [64, 26624], P(None, ('col', 'row'))
- down_expand_gradient: float32 [64, 16384], P(None, 'row')
All inputs are finite; a program needn't handle non-finite values.
Results may differ from a plain program's by a relative error of at most 0.017.
Values may be sent and summed in bfloat16 or wider, within the bound.
No kernel may reach another device: no remote copies, remote signals or barrier semaphores. Data moves between devices by JAX's collectives and lax.ppermute only.
A program may use at most 128 MiB of HBM per device.

v0:
```python
import jax
import jax.numpy as jnp
from jax import lax
from jax.sharding import PartitionSpec as P

BLOCK = 128


adapter_scale = 0.5


def dequantize(values, scales):
    height, breadth = values.shape
    blocks = values.astype(jnp.float32).reshape(height // BLOCK, BLOCK, breadth // BLOCK, BLOCK)
    return (blocks * scales[:, None, :, None]).reshape(height, breadth).astype(jnp.bfloat16)


def contract_matrices(left, right, left_dim, right_dim):
    return lax.dot_general(
        left, right, (((left_dim,), (right_dim,)), ((), ())), preferred_element_type=jnp.float32
    )


def matrix_multiply(left, right):
    return jnp.dot(left, right, preferred_element_type=jnp.float32)


def swiglu_back(gate_preact, upper_preact, backward_result):
    sigma = jax.nn.sigmoid(gate_preact)
    activated = gate_preact * sigma
    hidden_state = (activated * upper_preact).astype(jnp.bfloat16)
    gate_gradient = (
        backward_result * upper_preact * sigma * (1.0 + gate_preact * (1.0 - sigma))
    ).astype(jnp.bfloat16)
    upper_gradient = (backward_result * activated).astype(jnp.bfloat16)
    return (hidden_state, gate_gradient, upper_gradient)


def per_device(
    tokens,
    output_gradient,
    gate_values,
    gate_scales,
    up_values,
    up_scales,
    down_values,
    down_scales,
    gate_reduce_factor,
    gate_expand,
    up_reduce_factor,
    up_expand,
    down_reduce,
    down_expand,
):
    piece = gate_expand.shape[1]
    position = lax.axis_index("row")
    low_sums = lax.psum(
        (
            contract_matrices(tokens, gate_reduce_factor, 1, 1),
            contract_matrices(tokens, up_reduce_factor, 1, 1),
            contract_matrices(output_gradient, down_expand, 1, 1),
        ),
        "row",
    )
    gate_lowrank = low_sums[0].astype(jnp.bfloat16)
    up_lowrank = low_sums[1].astype(jnp.bfloat16)
    down_lowrank = low_sums[2].astype(jnp.bfloat16)
    gate_weight = dequantize(gate_values, gate_scales)
    up_weight = dequantize(up_values, up_scales)
    down_weight = dequantize(down_values, down_scales)
    offset = position * piece
    base = jnp.stack(
        [
            matrix_multiply(tokens, gate_weight),
            matrix_multiply(tokens, up_weight),
            contract_matrices(output_gradient, down_weight, 1, 1),
        ],
        axis=1,
    )
    extra_term = adapter_scale * jnp.stack(
        [
            matrix_multiply(gate_lowrank, gate_expand),
            matrix_multiply(up_lowrank, up_expand),
            matrix_multiply(down_lowrank, down_reduce),
        ],
        axis=1,
    )
    current = lax.dynamic_slice_in_dim(base, offset, piece, 2)
    sums = lax.psum_scatter(
        lax.dynamic_update_slice_in_dim(base, current + extra_term, offset, 2),
        "row",
        scatter_dimension=0,
        tiled=True,
    )
    hidden_state, gate_gradient, upper_gradient = swiglu_back(sums[:, 0], sums[:, 1], sums[:, 2])
    all_hidden, all_gate, all_upper = (
        lax.all_gather(hidden_state, "row", axis=0, tiled=True),
        lax.all_gather(gate_gradient, "row", axis=0, tiled=True),
        lax.all_gather(upper_gradient, "row", axis=0, tiled=True),
    )
    input_portion = contract_matrices(all_gate, gate_weight, 1, 1) + contract_matrices(
        all_upper, up_weight, 1, 1
    )
    hidden_column_block = lax.dynamic_slice_in_dim(all_hidden, offset, piece, 1)
    gate_column_block = lax.dynamic_slice_in_dim(all_gate, offset, piece, 1)
    upper_column_block = lax.dynamic_slice_in_dim(all_upper, offset, piece, 1)
    gate_part, up_part, hidden_part = lax.psum(
        (
            contract_matrices(gate_column_block, gate_expand, 1, 1),
            contract_matrices(upper_column_block, up_expand, 1, 1),
            contract_matrices(hidden_column_block, down_reduce, 1, 1),
        ),
        ("col", "row"),
    )
    gate_expand_gradient = adapter_scale * contract_matrices(gate_lowrank, gate_column_block, 0, 0)
    up_expand_gradient = adapter_scale * contract_matrices(up_lowrank, upper_column_block, 0, 0)
    down_reduce_gradient = adapter_scale * contract_matrices(
        down_lowrank, hidden_column_block, 0, 0
    )
    gate_total_sum = gate_part.astype(jnp.bfloat16)
    up_total_sum = up_part.astype(jnp.bfloat16)
    hidden_total_sum = hidden_part.astype(jnp.bfloat16)
    input_summed_total = lax.psum_scatter(
        input_portion.astype(jnp.bfloat16), "col", scatter_dimension=0, tiled=True
    ).astype(jnp.float32)
    share = input_summed_total.shape[0]
    first = lax.axis_index("col") * share
    gate_row_block = lax.dynamic_slice_in_dim(gate_total_sum, first, share, 0)
    up_row_block = lax.dynamic_slice_in_dim(up_total_sum, first, share, 0)
    input_gradient = (
        input_summed_total
        + adapter_scale
        * (
            matrix_multiply(gate_row_block, gate_reduce_factor)
            + matrix_multiply(up_row_block, up_reduce_factor)
        )
    ).astype(jnp.bfloat16)
    gate_reduce_gradient = adapter_scale * contract_matrices(gate_total_sum, tokens, 0, 0)
    up_reduce_gradient = adapter_scale * contract_matrices(up_total_sum, tokens, 0, 0)
    down_expand_gradient = adapter_scale * contract_matrices(
        hidden_total_sum, output_gradient, 0, 0
    )
    return (
        input_gradient,
        gate_reduce_gradient,
        gate_expand_gradient,
        up_reduce_gradient,
        up_expand_gradient,
        down_reduce_gradient,
        down_expand_gradient,
    )


def solution(mesh):
    in_specs = (
        P(None, "row"),
        P(None, "row"),
        P("row", "col"),
        P("row", "col"),
        P("row", "col"),
        P("row", "col"),
        P("col", "row"),
        P("col", "row"),
        P(None, "row"),
        P(None, ("col", "row")),
        P(None, "row"),
        P(None, ("col", "row")),
        P(None, ("col", "row")),
        P(None, "row"),
    )
    out_specs = (
        P("col", "row"),
        P(None, "row"),
        P(None, ("col", "row")),
        P(None, "row"),
        P(None, ("col", "row")),
        P(None, ("col", "row")),
        P(None, "row"),
    )
    return jax.shard_map(
        per_device, mesh=mesh, in_specs=in_specs, out_specs=out_specs, check_vma=False
    )
```

profile of v0, /device:TPU:1, one launch (start us, length us, event | category | flops | bytes accessed | tf_op | source)
XLA Modules:
  0.0 1355.3 jit_solution(15070146667612088314)
XLA Ops:
  8.6 4.8 copy.32
  14.3 6.1 copy.30
  22.7 2.6 mul.93
  25.3 3.3 convolution_bitcast_fusion.1
  29.0 1.8 mul.90
  30.9 7.4 convolution_bitcast_fusion.2
  39.1 1.8 mul.96
  41.0 2.9 convolution_bitcast_fusion
  43.9 275.9 %all-reduce.2 = (bf16[128,64]{0,1:T(8,128)(2,1)}, bf16[128,64]{0,1:T(8,128)(2,1)}, bf16[128,64]{0,1:T(8,128)(2,1)}) all-reduce(f32[128,64]{0,1:T(8,128)} %fusion.53, f32[128,64]{0,1:T(8,128)} %fusion.52, f32[128,64]{0,1:T(8,128)} %fusion.51), channel_id=1, replica_groups=mesh['col'=4,'row'=64] {'row'}, use_global_device_ids=true, to_apply=%region_2.0 | all-reduce | flops 24576 | bytes 147456 | tf_op jit(solution)/shard_map/psum | solution.py:57
  322.6 7.5 pad_maximum_fusion
  330.1 1.6 fusion.9
  331.7 15.0 %copy.35 = f32[128,3,6656]{2,1,0:T(4,128)} copy(f32[128,3,6656]{0,2,1:T(8,128)} %fusion.9) | data formatting | bytes 20447232 | tf_op jit(solution)/shard_map/dynamic_update_slice | solution.py:90
  348.6 593.2 %all-reduce.5.cloned.1.call-done = f32[128,3,6656]{2,1,0:T(4,128)} async-done(((f32[128,3,6656]{2,1,0:T(4,128)}), f32[128,3,6656]{2,1,0:T(4,128)}) %all-reduce.5.cloned.1.call-update) | async-done | bytes 10223632
  945.5 105.0 %all-gather.7.cloned.1.call-done = bf16[64,2,6656]{2,1,0:T(2,128)(2,1)} async-done(((bf16[1,2,6656]{2,1,0:T(2,128)(2,1)}), bf16[64,2,6656]{2,1,0:T(2,128)(2,1)}) %all-gather.7.cloned.1.call-update) | async-done | bytes 1703952 | tf_op jit(solution)/shard_map/all_gather | solution.py:98
  1050.4 4.7 reshape.27
  1055.2 102.0 %all-gather.9.cloned.1.call-done = bf16[64,2,6656]{2,1,0:T(2,128)(2,1)} async-done(((bf16[1,2,6656]{2,1,0:T(2,128)(2,1)}), bf16[64,2,6656]{2,1,0:T(2,128)(2,1)}) %all-gather.9.cloned.1.call-update) | async-done | bytes 1703952 | tf_op jit(solution)/shard_map/all_gather | solution.py:99
  1157.2 4.9 reshape.29
  1163.1 1.7 convolution_multiply_fusion.4
  1165.9 1.7 convolution_multiply_fusion.5
  1167.6 5.3 fusion.46
  1176.1 87.8 %all-gather.11.cloned.1.call-done = bf16[64,2,6656]{2,1,0:T(2,128)(2,1)} async-done(((bf16[1,2,6656]{2,1,0:T(2,128)(2,1)}), bf16[64,2,6656]{2,1,0:T(2,128)(2,1)}) %all-gather.11.cloned.1.call-update) | async-done | bytes 1703952 | tf_op jit(solution)/shard_map/all_gather | solution.py:97
  1263.9 3.9 reshape.31
  1268.0 75.8 %all-reduce.1 = (bf16[128,64]{0,1:T(8,128)(2,1)S(1)}, bf16[128,64]{0,1:T(8,128)(2,1)S(1)}, bf16[128,64]{0,1:T(8,128)(2,1)S(1)}) all-reduce(f32[128,64]{0,1:T(8,128)S(1)} %fusion.23, f32[128,64]{0,1:T(8,128)S(1)} %fusion.20, f32[128,64]{0,1:T(8,128)S(1)} %fusion.16), channel_id=1, replica_groups=mesh['col'=4,'row'=64] {'col','row'}, use_global_device_ids=true, to_apply=%region_5.0 | all-reduce | flops 24576 | bytes 147456 | tf_op jit(solution)/shard_map/psum | solution.py:107
  1347.2 1.6 fusion.7
  (87 shorter events, 22.5 us)
Async XLA Ops:
  7.2 14.0 %copy-start = (bf16[128,256]{1,0:T(8,128)(2,1)S(1)}, bf16[128,256]{1,0:T(8,128)(2,1)}, u32[]{:S(2)}) copy-start(bf16[128,256]{1,0:T(8,128)(2,1)} %param.14) | copy-start | bytes 196612
  7.2 934.6 %all-reduce.5.cloned.1.call-start = ((), (), s32[]{:S(2)}) async-start(), calls=%async_computation.5 | async-start | bytes 27262976
  13.4 11.9 copy-start.3
  14.3 6.9 copy-start.11
  14.3 7.6 copy-start.9
  30.8 7.4 copy-start.2
  30.9 7.4 copy-start.8
  30.9 7.4 copy-start.21
  30.9 8.2 copy-start.13
  41.0 279.7 %copy-start.15 = (bf16[64,104]{1,0:T(8,128)(2,1)S(1)}, bf16[64,104]{1,0:T(8,128)(2,1)}, u32[]{:S(2)}) copy-start(bf16[64,104]{1,0:T(8,128)(2,1)} %param.25) | copy-start | bytes 39940
  41.0 281.6 %copy-start.5 = (f32[128,1,6656]{0,2,1:T(8,128)S(1)}, f32[128,1,6656]{0,2,1:T(8,128)}, u32[]{:S(2)}) copy-start(f32[128,1,6656]{0,2,1:T(8,128)} %convolution_bitcast_fusion.1) | copy-start | bytes 10223620
  346.7 703.7 %all-gather.7.cloned.1.call-start = ((), (), s32[]{:S(2)}) async-start(), calls=%async_computation.2 | async-start | bytes 1730560 | tf_op jit(solution)/shard_map/all_gather | solution.py:98
  943.9 213.3 %all-gather.9.cloned.1.call-start = ((), (), s32[]{:S(2)}) async-start(), calls=%async_computation.3 | async-start | bytes 1730560 | tf_op jit(solution)/shard_map/all_gather | solution.py:99
  944.6 319.2 %all-gather.11.cloned.1.call-start = ((), (), s32[]{:S(2)}) async-start(), calls=%async_computation.4 | async-start | bytes 1730560 | tf_op jit(solution)/shard_map/all_gather | solution.py:97
  945.2 401.9 %reduce-scatter.2.cloned.1.call-start = ((), (), s32[]{:S(2)}) async-start(), calls=%async_computation.1 | async-start | bytes 81920 | tf_op jit(solution)/shard_map/reduce_scatter | solution.py:123
  945.5 217.7 %copy-start.20 = (bf16[128,64]{0,1:T(8,128)(2,1)S(1)}, bf16[128,64]{0,1:T(8,128)(2,1)}, u32[]{:S(2)}) copy-start(bf16[128,64]{0,1:T(8,128)(2,1)} %get-tuple-element.11) | copy-start | bytes 49156
  945.5 219.4 %copy-start.16 = (bf16[64,104]{1,0:T(8,128)(2,1)S(1)}, bf16[64,104]{1,0:T(8,128)(2,1)}, u32[]{:S(2)}) copy-start(bf16[64,104]{1,0:T(8,128)(2,1)} %param.23) | copy-start | bytes 39940
  945.5 220.4 %copy-start.19 = (bf16[128,64]{0,1:T(8,128)(2,1)S(1)}, bf16[128,64]{0,1:T(8,128)(2,1)}, u32[]{:S(2)}) copy-start(bf16[128,64]{0,1:T(8,128)(2,1)} %get-tuple-element.12) | copy-start | bytes 49156
  1157.2 15.7 %slice-start = ((s8[6815744]{0:T(1024)(128)(4,1)}), s8[2621440]{0:T(1024)(128)(4,1)S(1)}, s32[]{:S(2)}) async-start(s8[6815744]{0:T(1024)(128)(4,1)} %bitcast.132), calls=%async_computation.6 | async-start | bytes 5242880
  1167.6 7.1 copy-start.6
  1176.1 91.7 %copy-start.17 = (bf16[64,104]{1,0:T(8,128)(2,1)S(1)}, bf16[64,104]{1,0:T(8,128)(2,1)}, u32[]{:S(2)}) copy-start(bf16[64,104]{1,0:T(8,128)(2,1)} %param.26) | copy-start | bytes 39940
  1176.1 168.5 %copy-start.12 = (bf16[64,256]{1,0:T(8,128)(2,1)S(1)}, bf16[64,256]{1,0:T(8,128)(2,1)}, u32[]{:S(2)}) copy-start(bf16[64,256]{1,0:T(8,128)(2,1)} %param.22) | copy-start | bytes 98308
  1176.1 170.3 %copy-start.18 = (bf16[128,64]{0,1:T(8,128)(2,1)S(1)}, bf16[128,64]{0,1:T(8,128)(2,1)}, u32[]{:S(2)}) copy-start(bf16[128,64]{0,1:T(8,128)(2,1)} %get-tuple-element.10) | copy-start | bytes 49156
  1176.1 171.1 %copy-start.10 = (bf16[64,256]{1,0:T(8,128)(2,1)S(1)}, bf16[64,256]{1,0:T(8,128)(2,1)}, u32[]{:S(2)}) copy-start(bf16[64,256]{1,0:T(8,128)(2,1)} %param.24) | copy-start | bytes 98308
  (8 other events, 33.4 us)
Sparse Core Ops, SparseCore 0:
  346.8 594.9 all-reduce.4
  944.4 106.0 all-gather.6
  1053.0 104.1 all-gather.8
  1159.7 104.1 all-gather.10
  1266.3 21.2 reduce-scatter.1
where the time goes:
time: 1360 us
  waiting for transfers between devices  889 us (65%)
  blocking collectives  352 us (26%)
  local copies, waits for them, and re-layouts  53.5 us (4%)
  matrix products  36 us (3%)
  between operations  14.7 us (1%)
    unnamed x6, waiting for transfers between devices  594 us
    psum x1, blocking collectives, per_device(): lax.psum((contract_matrices(tokens, gate_reduce_factor, 1, 1), contract_m...  276 us
    all_gather x1, waiting for transfers between devices, per_device(): lax.all_gather(gate_gradient, 'row', axis=0, tiled=True)  105 us
    all_gather x1, waiting for transfers between devices, per_device(): lax.all_gather(upper_gradient, 'row', axis=0, tiled=True)  102 us
    all_gather x1, waiting for transfers between devices, per_device(): lax.all_gather(hidden_state, 'row', axis=0, tiled=True)  87.8 us
    psum x1, blocking collectives, per_device(): lax.psum((contract_matrices(gate_column_block, gate_expand, 1, 1), contra...  75.8 us
    unnamed x63, local copies, waits for them, and re-layouts  31 us
  transfers between devices with their start and end apart: 5, of which 4 were waited for; matrix products, arithmetic and copies ran while one was open for 2% of the time, Pallas kernels for 0%

commit v1 on v0

v1 whole, which is shorter than its diff:
```python
import functools

import jax
import jax.numpy as jnp
from jax import lax
from jax.experimental import pallas as pl
from jax.experimental.pallas import tpu as pltpu
from jax.sharding import PartitionSpec as P

BLOCK = 128
SCALE = 0.5
STEPS = 4
BF16 = jnp.bfloat16
F32 = jnp.float32
LIMIT = 24 * 1024 * 1024


def params():
    return pltpu.CompilerParams(vmem_limit_bytes=LIMIT)


def dot(left, right, left_dim, right_dim):
    return lax.dot_general(
        left, right, (((left_dim,), (right_dim,)), ((), ())), preferred_element_type=F32
    )


def whole(shape):
    return pl.BlockSpec(shape, lambda *_: (0,) * len(shape))


def smem():
    return pl.BlockSpec(memory_space=pltpu.SMEM)


def dequantize_wide(values_ref, scales_ref, first, weight_ref):
    for block in range(values_ref.shape[1] // BLOCK):
        columns = pl.ds(block * BLOCK, BLOCK)
        for part in range(values_ref.shape[0] // BLOCK):
            rows = pl.ds(part * BLOCK, BLOCK)
            scale = scales_ref[part, first + block]
            weight_ref[rows, columns] = (values_ref[rows, columns].astype(F32) * scale).astype(BF16)


def dequantize_tall(values_ref, scales_ref, first, weight_ref):
    for block in range(values_ref.shape[0] // BLOCK):
        rows = pl.ds(block * BLOCK, BLOCK)
        for part in range(values_ref.shape[1] // BLOCK):
            columns = pl.ds(part * BLOCK, BLOCK)
            scale = scales_ref[first + block, part]
            weight_ref[rows, columns] = (values_ref[rows, columns].astype(F32) * scale).astype(BF16)


def partial_kernel(tall, where_ref, scales_ref, inputs_ref, values_ref, send_ref, keep_ref, weight_ref, sums_ref):
    core = where_ref[0]
    blocks = weight_ref.shape[0 if tall else 1] // BLOCK
    first = pl.program_id(0) * blocks
    if tall:
        dequantize_tall(values_ref, scales_ref, first, weight_ref)
        sums_ref[...] = dot(weight_ref[...], inputs_ref[...], 1, 1)
    else:
        dequantize_wide(values_ref, scales_ref, first, weight_ref)
        product = dot(inputs_ref[...], weight_ref[...], 1, 0)
        sums_ref[...] = product.T
    chips, piece = send_ref.shape[:2]
    for chip in range(chips):
        start = chip * 2 * piece
        mine = pl.multiple_of(start + core * piece, 8)
        theirs = pl.multiple_of(start + (1 - core) * piece, 8)
        keep_ref[chip] = sums_ref[pl.ds(mine, piece), :].astype(BF16)
        send_ref[chip] = sums_ref[pl.ds(theirs, piece), :].astype(BF16)


def partial_sums(tall, where, scales, inputs, values, piece):
    hidden = values.shape[0 if tall else 1]
    width = values.shape[1 if tall else 0]
    part = hidden // STEPS
    chips = hidden // (2 * piece)
    tokens = inputs.shape[0]
    out = jax.ShapeDtypeStruct((chips, piece, tokens), BF16)
    block = pl.BlockSpec((chips // STEPS, piece, tokens), lambda i: (i, 0, 0))
    values_block = (
        pl.BlockSpec((part, width), lambda i: (i, 0))
        if tall
        else pl.BlockSpec((width, part), lambda i: (0, i))
    )
    return pl.pallas_call(
        functools.partial(partial_kernel, tall),
        grid=(STEPS,),
        in_specs=[smem(), smem(), whole(inputs.shape), values_block],
        out_specs=[block, block],
        out_shape=[out, out],
        scratch_shapes=[
            pltpu.VMEM((part, width) if tall else (width, part), BF16),
            pltpu.VMEM((part, tokens), F32),
        ],
        compiler_params=params(),
        cost_estimate=pl.CostEstimate(
            flops=2 * tokens * width * hidden, bytes_accessed=2 * width * hidden, transcendentals=0
        ),
    )(where, scales, inputs, values)


def low_kernel(where_ref, tokens_ref, gradient_ref, gate_ref, up_ref, down_ref, send_ref, keep_ref, low_ref):
    core = where_ref[0]
    half = low_ref.shape[1] // 2
    low_ref[0] = dot(gate_ref[...], tokens_ref[...], 1, 1)
    low_ref[1] = dot(up_ref[...], tokens_ref[...], 1, 1)
    low_ref[2] = dot(down_ref[...], gradient_ref[...], 1, 1)
    mine = pl.multiple_of(core * half, half)
    theirs = pl.multiple_of((1 - core) * half, half)
    for kind in range(3):
        keep_ref[kind] = low_ref[kind, pl.ds(mine, half), :].astype(BF16)
        send_ref[kind] = low_ref[kind, pl.ds(theirs, half), :].astype(BF16)


def low_partials(where, tokens, gradient, gate_reduce, up_reduce, down_expand):
    rank, count = gate_reduce.shape[0], tokens.shape[0]
    out = jax.ShapeDtypeStruct((3, rank // 2, count), BF16)
    return pl.pallas_call(
        low_kernel,
        in_specs=[smem()] + [pl.BlockSpec(memory_space=pltpu.VMEM)] * 5,
        out_specs=[pl.BlockSpec(memory_space=pltpu.VMEM)] * 2,
        out_shape=[out, out],
        scratch_shapes=[pltpu.VMEM((3, rank, count), F32)],
        compiler_params=params(),
    )(where, tokens, gradient, gate_reduce, up_reduce, down_expand)


def pack_kernel(*refs):
    keeps, received, out_ref = refs[:4], refs[4:8], refs[8]
    low = (keeps[3][...].astype(F32) + received[3][...].astype(F32)).reshape(-1, out_ref.shape[2])
    for chip in range(out_ref.shape[0]):
        parts = [keeps[k][chip].astype(F32) + received[k][chip].astype(F32) for k in range(3)]
        out_ref[chip] = jnp.concatenate(parts + [low], axis=0).astype(BF16)


def pack(keeps, received):
    chips, piece, tokens = keeps[0].shape
    low_shape = keeps[3].shape
    rows = 3 * piece + low_shape[0] * low_shape[1]
    block = pl.BlockSpec((chips // STEPS, piece, tokens), lambda i: (i, 0, 0))
    specs = [block] * 3 + [whole(low_shape)]
    return pl.pallas_call(
        pack_kernel,
        grid=(STEPS,),
        in_specs=specs + specs,
        out_specs=pl.BlockSpec((chips // STEPS, rows, tokens), lambda i: (i, 0, 0)),
        out_shape=jax.ShapeDtypeStruct((chips, rows, tokens), BF16),
        compiler_params=params(),
    )(*keeps, *received)


def total_kernel(parts_ref, sums_ref, low_ref):
    rows = sums_ref.shape[0]

    def add(first, count):
        total = parts_ref[0, first : first + count].astype(F32)
        for chip in range(1, parts_ref.shape[0]):
            total = total + parts_ref[chip, first : first + count].astype(F32)
        return total

    for first in range(0, rows, 104):
        sums_ref[first : first + 104] = add(first, 104)
    low_ref[...] = add(rows, low_ref.shape[0]).astype(BF16)


def total(parts, rows):
    _, everything, tokens = parts.shape
    return pl.pallas_call(
        total_kernel,
        in_specs=[pl.BlockSpec(memory_space=pltpu.VMEM)],
        out_specs=[pl.BlockSpec(memory_space=pltpu.VMEM)] * 2,
        out_shape=[
            jax.ShapeDtypeStruct((rows, tokens), F32),
            jax.ShapeDtypeStruct((everything - rows, tokens), BF16),
        ],
        compiler_params=params(),
    )(parts)


def middle_kernel(
    where_ref, sums_ref, mine_ref, theirs_ref, gate_expand_ref, up_expand_ref, down_reduce_ref,
    send_ref, keep_ref, gate_out, up_out, down_out, low_ref, rank_ref,
):
    core = where_ref[0]
    piece = gate_expand_ref.shape[1]
    half = low_ref.shape[1] // 2
    mine = pl.multiple_of(core * half, half)
    theirs = pl.multiple_of((1 - core) * half, half)
    for kind in range(3):
        low_ref[kind, pl.ds(mine, half), :] = mine_ref[kind * half : (kind + 1) * half].astype(F32)
        low_ref[kind, pl.ds(theirs, half), :] = theirs_ref[kind * half : (kind + 1) * half].astype(F32)
    expands = [gate_expand_ref[...], up_expand_ref[...], down_reduce_ref[...]]
    lows = [low_ref[kind].astype(BF16) for kind in range(3)]
    gate, upper, back = [
        sums_ref[kind * piece : (kind + 1) * piece] + SCALE * dot(expands[kind], lows[kind], 0, 0)
        for kind in range(3)
    ]
    sigma = jax.nn.sigmoid(gate)
    activated = gate * sigma
    hidden = (activated * upper).astype(BF16)
    grad_gate = (back * upper * sigma * (1.0 + gate * (1.0 - sigma))).astype(BF16)
    grad_upper = (back * activated).astype(BF16)
    gate_out[...] = SCALE * dot(lows[0], grad_gate, 1, 1)
    up_out[...] = SCALE * dot(lows[1], grad_upper, 1, 1)
    down_out[...] = SCALE * dot(lows[2], hidden, 1, 1)
    rank_ref[0] = dot(expands[0], grad_gate, 1, 0)
    rank_ref[1] = dot(expands[1], grad_upper, 1, 0)
    rank_ref[2] = dot(expands[2], hidden, 1, 0)
    first = core == 0
    keep_rows = [jnp.where(first, grad_gate.astype(F32), grad_upper.astype(F32))]
    send_rows = [jnp.where(first, grad_upper.astype(F32), grad_gate.astype(F32))]
    for kind in range(3):
        keep_rows.append(rank_ref[kind, pl.ds(mine, half), :])
        send_rows.append(rank_ref[kind, pl.ds(theirs, half), :])
    keep_ref[...] = jnp.concatenate(keep_rows, axis=0)
    send_ref[...] = jnp.concatenate(send_rows, axis=0).astype(BF16)


def middle(where, sums, mine, theirs, gate_expand, up_expand, down_reduce):
    rank, piece = gate_expand.shape
    tokens = sums.shape[1]
    rows = piece + 3 * rank // 2
    vmem = pl.BlockSpec(memory_space=pltpu.VMEM)
    return pl.pallas_call(
        middle_kernel,
        in_specs=[smem()] + [vmem] * 6,
        out_specs=[vmem] * 5,
        out_shape=[
            jax.ShapeDtypeStruct((rows, tokens), BF16),
            jax.ShapeDtypeStruct((rows, tokens), F32),
        ]
        + [jax.ShapeDtypeStruct((rank, piece), F32)] * 3,
        scratch_shapes=[pltpu.VMEM((3, rank, tokens), F32), pltpu.VMEM((3, rank, tokens), F32)],
        compiler_params=params(),
    )(where, sums, mine, theirs, gate_expand, up_expand, down_reduce)


def spread_kernel(piece, where_ref, keep_ref, received_ref, out_ref):
    first = where_ref[0] == 0
    kept = keep_ref[:piece]
    arrived = received_ref[:piece].astype(F32)
    block = jnp.concatenate(
        [
            jnp.where(first, kept, arrived),
            jnp.where(first, arrived, kept),
            keep_ref[piece:] + received_ref[piece:].astype(F32),
        ],
        axis=0,
    ).astype(BF16)
    for chip in range(out_ref.shape[0]):
        out_ref[chip] = block


def spread(where, keep, received, piece, chips):
    rows, tokens = keep.shape
    vmem = pl.BlockSpec(memory_space=pltpu.VMEM)
    return pl.pallas_call(
        functools.partial(spread_kernel, piece),
        in_specs=[smem(), vmem, vmem],
        out_specs=vmem,
        out_shape=jax.ShapeDtypeStruct((chips, rows + piece, tokens), BF16),
        compiler_params=params(),
    )(where, keep, received)


def back_kernel(last, *refs):
    if last:
        (where_ref, gate_scales, up_scales, grads_ref, gate_ref, up_ref, before_ref, before_rank_ref,
         own_ref, *to_refs, weight_ref, total_ref, rank_ref, turned_ref) = refs
    else:
        (where_ref, gate_scales, up_scales, grads_ref, gate_ref, up_ref,
         total_ref, rank_ref, weight_ref) = refs
    step = pl.program_id(0)
    gate_turn = where_ref[0] == (1 if last else 0)
    blocks = weight_ref.shape[1] // BLOCK
    first = step * blocks
    unit_rows = weight_ref.shape[1] // grads_ref.shape[0]

    @pl.when(gate_turn)
    def _():
        dequantize_wide(gate_ref, gate_scales, first, weight_ref)

    @pl.when(jnp.logical_not(gate_turn))
    def _():
        dequantize_wide(up_ref, up_scales, first, weight_ref)

    grads = jnp.concatenate([grads_ref[chip, :unit_rows] for chip in range(grads_ref.shape[0])], axis=0)
    product = dot(weight_ref[...], grads, 1, 0)
    rank = grads_ref[0, unit_rows:].astype(F32)
    for chip in range(1, grads_ref.shape[0]):
        rank = rank + grads_ref[chip, unit_rows:].astype(F32)

    @pl.when(step == 0)
    def _():
        total_ref[...] = product + before_ref[...] if last else product
        rank_ref[...] = rank

    @pl.when(step > 0)
    def _():
        total_ref[...] += product
        rank_ref[...] += rank

    if last:

        @pl.when(step == pl.num_programs(0) - 1)
        def _():
            core, column = where_ref[0], where_ref[1]
            turned_ref[...] = total_ref[...].T
            half = rank_ref.shape[0] // 3
            mine = [before_rank_ref[k * half : (k + 1) * half] for k in range(3)]
            theirs = [rank_ref[k * half : (k + 1) * half] for k in range(3)]
            rows = []
            for kind in range(3):
                rows.append(jnp.where(core == 0, mine[kind], theirs[kind]))
                rows.append(jnp.where(core == 0, theirs[kind], mine[kind]))
            share = turned_ref.shape[0] // 4
            for offset, out_ref in enumerate([own_ref, *to_refs]):
                start = pl.multiple_of(lax.rem(column + offset, 4) * share, share)
                piece = turned_ref[pl.ds(start, share), :]
                block = jnp.concatenate([piece[:, :BLOCK], piece[:, BLOCK:], *rows], axis=0)
                out_ref[...] = block.astype(BF16)


def back(last, where, gate_scales, up_scales, grads, gate_values, up_values, before=()):
    width, hidden = gate_values.shape
    chips, rows, tokens = grads.shape
    part = hidden // STEPS
    unit_rows = hidden // chips
    rank_rows = rows - unit_rows
    turn = 1 if last else 0
    gate_block = pl.BlockSpec((width, part), lambda i, w, *_: (0, jnp.where(w[0] == turn, i, 0)))
    up_block = pl.BlockSpec((width, part), lambda i, w, *_: (0, jnp.where(w[0] == turn, 0, i)))
    in_specs = [pl.BlockSpec((chips // STEPS, rows, tokens), lambda i, *_: (i, 0, 0)), gate_block, up_block]
    if last:
        in_specs += [whole((width, tokens)), whole((rank_rows, tokens))]
        out_shape = [jax.ShapeDtypeStruct((64 + 2 * rank_rows, tokens), BF16)] * 4
    else:
        out_shape = [
            jax.ShapeDtypeStruct((width, tokens), F32),
            jax.ShapeDtypeStruct((rank_rows, tokens), F32),
        ]
    scratch = [pltpu.VMEM((width, part), BF16)]
    if last:
        scratch += [
            pltpu.VMEM((width, tokens), F32),
            pltpu.VMEM((rank_rows, tokens), F32),
            pltpu.VMEM((tokens, width), F32),
        ]
    return pl.pallas_call(
        functools.partial(back_kernel, last),
        grid_spec=pltpu.PrefetchScalarGridSpec(
            num_scalar_prefetch=3,
            grid=(STEPS,),
            in_specs=in_specs,
            out_specs=[whole(s.shape) for s in out_shape],
            scratch_shapes=scratch,
        ),
        out_shape=out_shape,
        compiler_params=params(),
        cost_estimate=pl.CostEstimate(
            flops=2 * tokens * width * hidden, bytes_accessed=2 * width * hidden, transcendentals=0
        ),
    )(where, gate_scales, up_scales, grads, gate_values, up_values, *before)


def last_kernel(
    where_ref, own_ref, one_ref, two_ref, three_ref, tokens_ref, gradient_ref, gate_reduce_ref, up_reduce_ref,
    input_out, gate_out, up_out, down_out, parts_ref, wide_ref,
):
    column = where_ref[1]
    for offset, ref in enumerate([own_ref, one_ref, two_ref, three_ref]):
        parts_ref[lax.rem(column + 4 - offset, 4)] = ref[...].astype(F32)
    summed = parts_ref[0] + parts_ref[1] + parts_ref[2] + parts_ref[3]
    share = input_out.shape[0]
    rank = gate_out.shape[0]
    sums = [summed[2 * share + k * rank : 2 * share + (k + 1) * rank].astype(BF16) for k in range(3)]
    wide_ref[...] = dot(sums[0], gate_reduce_ref[...], 0, 0) + dot(sums[1], up_reduce_ref[...], 0, 0)
    start = pl.multiple_of(column * share, share)
    main = jnp.concatenate([summed[:share], summed[share : 2 * share]], axis=1)
    input_out[...] = (main + SCALE * wide_ref[pl.ds(start, share), :]).astype(BF16)
    gate_out[...] = SCALE * dot(sums[0], tokens_ref[...], 1, 0)
    up_out[...] = SCALE * dot(sums[1], tokens_ref[...], 1, 0)
    down_out[...] = SCALE * dot(sums[2], gradient_ref[...], 1, 0)


def finish(where, own, others, tokens, gradient, gate_reduce, up_reduce):
    rank, width = gate_reduce.shape
    count = tokens.shape[0]
    vmem = pl.BlockSpec(memory_space=pltpu.VMEM)
    return pl.pallas_call(
        last_kernel,
        in_specs=[smem()] + [vmem] * 8,
        out_specs=[vmem] * 4,
        out_shape=[jax.ShapeDtypeStruct((count // 4, width), BF16)]
        + [jax.ShapeDtypeStruct((rank, width), F32)] * 3,
        scratch_shapes=[pltpu.VMEM((4,) + own.shape, F32), pltpu.VMEM((count, width), F32)],
        compiler_params=params(),
    )(where, own, *others, tokens, gradient, gate_reduce, up_reduce)


def per_device(
    tokens,
    output_gradient,
    gate_values,
    gate_scales,
    up_values,
    up_scales,
    down_values,
    down_scales,
    gate_reduce_factor,
    gate_expand,
    up_reduce_factor,
    up_expand,
    down_reduce,
    down_expand,
):
    piece = gate_expand.shape[1]
    n_row = lax.axis_size("row")
    chips = n_row // 2
    position = lax.axis_index("row")
    where = jnp.stack([position % 2, lax.axis_index("col")]).astype(jnp.int32)
    swap = [(i, i ^ 1) for i in range(n_row)]
    same_core = [[2 * i + core for i in range(chips)] for core in range(2)]

    def exchange(value):
        return lax.ppermute(value, "row", swap)

    def across_chips(value):
        return lax.all_to_all(value, "row", 0, 0, tiled=True, axis_index_groups=same_core)

    sends = [
        partial_sums(False, where, gate_scales, tokens, gate_values, piece),
        partial_sums(False, where, up_scales, tokens, up_values, piece),
        partial_sums(True, where, down_scales, output_gradient, down_values, piece),
        low_partials(where, tokens, output_gradient, gate_reduce_factor, up_reduce_factor, down_expand),
    ]
    received = [exchange(send) for send, _ in sends]
    parts = across_chips(pack([keep for _, keep in sends], received))
    sums, low = total(parts, 3 * piece)
    send, keep, gate_expand_gradient, up_expand_gradient, down_reduce_gradient = middle(
        where, sums, low, exchange(low), gate_expand, up_expand, down_reduce
    )
    mine = across_chips(spread(where, keep, exchange(send), piece, chips))
    theirs = exchange(mine)
    begun = back(False, where, gate_scales, up_scales, mine, gate_values, up_values)
    own, *out = back(True, where, gate_scales, up_scales, theirs, gate_values, up_values, begun)
    others = [
        lax.ppermute(value, "col", [(i, (i + offset) % 4) for i in range(4)])
        for offset, value in zip((1, 2, 3), out)
    ]
    input_gradient, gate_reduce_gradient, up_reduce_gradient, down_expand_gradient = finish(
        where, own, others, tokens, output_gradient, gate_reduce_factor, up_reduce_factor
    )
    return (
        input_gradient,
        gate_reduce_gradient,
        gate_expand_gradient,
        up_reduce_gradient,
        up_expand_gradient,
        down_reduce_gradient,
        down_expand_gradient,
    )


def solution(mesh):
    in_specs = (
        P(None, "row"),
        P(None, "row"),
        P("row", "col"),
        P("row", "col"),
        P("row", "col"),
        P("row", "col"),
        P("col", "row"),
        P("col", "row"),
        P(None, "row"),
        P(None, ("col", "row")),
        P(None, "row"),
        P(None, ("col", "row")),
        P(None, ("col", "row")),
        P(None, "row"),
    )
    out_specs = (
        P("col", "row"),
        P(None, "row"),
        P(None, ("col", "row")),
        P(None, "row"),
        P(None, ("col", "row")),
        P(None, ("col", "row")),
        P(None, "row"),
    )
    return jax.shard_map(
        per_device, mesh=mesh, in_specs=in_specs, out_specs=out_specs, check_vma=False
    )
```

time: 1360 us -> 137 us (0.10)
  waiting for transfers between devices: 889 us -> 8.58 us
  blocking collectives: 352 us -> 83.2 us
  local copies, waits for them, and re-layouts: 53.5 us -> 5.32 us
  matrix products: 36 us -> 0 us
  Pallas kernels: 0 us -> 21.5 us
  starting transfers between devices: 0.38 us -> 17.6 us
  between operations: 14.7 us -> 0.79 us
    unnamed x6 -> x0, waiting for transfers between devices: 594 us -> none
    psum x2 -> x0, blocking collectives: 352 us -> none  [the longest x1 276 us: per_device(): lax.psum((contract_matrices(tokens, gate_reduce_factor, 1, 1), contract_m...]
    all_gather x3 -> x0, waiting for transfers between devices: 295 us -> none  [the longest x1 105 us: per_device(): lax.all_gather(gate_gradient, 'row', axis=0, tiled=True)]
    all_to_all x0 -> x2, blocking collectives: none -> 83.2 us  [across_chips(): lax.all_to_all(value, 'row', 0, 0, tiled=True, axis_index_groups=same_core)]
    dot_general x22 -> x0, matrix products: 36 us -> none  [the longest x15 20.7 us: contract_matrices(): lax.dot_general(left, right, (((left_dim,), (right_dim,)), ((), ())), pre...]
    unnamed x63 -> x33, local copies, waits for them, and re-layouts: 31 us -> 5.32 us
    pallas_call x0 -> x11, Pallas kernels: none -> 21.5 us  [the longest x3 9.18 us: partial_sums(): pl.pallas_call(functools.partial(partial_kernel, tall), grid=(STEPS,), in...]
    ppermute x0 -> x10, starting transfers between devices: none -> 17.6 us  [the longest x3 9.67 us: per_device(): lax.ppermute(value, 'col', [(i, (i + offset) % 4) for i in range(4)])]
  transfers between devices with their start and end apart: 5 -> 10, of which waited for: 4 -> 6; matrix products, arithmetic and copies ran while one was open for 2% -> 0% of each run, Pallas kernels for 0% -> 8%
where the time goes in v1:
time: 137 us
  blocking collectives  83.2 us (61%)
  Pallas kernels  21.5 us (16%)
  starting transfers between devices  17.6 us (13%)
  waiting for transfers between devices  8.58 us (6%)
  local copies, waits for them, and re-layouts  5.32 us (4%)
    all_to_all x2, blocking collectives, across_chips(): lax.all_to_all(value, 'row', 0, 0, tiled=True, axis_index_groups=same_core)  83.2 us
    ppermute x3, starting transfers between devices, per_device(): lax.ppermute(value, 'col', [(i, (i + offset) % 4) for i in range(4)])  9.67 us
    pallas_call x3, Pallas kernels, partial_sums(): pl.pallas_call(functools.partial(partial_kernel, tall), grid=(STEPS,), in...  9.18 us
    ppermute x7, starting transfers between devices, exchange(): return lax.ppermute(value, 'row', swap)  7.91 us
    pallas_call x2, Pallas kernels, back(): pl.pallas_call(functools.partial(back_kernel, last), grid_spec=pltpu.Pref...  6.77 us
    unnamed x33, local copies, waits for them, and re-layouts  5.32 us
    ppermute x3, waiting for transfers between devices, per_device(): lax.ppermute(value, 'col', [(i, (i + offset) % 4) for i in range(4)])  4.69 us
    ppermute x7, waiting for transfers between devices, exchange(): return lax.ppermute(value, 'row', swap)  3.89 us
  transfers between devices with their start and end apart: 10, of which 6 were waited for; matrix products, arithmetic and copies ran while one was open for 0% of the time, Pallas kernels for 8%

profile of v1, /device:TPU:1, one launch (start us, length us, event | category | flops | bytes accessed | tf_op | source)
XLA Modules:
  0.0 137.1 jit_solution(14645405076808767905)
XLA Ops:
  0.7 0.9 copy.21.scales_ref
  1.7 2.0 %copy-done.2 = bf16[6656,256]{1,0:T(8,128)(2,1)S(1)} copy-done((bf16[6656,256]{1,0:T(8,128)(2,1)S(1)}, bf16[6656,256]{1,0:T(8,128)(2,1)}, u32[]{:S(2)}) %copy-start.2) | copy-done | bytes 3407896
  4.5 2.9 %shard_map.191 = (bf16[32,104,128]{2,1,0:T(8,128)(2,1)S(1)}, bf16[32,104,128]{2,1,0:T(8,128)(2,1)S(1)}) custom-call(s32[2]{0:T(128)S(1)} %pad_add_fusion.where_ref.refs_0_, f32[52,2]{1,0:T(8,128)S(1)} %copy.21.scales_ref, bf16[128,256]{1,0:T(8,128)(2,1)S(1)} %copy-done.5, bf16[6656,256]{1,0:T(8,128)(2,1)S(1)} %copy-done.2), custom_call_target="tpu_custom_call" | custom-call | flops 436207616 | bytes 3407872 | tf_op jit(solution)/shard_map/pallas_call | solution.py:87
  7.4 3.3 %collective-permute-start.2 = (bf16[32,104,128]{2,1,0:T(8,128)(2,1)S(1)}, bf16[32,104,128]{2,1,0:T(8,128)(2,1)S(1)}, u32[]{:S(2)}, u32[]{:S(2)}) collective-permute-start(bf16[32,104,128]{2,1,0:T(8,128)(2,1)S(1)} %get-tuple-element.38), channel_id=1, source_target_pairs={{0,1},{1,0},{2,3},{3,2},{4,5},{5,4},{6,7},{7,6},{8,9},{9,8},{10,11... | collective-permute-start | bytes 2555912 | tf_op jit(solution)/shard_map/ppermute | solution.py:428
  10.7 0.8 copy-done.3
  12.2 3.2 %shard_map.189 = (bf16[32,104,128]{2,1,0:T(8,128)(2,1)S(1)}, bf16[32,104,128]{2,1,0:T(8,128)(2,1)S(1)}) custom-call(s32[2]{0:T(128)S(1)} %pad_add_fusion.where_ref.refs_0_, f32[2,52]{1,0:T(2,128)S(1)} %copy-done.13, bf16[128,256]{1,0:T(8,128)(2,1)S(1)} %copy-done.3, bf16[256,6656]{1,0:T(8,128)(2,1)S(1)} %copy-done), custom_call_target="tpu_custom_call" | custom-call | flops 436207616 | bytes 3407872 | tf_op jit(solution)/shard_map/pallas_call | solution.py:87
  15.5 3.2 %shard_map.190 = (bf16[32,104,128]{2,1,0:T(8,128)(2,1)S(1)}, bf16[32,104,128]{2,1,0:T(8,128)(2,1)S(1)}) custom-call(s32[2]{0:T(128)S(1)} %pad_add_fusion.where_ref.refs_0_, f32[2,52]{1,0:T(2,128)S(1)} %copy-done.15, bf16[128,256]{1,0:T(8,128)(2,1)S(1)} %copy-done.4, bf16[256,6656]{1,0:T(8,128)(2,1)S(1)} %copy-done.1), custom_call_target="tpu_custom_call" | custom-call | flops 436207616 | bytes 3407872 | tf_op jit(solution)/shard_map/pallas_call | solution.py:87
  20.1 1.1 collective-permute-done.3.refs_7_
  22.0 48.3 %all_to_all.10.parts_ref = bf16[32,408,128]{2,1,0:T(8,128)(2,1)S(1)} all-to-all(bf16[32,408,128]{2,1,0:T(8,128)(2,1)S(1)} %shard_map.193), channel_id=1, replica_groups={{0,2,4,6,8,10,12,14,16,18,20,22,24,26,28,30,32,34,36,38,40,42,44,46,48,..., dimensions={0} | all-to-all | bytes 6684672 | tf_op jit(solution)/shard_map/all_to_all | solution.py:431
  70.7 1.5 %collective-permute-start.4 = (bf16[96,128]{1,0:T(8,128)(2,1)S(1)}, bf16[96,128]{1,0:T(8,128)(2,1)S(1)}, u32[]{:S(2)}, u32[]{:S(2)}) collective-permute-start(bf16[96,128]{1,0:T(8,128)(2,1)S(1)} %get-tuple-element.41.mine_ref), channel_id=1, source_target_pairs={{0,1},{1,0},{2,3},{3,2},{4,5},{5,4},{6,7},{7,6},{8,9},{9,8},{10,11... | collective-permute-start | bytes 73736 | tf_op jit(solution)/shard_map/ppermute | solution.py:428
  72.2 0.8 collective-permute-done.4.theirs_ref
  73.0 1.6 %shard_map.195 = (bf16[200,128]{1,0:T(8,128)(2,1)S(1)}, f32[200,128]{1,0:T(8,128)S(1)}, f32[64,104]{1,0:T(8,128)}, f32[64,104]{1,0:T(8,128)}, f32[64,104]{1,0:T(8,128)}) custom-call(s32[2]{0:T(128)S(1)} %pad_add_fusion.where_ref.refs_0_, f32[312,128]{1,0:T(8,128)S(1)} %get-tuple-element.40.sums_ref, bf16[96,128]{1,0:T(8,128)(2,1)S(1)} %get-tuple-element.41.mine_ref, ...), custom_call_target="tpu_custom_call" | custom-call | tf_op jit(solution)/shard_map/pallas_call | solution.py:226
  75.0 0.9 collective-permute-done.5.received_ref
  76.6 35.0 %all_to_all.11.refs_3_ = bf16[32,304,128]{2,1,0:T(8,128)(2,1)S(1)} all-to-all(bf16[32,304,128]{2,1,0:T(8,128)(2,1)S(1)} %shard_map.196), channel_id=1, replica_groups={{0,2,4,6,8,10,12,14,16,18,20,22,24,26,28,30,32,34,36,38,40,42,44,46,48,..., dimensions={0} | all-to-all | bytes 4980736 | tf_op jit(solution)/shard_map/all_to_all | solution.py:431
  111.6 2.0 %collective-permute-start.6 = (bf16[32,304,128]{2,1,0:T(8,128)(2,1)S(1)}, bf16[32,304,128]{2,1,0:T(8,128)(2,1)S(1)}, u32[]{:S(2)}, u32[]{:S(2)}) collective-permute-start(bf16[32,304,128]{2,1,0:T(8,128)(2,1)S(1)} %all_to_all.11.refs_3_), channel_id=1, source_target_pairs={{0,1},{1,0},{2,3},{3,2},{4,5},{5,4},{6,7},{7,6},{8,9},{9,8},{10,11... | collective-permute-start | bytes 7471112 | tf_op jit(solution)/shard_map/ppermute | solution.py:428
  113.5 3.3 %shard_map.197 = (f32[256,128]{1,0:T(8,128)S(1)}, f32[96,128]{1,0:T(8,128)S(1)}) custom-call(s32[2]{0:T(128)S(1)} %pad_add_fusion.where_ref.refs_0_, f32[2,52]{1,0:T(2,128)S(1)} %copy-done.14, f32[2,52]{1,0:T(2,128)S(1)} %copy-done.15, bf16[32,304,128]{2,1,0:T(8,128)(2,1)S(1)} %all_to_all.11.refs_3_, bf16[256,6656]{1,0:T(8,128)(2,1)S(1)} %copy-done, ...), custom_call_target="tpu_custom_call" | custom-call | flops 436207616 | bytes 3407872 | tf_op jit(solution)/shard_map/pallas_call | solution.py:351
  116.9 1.0 collective-permute-done.6.refs_3_
  117.9 3.4 %shard_map.198 = (bf16[256,128]{1,0:T(8,128)(2,1)S(1)}, bf16[256,128]{1,0:T(8,128)(2,1)S(1)}, bf16[256,128]{1,0:T(8,128)(2,1)S(1)}, bf16[256,128]{1,0:T(8,128)(2,1)S(1)}) custom-call(s32[2]{0:T(128)S(1)} %pad_add_fusion.where_ref.refs_0_, f32[2,52]{1,0:T(2,128)S(1)} %copy-done.14, f32[2,52]{1,0:T(2,128)S(1)} %copy-done.15, ...), custom_call_target="tpu_custom_call" | custom-call | flops 436207616 | bytes 3407872 | tf_op jit(solution)/shard_map/pallas_call | solution.py:351
  121.3 3.1 %collective-permute-start.7 = (bf16[256,128]{1,0:T(8,128)(2,1)S(1)}, bf16[256,128]{1,0:T(8,128)(2,1)S(1)}, u32[]{:S(2)}, u32[]{:S(2)}) collective-permute-start(bf16[256,128]{1,0:T(8,128)(2,1)S(1)} %get-tuple-element.47), channel_id=1, source_target_pairs={{0,64},{64,128},{128,192},{192,0},{1,65},{65,129},{129,193},{193,1... | collective-permute-start | bytes 196616 | tf_op jit(solution)/shard_map/ppermute | solution.py:450
  124.4 4.2 %collective-permute-start.8 = (bf16[256,128]{1,0:T(8,128)(2,1)S(1)}, bf16[256,128]{1,0:T(8,128)(2,1)S(1)}, u32[]{:S(2)}, u32[]{:S(2)}) collective-permute-start(bf16[256,128]{1,0:T(8,128)(2,1)S(1)} %get-tuple-element.48), channel_id=1, source_target_pairs={{0,128},{64,192},{128,0},{192,64},{1,129},{65,193},{129,1},{193,65... | collective-permute-start | bytes 196616 | tf_op jit(solution)/shard_map/ppermute | solution.py:450
  128.6 2.4 %collective-permute-start.9 = (bf16[256,128]{1,0:T(8,128)(2,1)S(1)}, bf16[256,128]{1,0:T(8,128)(2,1)S(1)}, u32[]{:S(2)}, u32[]{:S(2)}) collective-permute-start(bf16[256,128]{1,0:T(8,128)(2,1)S(1)} %get-tuple-element.49), channel_id=1, source_target_pairs={{0,192},{64,0},{128,64},{192,128},{1,193},{65,1},{129,65},{193,129... | collective-permute-start | bytes 196616 | tf_op jit(solution)/shard_map/ppermute | solution.py:450
  131.0 2.7 %collective-permute-done.8.two_ref = bf16[256,128]{1,0:T(8,128)(2,1)S(1)} collective-permute-done((bf16[256,128]{1,0:T(8,128)(2,1)S(1)}, bf16[256,128]{1,0:T(8,128)(2,1)S(1)}, u32[]{:S(2)}, u32[]{:S(2)}) %collective-permute-start.8) | collective-permute-done | bytes 65568 | tf_op jit(solution)/shard_map/ppermute | solution.py:450
  133.7 2.0 %collective-permute-done.9.three_ref = bf16[256,128]{1,0:T(8,128)(2,1)S(1)} collective-permute-done((bf16[256,128]{1,0:T(8,128)(2,1)S(1)}, bf16[256,128]{1,0:T(8,128)(2,1)S(1)}, u32[]{:S(2)}, u32[]{:S(2)}) %collective-permute-start.9) | collective-permute-done | bytes 65568 | tf_op jit(solution)/shard_map/ppermute | solution.py:450
  135.7 1.4 %shard_map.199 = (bf16[32,256]{1,0:T(8,128)(2,1)}, f32[64,256]{1,0:T(8,128)}, f32[64,256]{1,0:T(8,128)}, f32[64,256]{1,0:T(8,128)}) custom-call(s32[2]{0:T(128)S(1)} %pad_add_fusion.where_ref.refs_0_, bf16[256,128]{1,0:T(8,128)(2,1)S(1)} %get-tuple-element.46.own_ref, bf16[256,128]{1,0:T(8,128)(2,1)S(1)} %collective-permute-done.7.one_ref, ...), custom_call_target="tpu_custom_call" | custom-call | tf_op jit(solution)/shard_map/pallas_call | solution.py:392
  (43 shorter events, 5.4 us)
Async XLA Ops:
  0.6 10.0 %copy-start = (bf16[256,6656]{1,0:T(8,128)(2,1)S(1)}, bf16[256,6656]{1,0:T(8,128)(2,1)}, u32[]{:S(2)}) copy-start(bf16[256,6656]{1,0:T(8,128)(2,1)} %refs_4_.3) | copy-start | bytes 10223620
  1.7 2.0 %copy-start.2 = (bf16[6656,256]{1,0:T(8,128)(2,1)S(1)}, bf16[6656,256]{1,0:T(8,128)(2,1)}, u32[]{:S(2)}) copy-start(bf16[6656,256]{1,0:T(8,128)(2,1)} %values_ref.5) | copy-start | bytes 10223620
  4.5 11.0 %copy-start.1 = (bf16[256,6656]{1,0:T(8,128)(2,1)S(1)}, bf16[256,6656]{1,0:T(8,128)(2,1)}, u32[]{:S(2)}) copy-start(bf16[256,6656]{1,0:T(8,128)(2,1)} %refs_5_.3) | copy-start | bytes 10223620
  7.4 13.9 %collective-permute-start.2 = (bf16[32,104,128]{2,1,0:T(8,128)(2,1)S(1)}, bf16[32,104,128]{2,1,0:T(8,128)(2,1)S(1)}, u32[]{:S(2)}, u32[]{:S(2)}) collective-permute-start(bf16[32,104,128]{2,1,0:T(8,128)(2,1)S(1)} %get-tuple-element.38), channel_id=1, source_target_pairs={{0,1},{1,0},{2,3},{3,2},{4,5},{5,4},{6,7},{7,6},{8,9},{9,8},{10,11... | collective-permute-start | bytes 2555912 | tf_op jit(solution)/shard_map/ppermute | solution.py:428
  10.7 0.8 copy-start.3
  12.2 3.3 %copy-start.4 = (bf16[128,256]{1,0:T(8,128)(2,1)S(1)}, bf16[128,256]{1,0:T(8,128)(2,1)}, u32[]{:S(2)}) copy-start(bf16[128,256]{1,0:T(8,128)(2,1)} %tokens_ref.3) | copy-start | bytes 196612
  12.2 3.3 %copy-start.15 = (f32[2,52]{1,0:T(2,128)S(1)}, f32[2,52]{1,0:T(2,128)}, u32[]{:S(2)}) copy-start(f32[2,52]{1,0:T(2,128)} %refs_2_.3) | copy-start | bytes 1252
  12.2 7.0 %copy-start.6 = (bf16[128,256]{1,0:T(8,128)(2,1)S(1)}, bf16[128,256]{1,0:T(8,128)(2,1)}, u32[]{:S(2)}) copy-start(bf16[128,256]{1,0:T(8,128)(2,1)} %gradient_ref.3) | copy-start | bytes 196612
  12.2 7.0 %copy-start.7 = (bf16[64,256]{1,0:T(8,128)(2,1)S(1)}, bf16[64,256]{1,0:T(8,128)(2,1)}, u32[]{:S(2)}) copy-start(bf16[64,256]{1,0:T(8,128)(2,1)} %gate_reduce_ref.1) | copy-start | bytes 98308
  12.2 7.0 %copy-start.8 = (bf16[64,256]{1,0:T(8,128)(2,1)S(1)}, bf16[64,256]{1,0:T(8,128)(2,1)}, u32[]{:S(2)}) copy-start(bf16[64,256]{1,0:T(8,128)(2,1)} %up_reduce_ref.1) | copy-start | bytes 98308
  12.2 7.0 %copy-start.9 = (bf16[64,256]{1,0:T(8,128)(2,1)S(1)}, bf16[64,256]{1,0:T(8,128)(2,1)}, u32[]{:S(2)}) copy-start(bf16[64,256]{1,0:T(8,128)(2,1)} %down_ref.1) | copy-start | bytes 98308
  15.4 5.9 %collective-permute-start = (bf16[32,104,128]{2,1,0:T(8,128)(2,1)S(1)}, bf16[32,104,128]{2,1,0:T(8,128)(2,1)S(1)}, u32[]{:S(2)}, u32[]{:S(2)}) collective-permute-start(bf16[32,104,128]{2,1,0:T(8,128)(2,1)S(1)} %get-tuple-element.36), channel_id=1, source_target_pairs={{0,1},{1,0},{2,3},{3,2},{4,5},{5,4},{6,7},{7,6},{8,9},{9,8},{10,11... | collective-permute-start | bytes 2555912 | tf_op jit(solution)/shard_map/ppermute | solution.py:428
  18.7 2.6 %collective-permute-start.1 = (bf16[32,104,128]{2,1,0:T(8,128)(2,1)S(1)}, bf16[32,104,128]{2,1,0:T(8,128)(2,1)S(1)}, u32[]{:S(2)}, u32[]{:S(2)}) collective-permute-start(bf16[32,104,128]{2,1,0:T(8,128)(2,1)S(1)} %get-tuple-element.37), channel_id=1, source_target_pairs={{0,1},{1,0},{2,3},{3,2},{4,5},{5,4},{6,7},{7,6},{8,9},{9,8},{10,11... | collective-permute-start | bytes 2555912 | tf_op jit(solution)/shard_map/ppermute | solution.py:428
  20.0 1.3 collective-permute-start.3
  70.2 2.8 %copy-start.10 = (bf16[64,104]{1,0:T(8,128)(2,1)S(1)}, bf16[64,104]{1,0:T(8,128)(2,1)}, u32[]{:S(2)}) copy-start(bf16[64,104]{1,0:T(8,128)(2,1)} %gate_expand_ref.1) | copy-start | bytes 39940
  70.2 2.8 %copy-start.11 = (bf16[64,104]{1,0:T(8,128)(2,1)S(1)}, bf16[64,104]{1,0:T(8,128)(2,1)}, u32[]{:S(2)}) copy-start(bf16[64,104]{1,0:T(8,128)(2,1)} %up_expand_ref.1) | copy-start | bytes 39940
  70.2 2.8 %copy-start.12 = (bf16[64,104]{1,0:T(8,128)(2,1)S(1)}, bf16[64,104]{1,0:T(8,128)(2,1)}, u32[]{:S(2)}) copy-start(bf16[64,104]{1,0:T(8,128)(2,1)} %down_reduce_ref.1) | copy-start | bytes 39940
  70.7 2.3 %collective-permute-start.4 = (bf16[96,128]{1,0:T(8,128)(2,1)S(1)}, bf16[96,128]{1,0:T(8,128)(2,1)S(1)}, u32[]{:S(2)}, u32[]{:S(2)}) collective-permute-start(bf16[96,128]{1,0:T(8,128)(2,1)S(1)} %get-tuple-element.41.mine_ref), channel_id=1, source_target_pairs={{0,1},{1,0},{2,3},{3,2},{4,5},{5,4},{6,7},{7,6},{8,9},{9,8},{10,11... | collective-permute-start | bytes 73736 | tf_op jit(solution)/shard_map/ppermute | solution.py:428
  74.6 1.2 collective-permute-start.5
  75.9 37.7 %copy-start.14 = (f32[2,52]{1,0:T(2,128)S(1)}, f32[2,52]{1,0:T(2,128)}, u32[]{:S(2)}) copy-start(f32[2,52]{1,0:T(2,128)} %refs_1_.3) | copy-start | bytes 1252
  111.6 6.3 %collective-permute-start.6 = (bf16[32,304,128]{2,1,0:T(8,128)(2,1)S(1)}, bf16[32,304,128]{2,1,0:T(8,128)(2,1)S(1)}, u32[]{:S(2)}, u32[]{:S(2)}) collective-permute-start(bf16[32,304,128]{2,1,0:T(8,128)(2,1)S(1)} %all_to_all.11.refs_3_), channel_id=1, source_target_pairs={{0,1},{1,0},{2,3},{3,2},{4,5},{5,4},{6,7},{7,6},{8,9},{9,8},{10,11... | collective-permute-start | bytes 7471112 | tf_op jit(solution)/shard_map/ppermute | solution.py:428
  121.3 9.7 %collective-permute-start.7 = (bf16[256,128]{1,0:T(8,128)(2,1)S(1)}, bf16[256,128]{1,0:T(8,128)(2,1)S(1)}, u32[]{:S(2)}, u32[]{:S(2)}) collective-permute-start(bf16[256,128]{1,0:T(8,128)(2,1)S(1)} %get-tuple-element.47), channel_id=1, source_target_pairs={{0,64},{64,128},{128,192},{192,0},{1,65},{65,129},{129,193},{193,1... | collective-permute-start | bytes 196616 | tf_op jit(solution)/shard_map/ppermute | solution.py:450
  124.4 9.3 %collective-permute-start.8 = (bf16[256,128]{1,0:T(8,128)(2,1)S(1)}, bf16[256,128]{1,0:T(8,128)(2,1)S(1)}, u32[]{:S(2)}, u32[]{:S(2)}) collective-permute-start(bf16[256,128]{1,0:T(8,128)(2,1)S(1)} %get-tuple-element.48), channel_id=1, source_target_pairs={{0,128},{64,192},{128,0},{192,64},{1,129},{65,193},{129,1},{193,65... | collective-permute-start | bytes 196616 | tf_op jit(solution)/shard_map/ppermute | solution.py:450
  128.6 7.1 %collective-permute-start.9 = (bf16[256,128]{1,0:T(8,128)(2,1)S(1)}, bf16[256,128]{1,0:T(8,128)(2,1)S(1)}, u32[]{:S(2)}, u32[]{:S(2)}) collective-permute-start(bf16[256,128]{1,0:T(8,128)(2,1)S(1)} %get-tuple-element.49), channel_id=1, source_target_pairs={{0,192},{64,0},{128,64},{192,128},{1,193},{65,1},{129,65},{193,129... | collective-permute-start | bytes 196616 | tf_op jit(solution)/shard_map/ppermute | solution.py:450
  (2 other events, 1.5 us)

commit v2 on v0

v2 whole, which is shorter than its diff:
```python
import functools

import jax
import jax.numpy as jnp
from jax import lax
from jax.experimental import pallas as pl
from jax.experimental.pallas import tpu as pltpu
from jax.sharding import PartitionSpec as P

BLOCK = 128
SCALE = 0.5
STEPS = 4
BF16 = jnp.bfloat16
F32 = jnp.float32
LIMIT = 32 * 1024 * 1024
CHUNK = 512
FIRST_PARTS = (1024, 2048, 3584)
LATER_PARTS = (6656,)


def params():
    return pltpu.CompilerParams(vmem_limit_bytes=LIMIT)


def dot(left, right, left_dim, right_dim):
    return lax.dot_general(
        left, right, (((left_dim,), (right_dim,)), ((), ())), preferred_element_type=F32
    )


def whole(shape):
    return pl.BlockSpec(shape, lambda *_: (0,) * len(shape))


def smem():
    return pl.BlockSpec(memory_space=pltpu.SMEM)


def dequantize_wide(values, scales_ref, first):
    columns = []
    for block in range(values.shape[1] // BLOCK):
        columns.append(
            jnp.concatenate(
                [
                    (values[part * BLOCK : (part + 1) * BLOCK, block * BLOCK : (block + 1) * BLOCK].astype(F32)
                     * scales_ref[part, first + block]).astype(BF16)
                    for part in range(values.shape[0] // BLOCK)
                ],
                axis=0,
            )
        )
    return jnp.concatenate(columns, axis=1)


def dequantize_tall(values, scales_ref, first):
    rows = []
    for block in range(values.shape[0] // BLOCK):
        rows.append(
            jnp.concatenate(
                [
                    (values[block * BLOCK : (block + 1) * BLOCK, part * BLOCK : (part + 1) * BLOCK].astype(F32)
                     * scales_ref[part, first + block]).astype(BF16)
                    for part in range(values.shape[1] // BLOCK)
                ],
                axis=1,
            )
        )
    return jnp.concatenate(rows, axis=0)


def split_by_core(core, sums_ref, send_ref, keep_ref):
    chips, piece = send_ref.shape[:2]
    for chip in range(chips):
        start = chip * 2 * piece
        mine = pl.multiple_of(start + core * piece, 8)
        theirs = pl.multiple_of(start + (1 - core) * piece, 8)
        keep_ref[chip] = sums_ref[pl.ds(mine, piece), :].astype(BF16)
        send_ref[chip] = sums_ref[pl.ds(theirs, piece), :].astype(BF16)


def stay(value):
    return pltpu.with_memory_space_constraint(value, pltpu.HBM)


def fetch_all(sources, buffers, sems):
    copies = [pltpu.make_async_copy(s, b, sems.at[i]) for i, (s, b) in enumerate(zip(sources, buffers))]
    for copy in copies:
        copy.start()
    return copies


def start_parts(values_ref, buffer_ref, sems, axis, sizes):
    parts, first = [], 0
    for step, size in enumerate(sizes):
        part = pl.ds(first, size)
        place = (part, slice(None)) if axis == 0 else (slice(None), part)
        copy = pltpu.make_async_copy(values_ref.at[place], buffer_ref.at[place], sems.at[step])
        copy.start()
        parts.append((copy, first, size))
        first += size
    return parts


def wide_kernel(
    where_ref, gate_scales_hbm, up_scales_hbm, tokens_hbm, gradient_hbm, gate_reduce_hbm, up_reduce_hbm,
    down_expand_hbm, gate_hbm, up_hbm, gate_send, gate_keep, up_send, up_keep, low_ref,
    gate_scales, up_scales, tokens_ref, gradient_ref, gate_reduce_ref, up_reduce_ref, down_expand_ref, gate_ref, up_ref, sums_ref, small, sems,
):
    small_copies = fetch_all(
        [gate_scales_hbm, tokens_hbm, up_scales_hbm, gradient_hbm, gate_reduce_hbm, up_reduce_hbm, down_expand_hbm],
        [gate_scales, tokens_ref, up_scales, gradient_ref, gate_reduce_ref, up_reduce_ref, down_expand_ref],
        small,
    )
    gate_parts = start_parts(gate_hbm, gate_ref, sems.at[0], 1, FIRST_PARTS)
    up_parts = start_parts(up_hbm, up_ref, sems.at[1], 1, LATER_PARTS)
    for copy in small_copies[:3]:
        copy.wait()
    for parts, values_ref, scales_ref, send_ref, keep_ref in (
        (gate_parts, gate_ref, gate_scales, gate_send, gate_keep),
        (up_parts, up_ref, up_scales, up_send, up_keep),
    ):
        for copy, first, size in parts:
            copy.wait()
            for start in range(first, first + size, CHUNK):
                part = slice(start, start + CHUNK)
                weight = dequantize_wide(values_ref[:, part], scales_ref, start // BLOCK)
                sums_ref[part] = dot(tokens_ref[...], weight, 1, 0).T
        split_by_core(where_ref[0], sums_ref, send_ref, keep_ref)
    for copy in small_copies[3:]:
        copy.wait()
    rank = gate_reduce_ref.shape[0]
    low_ref[:rank] = dot(gate_reduce_ref[...], tokens_ref[...], 1, 1).astype(BF16)
    low_ref[rank : 2 * rank] = dot(up_reduce_ref[...], tokens_ref[...], 1, 1).astype(BF16)
    low_ref[2 * rank :] = dot(down_expand_ref[...], gradient_ref[...], 1, 1).astype(BF16)


def tall_kernel(
    where_ref, scales_hbm, gradient_hbm, values_hbm, after_ref, send_ref, keep_ref,
    scales_ref, gradient_ref, values_ref, sums_ref, small, sems,
):
    small_copies = fetch_all([scales_hbm, gradient_hbm], [scales_ref, gradient_ref], small)
    parts = start_parts(values_hbm, values_ref, sems, 0, FIRST_PARTS)
    for copy in small_copies:
        copy.wait()
    for copy, first, size in parts:
        copy.wait()
        for start in range(first, first + size, CHUNK):
            part = slice(start, start + CHUNK)
            weight = dequantize_tall(values_ref[part], scales_ref, start // BLOCK)
            sums_ref[part] = dot(weight, gradient_ref[...], 1, 1)
    split_by_core(where_ref[0], sums_ref, send_ref, keep_ref)


def wide_sums(where, gate_scales, up_scales, tokens, gradient, gate_reduce, up_reduce, down_expand, gate, up, piece):
    width, hidden = gate.shape
    chips, count = hidden // (2 * piece), tokens.shape[0]
    vmem, hbm = pl.BlockSpec(memory_space=pltpu.VMEM), pl.BlockSpec(memory_space=pltpu.HBM)
    fetched = (tokens, gradient, gate_reduce, up_reduce, down_expand, gate, up)
    return pl.pallas_call(
        wide_kernel,
        in_specs=[smem()] + [hbm] * 9,
        out_specs=[vmem] * 5,
        out_shape=[jax.ShapeDtypeStruct((chips, piece, count), BF16)] * 4
        + [jax.ShapeDtypeStruct((3 * gate_reduce.shape[0], count), BF16)],
        scratch_shapes=[pltpu.SMEM(gate_scales.shape, F32)] * 2
        + [pltpu.VMEM(value.shape, BF16) for value in fetched]
        + [
            pltpu.VMEM((hidden, count), F32),
            pltpu.SemaphoreType.DMA((7,)),
            pltpu.SemaphoreType.DMA((2, len(FIRST_PARTS))),
        ],
        compiler_params=params(),
    )(where, *[stay(value) for value in (gate_scales, up_scales, *fetched)])


def tall_sums(where, scales, gradient, values, piece, after):
    hidden, width = values.shape
    chips, count = hidden // (2 * piece), gradient.shape[0]
    vmem, hbm = pl.BlockSpec(memory_space=pltpu.VMEM), pl.BlockSpec(memory_space=pltpu.HBM)
    return pl.pallas_call(
        tall_kernel,
        in_specs=[smem(), hbm, hbm, hbm, pl.BlockSpec(memory_space=pl.ANY)],
        out_specs=[vmem] * 2,
        out_shape=[jax.ShapeDtypeStruct((chips, piece, count), BF16)] * 2,
        scratch_shapes=[
            pltpu.SMEM(scales.shape, F32),
            pltpu.VMEM(gradient.shape, BF16),
            pltpu.VMEM(values.shape, BF16),
            pltpu.VMEM((hidden, count), F32),
            pltpu.SemaphoreType.DMA((2,)),
            pltpu.SemaphoreType.DMA((len(FIRST_PARTS),)),
        ],
        compiler_params=params(),
    )(where, stay(scales), stay(gradient), stay(values), after)


def weights_kernel(gate_scales, up_scales, gate_ref, up_ref, after_ref, gate_out, up_out):
    first = pl.program_id(0) * (gate_ref.shape[1] // BLOCK)
    gate_out[...] = dequantize_wide(gate_ref[...], gate_scales, first)
    up_out[...] = dequantize_wide(up_ref[...], up_scales, first)


def weights(gate_scales, up_scales, gate, up, after):
    width, hidden = gate.shape
    block = pl.BlockSpec((width, hidden // STEPS), lambda i: (0, i))
    return pl.pallas_call(
        weights_kernel,
        grid=(STEPS,),
        in_specs=[smem(), smem(), block, block, pl.BlockSpec(memory_space=pl.ANY)],
        out_specs=[block] * 2,
        out_shape=[jax.ShapeDtypeStruct(gate.shape, BF16)] * 2,
        compiler_params=params(),
        cost_estimate=pl.CostEstimate(
            flops=2 * width * hidden, bytes_accessed=8 * width * hidden, transcendentals=0
        ),
    )(gate_scales, up_scales, gate, up, after)


def vmem_call(kernel, out_shape, *args, scratch=(), unread=0):
    vmem = pl.BlockSpec(memory_space=pltpu.VMEM)
    return pl.pallas_call(
        kernel,
        in_specs=[smem()] + [vmem] * (len(args) - 1 - unread) + [pl.BlockSpec(memory_space=pl.ANY)] * unread,
        out_specs=[vmem] * len(out_shape),
        out_shape=out_shape,
        scratch_shapes=scratch,
        compiler_params=params(),
    )(*args)


def chip_of(core, first, z, second):
    return jnp.where(core == 0, first * 8 + z * 4 + second, second * 8 + z * 4 + first)


def pack_kernel(where_ref, *refs):
    keeps, received, outs = refs[:4], refs[4:8], refs[8:]
    core, first, second = where_ref[0], where_ref[3], where_ref[4]
    low = keeps[3][...].astype(F32) + received[3][...].astype(F32)
    pair = 6 * keeps[0].shape[1]
    for offset, out_ref in enumerate(outs):
        there = lax.rem(first + offset, 4)
        for step in range(4):
            parts = []
            for near in range(2):
                chip = chip_of(core, there, near, lax.rem(second + step, 4))
                parts += [keeps[k][chip].astype(F32) + received[k][chip].astype(F32) for k in range(3)]
            out_ref[step * pair : (step + 1) * pair] = jnp.concatenate(parts, axis=0).astype(out_ref.dtype)
        out_ref[4 * pair :] = low.astype(out_ref.dtype)


def pack(where, keeps, received):
    _, piece, tokens = keeps[0].shape
    rows = 24 * piece + keeps[3].shape[0]
    out_shape = [jax.ShapeDtypeStruct((rows, tokens), F32 if i == 0 else BF16) for i in range(4)]
    return vmem_call(pack_kernel, out_shape, where, *keeps, *received)


def second_kernel(where_ref, own_ref, one_ref, two_ref, three_ref, gate_ref, up_ref, *outs):
    pair = (own_ref.shape[0] - outs[0].shape[0]) // 3

    def add(first, count):
        rows = slice(first, first + count)
        arrived = one_ref[rows].astype(F32) + two_ref[rows].astype(F32) + three_ref[rows].astype(F32)
        return own_ref[rows] + arrived

    low = add(4 * pair, own_ref.shape[0] - 4 * pair)
    for step, out_ref in enumerate(outs):
        out_ref[:pair] = add(step * pair, pair).astype(out_ref.dtype)
        out_ref[pair:] = low.astype(out_ref.dtype)


def second(where, own, arrived, piece, ready):
    rows, tokens = own.shape
    rows -= 18 * piece
    out_shape = [jax.ShapeDtypeStruct((rows, tokens), F32 if i == 0 else BF16) for i in range(4)]
    return vmem_call(second_kernel, out_shape, where, own, *arrived, *ready, unread=2)


def third_kernel(
    where_ref, own_ref, one_ref, two_ref, three_ref, gate_expand_ref, up_expand_ref, down_reduce_ref, keep_ref, send_ref
):
    rows, count = keep_ref.shape
    arrived = one_ref[...].astype(F32) + two_ref[...].astype(F32) + three_ref[...].astype(F32)
    everything = own_ref[...] + arrived
    keep_ref[...] = everything
    send_ref[:rows] = everything.astype(BF16)
    rank, piece = gate_expand_ref.shape
    for kind, ref in enumerate((gate_expand_ref, up_expand_ref, down_reduce_ref)):
        place = slice(rows + kind * rank, rows + (kind + 1) * rank)
        send_ref[place, :piece] = ref[...]
        send_ref[place, piece:] = jnp.zeros((rank, count - piece), BF16)


def third(where, own, arrived, expands):
    rows, count = own.shape
    far_rows = rows + 3 * expands[0].shape[0]
    out_shape = [jax.ShapeDtypeStruct(own.shape, F32), jax.ShapeDtypeStruct((far_rows, count), BF16)]
    return vmem_call(third_kernel, out_shape, where, own, *arrived, *expands)


def middle_kernel(
    where_ref, own_ref, arrived_ref, gate_expand_ref, up_expand_ref, down_reduce_ref,
    send_ref, keep_ref, gate_out, up_out, down_out, expands_ref, grads_ref,
):
    core, z = where_ref[0], where_ref[2]
    rank, piece = gate_expand_ref.shape
    rows = own_ref.shape[0]
    sums = own_ref[...] + arrived_ref[:rows].astype(F32)
    for kind, ref in enumerate((gate_expand_ref, up_expand_ref, down_reduce_ref)):
        expands_ref[z, kind] = ref[...]
        expands_ref[1 - z, kind] = arrived_ref[rows + kind * rank : rows + (kind + 1) * rank, :piece]
    lows = [sums[6 * piece + k * rank : 6 * piece + (k + 1) * rank].astype(BF16) for k in range(3)]
    keeps, sends, ranks = [], [], [0.0] * 3
    first = core == 0
    for chip in range(2):
        start = 3 * piece * chip
        gate, upper, back = [
            sums[start + kind * piece : start + (kind + 1) * piece]
            + SCALE * dot(expands_ref[chip, kind], lows[kind], 0, 0)
            for kind in range(3)
        ]
        sigma = jax.nn.sigmoid(gate)
        activated = gate * sigma
        hidden = activated * upper
        grad_gate = back * upper * sigma * (1.0 + gate * (1.0 - sigma))
        grad_upper = back * activated
        keeps.append(jnp.where(first, grad_gate, grad_upper))
        sends.append(jnp.where(first, grad_upper, grad_gate))
        for kind, grad in enumerate((grad_gate, grad_upper, hidden)):
            grads_ref[chip, kind] = grad.astype(BF16)
            ranks[kind] = ranks[kind] + dot(expands_ref[chip, kind], grads_ref[chip, kind], 1, 0)
    keep_ref[...] = jnp.concatenate([*keeps, *ranks], axis=0)
    send_ref[...] = jnp.concatenate([*sends, *ranks], axis=0).astype(BF16)
    for kind, out_ref in enumerate((gate_out, up_out, down_out)):
        out_ref[...] = SCALE * dot(lows[kind], grads_ref[z, kind], 1, 1)


def middle(where, own, arrived, expands):
    rank, piece = expands[0].shape
    tokens = own.shape[1]
    rows = 2 * piece + 3 * rank
    out_shape = [
        jax.ShapeDtypeStruct((rows, tokens), BF16),
        jax.ShapeDtypeStruct((rows, tokens), F32),
    ] + [jax.ShapeDtypeStruct((rank, piece), F32)] * 3
    scratch = [pltpu.VMEM((2, 3, rank, piece), BF16), pltpu.VMEM((2, 3, piece, tokens), BF16)]
    return vmem_call(middle_kernel, out_shape, where, own, arrived, *expands, scratch=scratch)


def pair_kernel(piece, where_ref, keep_ref, arrived_ref, out_ref):
    first = where_ref[0] == 0
    kept, arrived = keep_ref[...], arrived_ref[...].astype(F32)
    rows = []
    for chip in range(2):
        here = slice(chip * piece, (chip + 1) * piece)
        rows.append(jnp.where(first, kept[here], arrived[here]))
        rows.append(jnp.where(first, arrived[here], kept[here]))
    rows.append(kept[2 * piece :] + arrived[2 * piece :])
    out_ref[...] = jnp.concatenate(rows, axis=0).astype(BF16)


def pair_block(where, keep, arrived, piece):
    rows, tokens = keep.shape
    out_shape = [jax.ShapeDtypeStruct((rows + 2 * piece, tokens), BF16)]
    return vmem_call(functools.partial(pair_kernel, piece), out_shape, where, keep, arrived)[0]


def join_kernel(slot, where_ref, own_ref, *refs):
    arrived, out_ref = refs[:-1], refs[-1]
    count = len(refs)
    unit = (out_ref.shape[0] - own_ref.shape[0]) // (count - 1)
    place = where_ref[slot]
    rank = own_ref[unit:].astype(F32)
    for offset, ref in enumerate([own_ref, *arrived]):
        start = pl.multiple_of(lax.rem(place + count - offset, count) * unit, 16)
        out_ref[pl.ds(start, unit), :] = ref[:unit]
        if offset:
            rank = rank + ref[unit:].astype(F32)
    out_ref[count * unit :] = rank.astype(BF16)


def join(slot, where, own, arrived, rank_rows):
    rows, tokens = own.shape
    out_shape = [jax.ShapeDtypeStruct((rows + len(arrived) * (rows - rank_rows), tokens), BF16)]
    return vmem_call(functools.partial(join_kernel, slot), out_shape, where, own, *arrived)[0]


def back_kernel(last, *refs):
    if last:
        (where_ref, *pieces, gate_ref, up_ref, before_ref, rank_ref,
         own_ref, to_one, to_two, to_three, grads_ref, total_ref, turned_ref) = refs
    else:
        where_ref, *pieces, gate_ref, up_ref, total_ref, rank_ref, grads_ref = refs
    core = 1 - where_ref[0] if last else where_ref[0]
    place = where_ref[4] if last else where_ref[3]
    part = grads_ref.shape[0] // 4
    unit = part // 8
    for offset, ref in enumerate(pieces):
        there = lax.rem(place + 4 - offset, 4)
        for other in range(4):
            for z in range(2):
                chip = chip_of(core, there, z, other)
                source = (other * 2 + z) * unit
                grads_ref[pl.ds(pl.multiple_of(chip * unit, 16), unit), :] = ref[source : source + unit]

    for turn, weight_ref in enumerate((gate_ref, up_ref)):

        @pl.when(core == turn)
        def _():
            product = dot(weight_ref[...], grads_ref[...], 1, 0)
            total_ref[...] = product + before_ref[...] if last else product

    if last:
        turned_ref[...] = total_ref[...].T
        share = turned_ref.shape[0] // 4
        for offset, out_ref in enumerate([own_ref, to_one, to_two, to_three]):
            start = pl.multiple_of(lax.rem(where_ref[1] + offset, 4) * share, share)
            piece = turned_ref[pl.ds(start, share), :]
            block = jnp.concatenate([piece[:, :BLOCK], piece[:, BLOCK:], rank_ref[...]], axis=0)
            out_ref[...] = block.astype(BF16)
    else:
        rank = pieces[0][part:].astype(F32)
        for ref in pieces[1:]:
            rank = rank + ref[part:].astype(F32)
        rank_ref[...] = rank


def back(last, where, pieces, gate_weight, up_weight, before=()):
    width, hidden = gate_weight.shape
    rows, tokens = pieces[0].shape
    rank_rows = rows - hidden // 4
    scratch = [pltpu.VMEM((hidden, tokens), BF16)]
    if last:
        out_shape = [jax.ShapeDtypeStruct((tokens // 4 * width // BLOCK + rank_rows, tokens), BF16)] * 4
        scratch += [pltpu.VMEM((width, tokens), F32), pltpu.VMEM((tokens, width), F32)]
    else:
        out_shape = [
            jax.ShapeDtypeStruct((width, tokens), F32),
            jax.ShapeDtypeStruct((rank_rows, tokens), F32),
        ]
    return vmem_call(
        functools.partial(back_kernel, last), out_shape, where, *pieces, gate_weight, up_weight, *before,
        scratch=scratch,
    )


def last_kernel(
    where_ref, own_ref, one_ref, two_ref, three_ref, tokens_ref, gradient_ref, gate_reduce_ref, up_reduce_ref,
    input_out, gate_out, up_out, down_out, parts_ref, wide_ref,
):
    column = where_ref[1]
    for offset, ref in enumerate([own_ref, one_ref, two_ref, three_ref]):
        parts_ref[lax.rem(column + 4 - offset, 4)] = ref[...].astype(F32)
    summed = parts_ref[0] + parts_ref[1] + parts_ref[2] + parts_ref[3]
    share = input_out.shape[0]
    rank = gate_out.shape[0]
    sums = [summed[2 * share + k * rank : 2 * share + (k + 1) * rank].astype(BF16) for k in range(3)]
    wide_ref[...] = dot(sums[0], gate_reduce_ref[...], 0, 0) + dot(sums[1], up_reduce_ref[...], 0, 0)
    start = pl.multiple_of(column * share, share)
    main = jnp.concatenate([summed[:share], summed[share : 2 * share]], axis=1)
    input_out[...] = (main + SCALE * wide_ref[pl.ds(start, share), :]).astype(BF16)
    gate_out[...] = SCALE * dot(sums[0], tokens_ref[...], 1, 0)
    up_out[...] = SCALE * dot(sums[1], tokens_ref[...], 1, 0)
    down_out[...] = SCALE * dot(sums[2], gradient_ref[...], 1, 0)


def finish(where, own, others, tokens, gradient, gate_reduce, up_reduce):
    rank, width = gate_reduce.shape
    count = tokens.shape[0]
    vmem = pl.BlockSpec(memory_space=pltpu.VMEM)
    return pl.pallas_call(
        last_kernel,
        in_specs=[smem()] + [vmem] * 8,
        out_specs=[vmem] * 4,
        out_shape=[jax.ShapeDtypeStruct((count // 4, width), BF16)]
        + [jax.ShapeDtypeStruct((rank, width), F32)] * 3,
        scratch_shapes=[pltpu.VMEM((4,) + own.shape, F32), pltpu.VMEM((count, width), F32)],
        compiler_params=params(),
    )(where, own, *others, tokens, gradient, gate_reduce, up_reduce)


def per_device(
    tokens,
    output_gradient,
    gate_values,
    gate_scales,
    up_values,
    up_scales,
    down_values,
    down_scales,
    gate_reduce_factor,
    gate_expand,
    up_reduce_factor,
    up_expand,
    down_reduce,
    down_expand,
):
    piece = gate_expand.shape[1]
    position = lax.axis_index("row")
    core, y, z, x = position & 1, (position >> 1) & 3, (position >> 3) & 1, position >> 4
    first, second_place = jnp.where(core == 0, x, y), jnp.where(core == 0, y, x)
    where = jnp.stack([core, lax.axis_index("col"), z, first, second_place]).astype(jnp.int32)

    def exchange(value):
        return lax.ppermute(value, "row", [(i, i ^ 1) for i in range(64)])

    def along_z(value):
        return lax.ppermute(value, "row", [(i, i ^ 8) for i in range(64)])

    def along(second_axis, values):
        out = [None] * 3
        for offset in (2, 1, 3):
            pairs = []
            for i in range(64):
                if (i % 2 == 0) != second_axis:
                    pairs.append((i, (i + 16 * offset) % 64))
                else:
                    pairs.append((i, i - (i // 2 % 4) * 2 + ((i // 2 + offset) % 4) * 2))
            out[offset - 1] = lax.ppermute(values[offset - 1], "row", pairs)
        return out

    expands = (gate_expand, up_expand, down_reduce)
    *wide, low = wide_sums(
        where, gate_scales, up_scales, tokens, output_gradient, gate_reduce_factor, up_reduce_factor, down_expand,
        gate_values, up_values, piece,
    )
    tall = tall_sums(where, down_scales.T, output_gradient, down_values, piece, low)
    sends = [wide[0], wide[2], tall[0], low]
    own, *out = pack(where, [wide[1], wide[3], tall[1], low], [exchange(send) for send in sends])
    gate_weight, up_weight = weights(gate_scales, up_scales, gate_values, up_values, own)
    own, *out = second(where, own, along(False, out), piece, (gate_weight, up_weight))
    own, out = third(where, own, along(True, out), expands)
    send, keep, gate_expand_gradient, up_expand_gradient, down_reduce_gradient = middle(
        where, own, along_z(out), expands
    )
    rank_rows = low.shape[0]
    block = pair_block(where, keep, exchange(send), piece)
    block = join(4, where, block, along(True, [block] * 3), rank_rows)
    mine = [block, *along(False, [block] * 3)]
    theirs = [exchange(value) for value in mine]
    begun = back(False, where, mine, gate_weight, up_weight)
    own, *out = back(True, where, theirs, gate_weight, up_weight, begun)
    others = [
        lax.ppermute(value, "col", [(i, (i + offset) % 4) for i in range(4)])
        for offset, value in zip((1, 2, 3), out)
    ]
    input_gradient, gate_reduce_gradient, up_reduce_gradient, down_expand_gradient = finish(
        where, own, others, tokens, output_gradient, gate_reduce_factor, up_reduce_factor
    )
    return (
        input_gradient,
        gate_reduce_gradient,
        gate_expand_gradient,
        up_reduce_gradient,
        up_expand_gradient,
        down_reduce_gradient,
        down_expand_gradient,
    )


def solution(mesh):
    in_specs = (
        P(None, "row"),
        P(None, "row"),
        P("row", "col"),
        P("row", "col"),
        P("row", "col"),
        P("row", "col"),
        P("col", "row"),
        P("col", "row"),
        P(None, "row"),
        P(None, ("col", "row")),
        P(None, "row"),
        P(None, ("col", "row")),
        P(None, ("col", "row")),
        P(None, "row"),
    )
    out_specs = (
        P("col", "row"),
        P(None, "row"),
        P(None, ("col", "row")),
        P(None, "row"),
        P(None, ("col", "row")),
        P(None, ("col", "row")),
        P(None, "row"),
    )
    return jax.shard_map(
        per_device, mesh=mesh, in_specs=in_specs, out_specs=out_specs, check_vma=False
    )
```

time: 1360 us -> 109 us (0.08)
  waiting for transfers between devices: 889 us -> 46 us
  blocking collectives: 352 us -> 0 us
  local copies, waits for them, and re-layouts: 53.5 us -> 0.14 us
  starting transfers between devices: 0.38 us -> 38.9 us
  matrix products: 36 us -> 0 us
  Pallas kernels: 0 us -> 22.6 us
  between operations: 14.7 us -> 0.86 us
    unnamed x6 -> x0, waiting for transfers between devices: 594 us -> none
    psum x2 -> x0, blocking collectives: 352 us -> none  [the longest x1 276 us: per_device(): lax.psum((contract_matrices(tokens, gate_reduce_factor, 1, 1), contract_m...]
    all_gather x3 -> x0, waiting for transfers between devices: 295 us -> none  [the longest x1 105 us: per_device(): lax.all_gather(gate_gradient, 'row', axis=0, tiled=True)]
    ppermute x0 -> x25, waiting for transfers between devices: none -> 46 us  [the longest x12 33.6 us: along(): out[offset - 1] = lax.ppermute(values[offset - 1], 'row', pairs)]
    ppermute x0 -> x25, starting transfers between devices: none -> 38.9 us  [the longest x9 16.3 us: exchange(): return lax.ppermute(value, 'row', [(i, i ^ 1) for i in range(64)])]
    dot_general x22 -> x0, matrix products: 36 us -> none  [the longest x15 20.7 us: contract_matrices(): lax.dot_general(left, right, (((left_dim,), (right_dim,)), ((), ())), pre...]
    unnamed x63 -> x22, local copies, waits for them, and re-layouts: 31 us -> 0.06 us
    pallas_call x0 -> x12, Pallas kernels: none -> 22.6 us  [the longest x8 9.34 us: vmem_call(): pl.pallas_call(kernel, in_specs=[smem()] + [vmem] * (len(args) - 1 - unre...]
  transfers between devices with their start and end apart: 5 -> 25, of which waited for: 4 -> 14; matrix products, arithmetic and copies ran while one was open for 2% -> 0% of each run, Pallas kernels for 0% -> 8%
where the time goes in v2:
time: 109 us
  waiting for transfers between devices  46 us (42%)
  starting transfers between devices  38.9 us (36%)
  Pallas kernels  22.6 us (21%)
    ppermute x12, waiting for transfers between devices, along(): out[offset - 1] = lax.ppermute(values[offset - 1], 'row', pairs)  33.6 us
    ppermute x9, starting transfers between devices, exchange(): return lax.ppermute(value, 'row', [(i, i ^ 1) for i in range(64)])  16.3 us
    ppermute x12, starting transfers between devices, along(): out[offset - 1] = lax.ppermute(values[offset - 1], 'row', pairs)  12.8 us
    pallas_call x8, Pallas kernels, vmem_call(): pl.pallas_call(kernel, in_specs=[smem()] + [vmem] * (len(args) - 1 - unre...  9.34 us
    ppermute x3, starting transfers between devices, per_device(): lax.ppermute(value, 'col', [(i, (i + offset) % 4) for i in range(4)])  9.09 us
    pallas_call x1, Pallas kernels, wide_sums(): pl.pallas_call(wide_kernel, in_specs=[smem()] + [hbm] * 9, out_specs=[vme...  5.29 us
    ppermute x3, waiting for transfers between devices, per_device(): lax.ppermute(value, 'col', [(i, (i + offset) % 4) for i in range(4)])  4.93 us
    ppermute x1, waiting for transfers between devices, along_z(): return lax.ppermute(value, 'row', [(i, i ^ 8) for i in range(64)])  4.55 us
  transfers between devices with their start and end apart: 25, of which 14 were waited for; matrix products, arithmetic and copies ran while one was open for 0% of the time, Pallas kernels for 8%

profile of v2, /device:TPU:1, one launch (start us, length us, event | category | flops | bytes accessed | tf_op | source)
XLA Modules:
  0.0 108.5 jit_solution(3342694712712478843)
XLA Ops:
  0.7 5.3 %shard_map.189 = (bf16[32,104,128]{2,1,0:T(8,128)(2,1)S(1)}, bf16[32,104,128]{2,1,0:T(8,128)(2,1)S(1)}, bf16[32,104,128]{2,1,0:T(8,128)(2,1)S(1)}, bf16[32,104,128]{2,1,0:T(8,128)(2,1)S(1)}, bf16[192,128]{1,0:T(8,128)(2,1)S(1)}) custom-call(s32[5]{0:T(128)S(1)} %stack.23.where_ref.refs_0_, f32[2,52]{1,0:T(2,128)} %gate_scales.1, f32[2,52]{1,0:T(2,128)} %up_scales.1, ...), custom_call_target="tpu_custom_call" | custom-call | tf_op jit(solution)/shard_map/pallas_call | solution.py:159
  6.0 3.3 %collective-permute-start = (bf16[32,104,128]{2,1,0:T(8,128)(2,1)S(1)}, bf16[32,104,128]{2,1,0:T(8,128)(2,1)S(1)}, u32[]{:S(2)}, u32[]{:S(2)}) collective-permute-start(bf16[32,104,128]{2,1,0:T(8,128)(2,1)S(1)} %get-tuple-element.45), channel_id=1, source_target_pairs={{0,1},{1,0},{2,3},{3,2},{4,5},{5,4},{6,7},{7,6},{8,9},{9,8},{10,11... | collective-permute-start | bytes 2555912 | tf_op jit(solution)/shard_map/ppermute | solution.py:505
  9.4 3.8 %shard_map.190 = (bf16[32,104,128]{2,1,0:T(8,128)(2,1)S(1)}, bf16[32,104,128]{2,1,0:T(8,128)(2,1)S(1)}) custom-call(s32[5]{0:T(128)S(1)} %stack.23.where_ref.refs_0_, f32[2,52]{1,0:T(2,128)} %bitcast.6, bf16[128,256]{1,0:T(8,128)(2,1)} %gradient_ref.1, bf16[6656,256]{1,0:T(8,128)(2,1)} %values_hbm.1, bf16[192,128]{1,0:T(8,128)(2,1)S(1)} %get-tuple-element.43.after_ref.refs_3_), custom_call_target="tpu_custom_call" | custom-call | tf_op jit(solution)/shard_map/pallas_call | solution.py:180
  13.9 2.0 %collective-permute-done.3.refs_7_ = bf16[192,128]{1,0:T(8,128)(2,1)S(1)} collective-permute-done((bf16[192,128]{1,0:T(8,128)(2,1)S(1)}, bf16[192,128]{1,0:T(8,128)(2,1)S(1)}, u32[]{:S(2)}, u32[]{:S(2)}) %collective-permute-start.3) | collective-permute-done | bytes 49184 | tf_op jit(solution)/shard_map/ppermute | solution.py:505
  17.1 2.2 %collective-permute-start.5 = (bf16[2688,128]{1,0:T(8,128)(2,1)S(1)}, bf16[2688,128]{1,0:T(8,128)(2,1)S(1)}, u32[]{:S(2)}, u32[]{:S(2)}) collective-permute-start(bf16[2688,128]{1,0:T(8,128)(2,1)S(1)} %get-tuple-element.50), channel_id=1, source_target_pairs={{0,32},{1,5},{2,34},{3,7},{4,36},{5,1},{6,38},{7,3},{8,40},{9,13},... | collective-permute-start | bytes 2064392 | tf_op jit(solution)/shard_map/ppermute | solution.py:519
  20.4 2.8 %shard_map.192 = (bf16[256,6656]{1,0:T(8,128)(2,1)S(1)}, bf16[256,6656]{1,0:T(8,128)(2,1)S(1)}) custom-call(f32[2,52]{1,0:T(2,128)S(1)} %copy-done.9, f32[2,52]{1,0:T(2,128)S(1)} %copy-done.10, bf16[256,6656]{1,0:T(8,128)(2,1)S(1)} %copy-done, bf16[256,6656]{1,0:T(8,128)(2,1)S(1)} %copy-done.1, f32[2688,128]{1,0:T(8,128)S(1)} %get-tuple-element.48.after_ref.own_ref), custom_call_target="tpu_custom_call" | custom-call | flops 3407872 | bytes 13631488 | tf_op jit(solution)/shard_map/pallas_call | solution.py:206
  23.1 12.6 %collective-permute-done.4.one_ref = bf16[2688,128]{1,0:T(8,128)(2,1)S(1)} collective-permute-done((bf16[2688,128]{1,0:T(8,128)(2,1)S(1)}, bf16[2688,128]{1,0:T(8,128)(2,1)S(1)}, u32[]{:S(2)}, u32[]{:S(2)}) %collective-permute-start.4) | collective-permute-done | bytes 688160 | tf_op jit(solution)/shard_map/ppermute | solution.py:519
  37.3 2.3 %collective-permute-start.8 = (bf16[816,128]{1,0:T(8,128)(2,1)S(1)}, bf16[816,128]{1,0:T(8,128)(2,1)S(1)}, u32[]{:S(2)}, u32[]{:S(2)}) collective-permute-start(bf16[816,128]{1,0:T(8,128)(2,1)S(1)} %get-tuple-element.56), channel_id=1, source_target_pairs={{0,4},{1,33},{2,6},{3,35},{4,0},{5,37},{6,2},{7,39},{8,12},{9,41},... | collective-permute-start | bytes 626696 | tf_op jit(solution)/shard_map/ppermute | solution.py:519
  40.7 5.0 %collective-permute-done.7.one_ref = bf16[816,128]{1,0:T(8,128)(2,1)S(1)} collective-permute-done((bf16[816,128]{1,0:T(8,128)(2,1)S(1)}, bf16[816,128]{1,0:T(8,128)(2,1)S(1)}, u32[]{:S(2)}, u32[]{:S(2)}) %collective-permute-start.7) | collective-permute-done | bytes 208928 | tf_op jit(solution)/shard_map/ppermute | solution.py:519
  47.7 4.5 %collective-permute-done.10.arrived_ref = bf16[1008,128]{1,0:T(8,128)(2,1)S(1)} collective-permute-done((bf16[1008,128]{1,0:T(8,128)(2,1)S(1)}, bf16[1008,128]{1,0:T(8,128)(2,1)S(1)}, u32[]{:S(2)}, u32[]{:S(2)}) %collective-permute-start.10) | collective-permute-done | bytes 258080 | tf_op jit(solution)/shard_map/ppermute | solution.py:508
  54.0 3.8 %collective-permute-start.11 = (bf16[400,128]{1,0:T(8,128)(2,1)S(1)}, bf16[400,128]{1,0:T(8,128)(2,1)S(1)}, u32[]{:S(2)}, u32[]{:S(2)}) collective-permute-start(bf16[400,128]{1,0:T(8,128)(2,1)S(1)} %get-tuple-element.61), channel_id=1, source_target_pairs={{0,1},{1,0},{2,3},{3,2},{4,5},{5,4},{6,7},{7,6},{8,9},{9,8},{10,11... | collective-permute-start | bytes 307208 | tf_op jit(solution)/shard_map/ppermute | solution.py:505
  59.3 2.4 %collective-permute-start.14 = (bf16[608,128]{1,0:T(8,128)(2,1)S(1)}, bf16[608,128]{1,0:T(8,128)(2,1)S(1)}, u32[]{:S(2)}, u32[]{:S(2)}) collective-permute-start(bf16[608,128]{1,0:T(8,128)(2,1)S(1)} %shard_map.196.own_ref), channel_id=1, source_target_pairs={{0,6},{1,49},{2,0},{3,51},{4,2},{5,53},{6,4},{7,55},{8,14},{9,57},... | collective-permute-start | bytes 466952 | tf_op jit(solution)/shard_map/ppermute | solution.py:519
  62.4 3.2 %collective-permute-done.14.refs_2_ = bf16[608,128]{1,0:T(8,128)(2,1)S(1)} collective-permute-done((bf16[608,128]{1,0:T(8,128)(2,1)S(1)}, bf16[608,128]{1,0:T(8,128)(2,1)S(1)}, u32[]{:S(2)}, u32[]{:S(2)}) %collective-permute-start.14) | collective-permute-done | bytes 155680 | tf_op jit(solution)/shard_map/ppermute | solution.py:519
  65.5 2.1 %collective-permute-done.13.refs_1_ = bf16[608,128]{1,0:T(8,128)(2,1)S(1)} collective-permute-done((bf16[608,128]{1,0:T(8,128)(2,1)S(1)}, bf16[608,128]{1,0:T(8,128)(2,1)S(1)}, u32[]{:S(2)}, u32[]{:S(2)}) %collective-permute-start.13) | collective-permute-done | bytes 155680 | tf_op jit(solution)/shard_map/ppermute | solution.py:519
  69.6 2.2 %collective-permute-start.20 = (bf16[1856,128]{1,0:T(8,128)(2,1)S(1)}, bf16[1856,128]{1,0:T(8,128)(2,1)S(1)}, u32[]{:S(2)}, u32[]{:S(2)}) collective-permute-start(bf16[1856,128]{1,0:T(8,128)(2,1)S(1)} %shard_map.197.refs_1_), channel_id=1, source_target_pairs={{0,48},{1,7},{2,50},{3,1},{4,52},{5,3},{6,54},{7,5},{8,56},{9,15},... | collective-permute-start | bytes 1425416 | tf_op jit(solution)/shard_map/ppermute | solution.py:519
  72.4 2.6 %collective-permute-start.15 = (bf16[1856,128]{1,0:T(8,128)(2,1)S(1)}, bf16[1856,128]{1,0:T(8,128)(2,1)S(1)}, u32[]{:S(2)}, u32[]{:S(2)}) collective-permute-start(bf16[1856,128]{1,0:T(8,128)(2,1)S(1)} %shard_map.197.refs_1_), channel_id=1, source_target_pairs={{0,1},{1,0},{2,3},{3,2},{4,5},{5,4},{6,7},{7,6},{8,9},{9,8},{10,11... | collective-permute-start | bytes 1425416 | tf_op jit(solution)/shard_map/ppermute | solution.py:505
  75.0 7.4 %collective-permute-done.20.refs_4_ = bf16[1856,128]{1,0:T(8,128)(2,1)S(1)} collective-permute-done((bf16[1856,128]{1,0:T(8,128)(2,1)S(1)}, bf16[1856,128]{1,0:T(8,128)(2,1)S(1)}, u32[]{:S(2)}, u32[]{:S(2)}) %collective-permute-start.20) | collective-permute-done | bytes 475168 | tf_op jit(solution)/shard_map/ppermute | solution.py:519
  82.4 2.9 %collective-permute-start.21 = (bf16[1856,128]{1,0:T(8,128)(2,1)S(1)}, bf16[1856,128]{1,0:T(8,128)(2,1)S(1)}, u32[]{:S(2)}, u32[]{:S(2)}) collective-permute-start(bf16[1856,128]{1,0:T(8,128)(2,1)S(1)} %collective-permute-done.20.refs_4_), channel_id=1, source_target_pairs={{0,1},{1,0},{2,3},{3,2},{4,5},{5,4},{6,7},{7,6},{8,9},{9,8},{10,11... | collective-permute-start | bytes 1425416 | tf_op jit(solution)/shard_map/ppermute | solution.py:505
  86.1 3.0 %collective-permute-start.17 = (bf16[1856,128]{1,0:T(8,128)(2,1)S(1)}, bf16[1856,128]{1,0:T(8,128)(2,1)S(1)}, u32[]{:S(2)}, u32[]{:S(2)}) collective-permute-start(bf16[1856,128]{1,0:T(8,128)(2,1)S(1)} %collective-permute-done.16.refs_2_), channel_id=1, source_target_pairs={{0,1},{1,0},{2,3},{3,2},{4,5},{5,4},{6,7},{7,6},{8,9},{9,8},{10,11... | collective-permute-start | bytes 1425416 | tf_op jit(solution)/shard_map/ppermute | solution.py:505
  91.0 2.1 %shard_map.199 = (bf16[256,128]{1,0:T(8,128)(2,1)S(1)}, bf16[256,128]{1,0:T(8,128)(2,1)S(1)}, bf16[256,128]{1,0:T(8,128)(2,1)S(1)}, bf16[256,128]{1,0:T(8,128)(2,1)S(1)}) custom-call(s32[5]{0:T(128)S(1)} %stack.23.where_ref.refs_0_, bf16[1856,128]{1,0:T(8,128)(2,1)S(1)} %collective-permute-done.15.refs_1_, ...), custom_call_target="tpu_custom_call" | custom-call | tf_op jit(solution)/shard_map/pallas_call | solution.py:221
  94.7 5.1 %collective-permute-start.23 = (bf16[256,128]{1,0:T(8,128)(2,1)S(1)}, bf16[256,128]{1,0:T(8,128)(2,1)S(1)}, u32[]{:S(2)}, u32[]{:S(2)}) collective-permute-start(bf16[256,128]{1,0:T(8,128)(2,1)S(1)} %get-tuple-element.66), channel_id=1, source_target_pairs={{0,128},{64,192},{128,0},{192,64},{1,129},{65,193},{129,1},{193,65... | collective-permute-start | bytes 196616 | tf_op jit(solution)/shard_map/ppermute | solution.py:544
  99.8 2.4 %collective-permute-start.24 = (bf16[256,128]{1,0:T(8,128)(2,1)S(1)}, bf16[256,128]{1,0:T(8,128)(2,1)S(1)}, u32[]{:S(2)}, u32[]{:S(2)}) collective-permute-start(bf16[256,128]{1,0:T(8,128)(2,1)S(1)} %get-tuple-element.67), channel_id=1, source_target_pairs={{0,192},{64,0},{128,64},{192,128},{1,193},{65,1},{129,65},{193,129... | collective-permute-start | bytes 196616 | tf_op jit(solution)/shard_map/ppermute | solution.py:544
  102.2 2.5 %collective-permute-done.23.two_ref = bf16[256,128]{1,0:T(8,128)(2,1)S(1)} collective-permute-done((bf16[256,128]{1,0:T(8,128)(2,1)S(1)}, bf16[256,128]{1,0:T(8,128)(2,1)S(1)}, u32[]{:S(2)}, u32[]{:S(2)}) %collective-permute-start.23) | collective-permute-done | bytes 65568 | tf_op jit(solution)/shard_map/ppermute | solution.py:544
  104.7 2.4 %collective-permute-done.24.three_ref = bf16[256,128]{1,0:T(8,128)(2,1)S(1)} collective-permute-done((bf16[256,128]{1,0:T(8,128)(2,1)S(1)}, bf16[256,128]{1,0:T(8,128)(2,1)S(1)}, u32[]{:S(2)}, u32[]{:S(2)}) %collective-permute-start.24) | collective-permute-done | bytes 65568 | tf_op jit(solution)/shard_map/ppermute | solution.py:544
  (61 shorter events, 19.9 us)
Async XLA Ops:
  6.0 9.9 %collective-permute-start = (bf16[32,104,128]{2,1,0:T(8,128)(2,1)S(1)}, bf16[32,104,128]{2,1,0:T(8,128)(2,1)S(1)}, u32[]{:S(2)}, u32[]{:S(2)}) collective-permute-start(bf16[32,104,128]{2,1,0:T(8,128)(2,1)S(1)} %get-tuple-element.45), channel_id=1, source_target_pairs={{0,1},{1,0},{2,3},{3,2},{4,5},{5,4},{6,7},{7,6},{8,9},{9,8},{10,11... | collective-permute-start | bytes 2555912 | tf_op jit(solution)/shard_map/ppermute | solution.py:505
  9.3 6.6 %collective-permute-start.1 = (bf16[32,104,128]{2,1,0:T(8,128)(2,1)S(1)}, bf16[32,104,128]{2,1,0:T(8,128)(2,1)S(1)}, u32[]{:S(2)}, u32[]{:S(2)}) collective-permute-start(bf16[32,104,128]{2,1,0:T(8,128)(2,1)S(1)} %get-tuple-element.46), channel_id=1, source_target_pairs={{0,1},{1,0},{2,3},{3,2},{4,5},{5,4},{6,7},{7,6},{8,9},{9,8},{10,11... | collective-permute-start | bytes 2555912 | tf_op jit(solution)/shard_map/ppermute | solution.py:505
  13.3 2.6 %collective-permute-start.2 = (bf16[32,104,128]{2,1,0:T(8,128)(2,1)S(1)}, bf16[32,104,128]{2,1,0:T(8,128)(2,1)S(1)}, u32[]{:S(2)}, u32[]{:S(2)}) collective-permute-start(bf16[32,104,128]{2,1,0:T(8,128)(2,1)S(1)} %get-tuple-element.47), channel_id=1, source_target_pairs={{0,1},{1,0},{2,3},{3,2},{4,5},{5,4},{6,7},{7,6},{8,9},{9,8},{10,11... | collective-permute-start | bytes 2555912 | tf_op jit(solution)/shard_map/ppermute | solution.py:505
  17.0 18.7 %collective-permute-start.4 = (bf16[2688,128]{1,0:T(8,128)(2,1)S(1)}, bf16[2688,128]{1,0:T(8,128)(2,1)S(1)}, u32[]{:S(2)}, u32[]{:S(2)}) collective-permute-start(bf16[2688,128]{1,0:T(8,128)(2,1)S(1)} %get-tuple-element.49), channel_id=1, source_target_pairs={{0,16},{1,3},{2,18},{3,5},{4,20},{5,7},{6,22},{7,1},{8,24},{9,11},... | collective-permute-start | bytes 2064392 | tf_op jit(solution)/shard_map/ppermute | solution.py:519
  17.1 18.7 %collective-permute-start.5 = (bf16[2688,128]{1,0:T(8,128)(2,1)S(1)}, bf16[2688,128]{1,0:T(8,128)(2,1)S(1)}, u32[]{:S(2)}, u32[]{:S(2)}) collective-permute-start(bf16[2688,128]{1,0:T(8,128)(2,1)S(1)} %get-tuple-element.50), channel_id=1, source_target_pairs={{0,32},{1,5},{2,34},{3,7},{4,36},{5,1},{6,38},{7,3},{8,40},{9,13},... | collective-permute-start | bytes 2064392 | tf_op jit(solution)/shard_map/ppermute | solution.py:519
  19.3 17.1 %collective-permute-start.6 = (bf16[2688,128]{1,0:T(8,128)(2,1)S(1)}, bf16[2688,128]{1,0:T(8,128)(2,1)S(1)}, u32[]{:S(2)}, u32[]{:S(2)}) collective-permute-start(bf16[2688,128]{1,0:T(8,128)(2,1)S(1)} %get-tuple-element.51), channel_id=1, source_target_pairs={{0,48},{1,7},{2,50},{3,1},{4,52},{5,3},{6,54},{7,5},{8,56},{9,15},... | collective-permute-start | bytes 2064392 | tf_op jit(solution)/shard_map/ppermute | solution.py:519
  37.2 8.5 %collective-permute-start.7 = (bf16[816,128]{1,0:T(8,128)(2,1)S(1)}, bf16[816,128]{1,0:T(8,128)(2,1)S(1)}, u32[]{:S(2)}, u32[]{:S(2)}) collective-permute-start(bf16[816,128]{1,0:T(8,128)(2,1)S(1)} %get-tuple-element.55), channel_id=1, source_target_pairs={{0,2},{1,17},{2,4},{3,19},{4,6},{5,21},{6,0},{7,23},{8,10},{9,25},... | collective-permute-start | bytes 626696 | tf_op jit(solution)/shard_map/ppermute | solution.py:519
  37.3 8.4 %collective-permute-start.8 = (bf16[816,128]{1,0:T(8,128)(2,1)S(1)}, bf16[816,128]{1,0:T(8,128)(2,1)S(1)}, u32[]{:S(2)}, u32[]{:S(2)}) collective-permute-start(bf16[816,128]{1,0:T(8,128)(2,1)S(1)} %get-tuple-element.56), channel_id=1, source_target_pairs={{0,4},{1,33},{2,6},{3,35},{4,0},{5,37},{6,2},{7,39},{8,12},{9,41},... | collective-permute-start | bytes 626696 | tf_op jit(solution)/shard_map/ppermute | solution.py:519
  39.6 6.7 %collective-permute-start.9 = (bf16[816,128]{1,0:T(8,128)(2,1)S(1)}, bf16[816,128]{1,0:T(8,128)(2,1)S(1)}, u32[]{:S(2)}, u32[]{:S(2)}) collective-permute-start(bf16[816,128]{1,0:T(8,128)(2,1)S(1)} %get-tuple-element.57), channel_id=1, source_target_pairs={{0,6},{1,49},{2,0},{3,51},{4,2},{5,53},{6,4},{7,55},{8,14},{9,57},... | collective-permute-start | bytes 626696 | tf_op jit(solution)/shard_map/ppermute | solution.py:519
  47.0 5.3 %collective-permute-start.10 = (bf16[1008,128]{1,0:T(8,128)(2,1)S(1)}, bf16[1008,128]{1,0:T(8,128)(2,1)S(1)}, u32[]{:S(2)}, u32[]{:S(2)}) collective-permute-start(bf16[1008,128]{1,0:T(8,128)(2,1)S(1)} %get-tuple-element.59), channel_id=1, source_target_pairs={{0,8},{1,9},{2,10},{3,11},{4,12},{5,13},{6,14},{7,15},{8,0},{9,1},... | collective-permute-start | bytes 774152 | tf_op jit(solution)/shard_map/ppermute | solution.py:508
  54.0 4.7 %collective-permute-start.11 = (bf16[400,128]{1,0:T(8,128)(2,1)S(1)}, bf16[400,128]{1,0:T(8,128)(2,1)S(1)}, u32[]{:S(2)}, u32[]{:S(2)}) collective-permute-start(bf16[400,128]{1,0:T(8,128)(2,1)S(1)} %get-tuple-element.61), channel_id=1, source_target_pairs={{0,1},{1,0},{2,3},{3,2},{4,5},{5,4},{6,7},{7,6},{8,9},{9,8},{10,11... | collective-permute-start | bytes 307208 | tf_op jit(solution)/shard_map/ppermute | solution.py:505
  59.3 6.3 %collective-permute-start.14 = (bf16[608,128]{1,0:T(8,128)(2,1)S(1)}, bf16[608,128]{1,0:T(8,128)(2,1)S(1)}, u32[]{:S(2)}, u32[]{:S(2)}) collective-permute-start(bf16[608,128]{1,0:T(8,128)(2,1)S(1)} %shard_map.196.own_ref), channel_id=1, source_target_pairs={{0,6},{1,49},{2,0},{3,51},{4,2},{5,53},{6,4},{7,55},{8,14},{9,57},... | collective-permute-start | bytes 466952 | tf_op jit(solution)/shard_map/ppermute | solution.py:519
  61.7 5.9 %collective-permute-start.13 = (bf16[608,128]{1,0:T(8,128)(2,1)S(1)}, bf16[608,128]{1,0:T(8,128)(2,1)S(1)}, u32[]{:S(2)}, u32[]{:S(2)}) collective-permute-start(bf16[608,128]{1,0:T(8,128)(2,1)S(1)} %shard_map.196.own_ref), channel_id=1, source_target_pairs={{0,4},{1,33},{2,6},{3,35},{4,0},{5,37},{6,2},{7,39},{8,12},{9,41},... | collective-permute-start | bytes 466952 | tf_op jit(solution)/shard_map/ppermute | solution.py:519
  61.7 7.3 %collective-permute-start.12 = (bf16[608,128]{1,0:T(8,128)(2,1)S(1)}, bf16[608,128]{1,0:T(8,128)(2,1)S(1)}, u32[]{:S(2)}, u32[]{:S(2)}) collective-permute-start(bf16[608,128]{1,0:T(8,128)(2,1)S(1)} %shard_map.196.own_ref), channel_id=1, source_target_pairs={{0,2},{1,17},{2,4},{3,19},{4,6},{5,21},{6,0},{7,23},{8,10},{9,25},... | collective-permute-start | bytes 466952 | tf_op jit(solution)/shard_map/ppermute | solution.py:519
  69.6 12.8 %collective-permute-start.20 = (bf16[1856,128]{1,0:T(8,128)(2,1)S(1)}, bf16[1856,128]{1,0:T(8,128)(2,1)S(1)}, u32[]{:S(2)}, u32[]{:S(2)}) collective-permute-start(bf16[1856,128]{1,0:T(8,128)(2,1)S(1)} %shard_map.197.refs_1_), channel_id=1, source_target_pairs={{0,48},{1,7},{2,50},{3,1},{4,52},{5,3},{6,54},{7,5},{8,56},{9,15},... | collective-permute-start | bytes 1425416 | tf_op jit(solution)/shard_map/ppermute | solution.py:519
  71.7 13.6 %collective-permute-start.18 = (bf16[1856,128]{1,0:T(8,128)(2,1)S(1)}, bf16[1856,128]{1,0:T(8,128)(2,1)S(1)}, u32[]{:S(2)}, u32[]{:S(2)}) collective-permute-start(bf16[1856,128]{1,0:T(8,128)(2,1)S(1)} %shard_map.197.refs_1_), channel_id=1, source_target_pairs={{0,32},{1,5},{2,34},{3,7},{4,36},{5,1},{6,38},{7,3},{8,40},{9,13},... | collective-permute-start | bytes 1425416 | tf_op jit(solution)/shard_map/ppermute | solution.py:519
  72.0 14.1 %collective-permute-start.16 = (bf16[1856,128]{1,0:T(8,128)(2,1)S(1)}, bf16[1856,128]{1,0:T(8,128)(2,1)S(1)}, u32[]{:S(2)}, u32[]{:S(2)}) collective-permute-start(bf16[1856,128]{1,0:T(8,128)(2,1)S(1)} %shard_map.197.refs_1_), channel_id=1, source_target_pairs={{0,16},{1,3},{2,18},{3,5},{4,20},{5,7},{6,22},{7,1},{8,24},{9,11},... | collective-permute-start | bytes 1425416 | tf_op jit(solution)/shard_map/ppermute | solution.py:519
  72.4 18.5 %collective-permute-start.15 = (bf16[1856,128]{1,0:T(8,128)(2,1)S(1)}, bf16[1856,128]{1,0:T(8,128)(2,1)S(1)}, u32[]{:S(2)}, u32[]{:S(2)}) collective-permute-start(bf16[1856,128]{1,0:T(8,128)(2,1)S(1)} %shard_map.197.refs_1_), channel_id=1, source_target_pairs={{0,1},{1,0},{2,3},{3,2},{4,5},{5,4},{6,7},{7,6},{8,9},{9,8},{10,11... | collective-permute-start | bytes 1425416 | tf_op jit(solution)/shard_map/ppermute | solution.py:505
  82.4 8.5 %collective-permute-start.21 = (bf16[1856,128]{1,0:T(8,128)(2,1)S(1)}, bf16[1856,128]{1,0:T(8,128)(2,1)S(1)}, u32[]{:S(2)}, u32[]{:S(2)}) collective-permute-start(bf16[1856,128]{1,0:T(8,128)(2,1)S(1)} %collective-permute-done.20.refs_4_), channel_id=1, source_target_pairs={{0,1},{1,0},{2,3},{3,2},{4,5},{5,4},{6,7},{7,6},{8,9},{9,8},{10,11... | collective-permute-start | bytes 1425416 | tf_op jit(solution)/shard_map/ppermute | solution.py:505
  85.3 5.6 %collective-permute-start.19 = (bf16[1856,128]{1,0:T(8,128)(2,1)S(1)}, bf16[1856,128]{1,0:T(8,128)(2,1)S(1)}, u32[]{:S(2)}, u32[]{:S(2)}) collective-permute-start(bf16[1856,128]{1,0:T(8,128)(2,1)S(1)} %collective-permute-done.18.refs_3_), channel_id=1, source_target_pairs={{0,1},{1,0},{2,3},{3,2},{4,5},{5,4},{6,7},{7,6},{8,9},{9,8},{10,11... | collective-permute-start | bytes 1425416 | tf_op jit(solution)/shard_map/ppermute | solution.py:505
  86.1 4.8 %collective-permute-start.17 = (bf16[1856,128]{1,0:T(8,128)(2,1)S(1)}, bf16[1856,128]{1,0:T(8,128)(2,1)S(1)}, u32[]{:S(2)}, u32[]{:S(2)}) collective-permute-start(bf16[1856,128]{1,0:T(8,128)(2,1)S(1)} %collective-permute-done.16.refs_2_), channel_id=1, source_target_pairs={{0,1},{1,0},{2,3},{3,2},{4,5},{5,4},{6,7},{7,6},{8,9},{9,8},{10,11... | collective-permute-start | bytes 1425416 | tf_op jit(solution)/shard_map/ppermute | solution.py:505
  93.1 9.1 %collective-permute-start.22 = (bf16[256,128]{1,0:T(8,128)(2,1)S(1)}, bf16[256,128]{1,0:T(8,128)(2,1)S(1)}, u32[]{:S(2)}, u32[]{:S(2)}) collective-permute-start(bf16[256,128]{1,0:T(8,128)(2,1)S(1)} %get-tuple-element.65), channel_id=1, source_target_pairs={{0,64},{64,128},{128,192},{192,0},{1,65},{65,129},{129,193},{193,1... | collective-permute-start | bytes 196616 | tf_op jit(solution)/shard_map/ppermute | solution.py:544
  94.7 10.0 %collective-permute-start.23 = (bf16[256,128]{1,0:T(8,128)(2,1)S(1)}, bf16[256,128]{1,0:T(8,128)(2,1)S(1)}, u32[]{:S(2)}, u32[]{:S(2)}) collective-permute-start(bf16[256,128]{1,0:T(8,128)(2,1)S(1)} %get-tuple-element.66), channel_id=1, source_target_pairs={{0,128},{64,192},{128,0},{192,64},{1,129},{65,193},{129,1},{193,65... | collective-permute-start | bytes 196616 | tf_op jit(solution)/shard_map/ppermute | solution.py:544
  99.8 7.3 %collective-permute-start.24 = (bf16[256,128]{1,0:T(8,128)(2,1)S(1)}, bf16[256,128]{1,0:T(8,128)(2,1)S(1)}, u32[]{:S(2)}, u32[]{:S(2)}) collective-permute-start(bf16[256,128]{1,0:T(8,128)(2,1)S(1)} %get-tuple-element.67), channel_id=1, source_target_pairs={{0,192},{64,0},{128,64},{192,128},{1,193},{65,1},{129,65},{193,129... | collective-permute-start | bytes 196616 | tf_op jit(solution)/shard_map/ppermute | solution.py:544
  (12 other events, 128.6 us)

commit v3 on v2

--- a/solution.py
+++ b/solution.py
@@ -16,6 +16,7 @@
 CHUNK = 512
 FIRST_PARTS = (1024, 2048, 3584)
 LATER_PARTS = (6656,)
+PIECES = (0, 1, 3, 2)
 
 
 def params():
@@ -69,8 +70,8 @@
 
 
 def split_by_core(core, sums_ref, send_ref, keep_ref):
-    chips, piece = send_ref.shape[:2]
-    for chip in range(chips):
+    piece = send_ref.shape[1]
+    for chip in range(sums_ref.shape[0] // (2 * piece)):
         start = chip * 2 * piece
         mine = pl.multiple_of(start + core * piece, 8)
         theirs = pl.multiple_of(start + (1 - core) * piece, 8)
@@ -103,7 +104,7 @@
 
 def wide_kernel(
     where_ref, gate_scales_hbm, up_scales_hbm, tokens_hbm, gradient_hbm, gate_reduce_hbm, up_reduce_hbm,
-    down_expand_hbm, gate_hbm, up_hbm, gate_send, gate_keep, up_send, up_keep, low_ref,
+    down_expand_hbm, gate_hbm, up_hbm, gate_send, gate_keep, up_send, up_keep,
     gate_scales, up_scales, tokens_ref, gradient_ref, gate_reduce_ref, up_reduce_ref, down_expand_ref, gate_ref, up_ref, sums_ref, small, sems,
 ):
     small_copies = fetch_all(
@@ -129,9 +130,19 @@
     for copy in small_copies[3:]:
         copy.wait()
     rank = gate_reduce_ref.shape[0]
-    low_ref[:rank] = dot(gate_reduce_ref[...], tokens_ref[...], 1, 1).astype(BF16)
-    low_ref[rank : 2 * rank] = dot(up_reduce_ref[...], tokens_ref[...], 1, 1).astype(BF16)
-    low_ref[2 * rank :] = dot(down_expand_ref[...], gradient_ref[...], 1, 1).astype(BF16)
+    chips, rows = gate_keep.shape[0], 3 * rank // 2
+    low = jnp.concatenate(
+        [
+            dot(gate_reduce_ref[...], tokens_ref[...], 1, 1),
+            dot(up_reduce_ref[...], tokens_ref[...], 1, 1),
+            dot(down_expand_ref[...], gradient_ref[...], 1, 1),
+        ],
+        axis=0,
+    ).astype(BF16)
+    for out_ref in (up_send, up_keep):
+        for block in range(2):
+            out_ref[chips + block, :rows] = low[block * rows : (block + 1) * rows]
+            out_ref[chips + block, rows:] = jnp.zeros_like(out_ref[chips + block, rows:])
 
 
 def tall_kernel(
@@ -159,9 +170,9 @@
     return pl.pallas_call(
         wide_kernel,
         in_specs=[smem()] + [hbm] * 9,
-        out_specs=[vmem] * 5,
-        out_shape=[jax.ShapeDtypeStruct((chips, piece, count), BF16)] * 4
-        + [jax.ShapeDtypeStruct((3 * gate_reduce.shape[0], count), BF16)],
+        out_specs=[vmem] * 4,
+        out_shape=[jax.ShapeDtypeStruct((chips, piece, count), BF16)] * 2
+        + [jax.ShapeDtypeStruct((chips + 2, piece, count), BF16)] * 2,
         scratch_shapes=[pltpu.SMEM(gate_scales.shape, F32)] * 2
         + [pltpu.VMEM(value.shape, BF16) for value in fetched]
         + [
@@ -194,26 +205,34 @@
     )(where, stay(scales), stay(gradient), stay(values), after)
 
 
-def weights_kernel(gate_scales, up_scales, gate_ref, up_ref, after_ref, gate_out, up_out):
+def weights_kernel(
+    gate_scales, up_scales, gate_ref, up_ref, gate_expand, up_expand, down_reduce, after_ref, gate_out, up_out, expand_ref
+):
+    @pl.when(pl.program_id(0) == 0)
+    def _():
+        for kind, ref in enumerate((gate_expand, up_expand, down_reduce)):
+            expand_ref[kind] = ref[...]
+
     first = pl.program_id(0) * (gate_ref.shape[1] // BLOCK)
     gate_out[...] = dequantize_wide(gate_ref[...], gate_scales, first)
     up_out[...] = dequantize_wide(up_ref[...], up_scales, first)
 
 
-def weights(gate_scales, up_scales, gate, up, after):
+def weights(gate_scales, up_scales, gate, up, expands, after):
     width, hidden = gate.shape
+    small = expands[0].shape
     block = pl.BlockSpec((width, hidden // STEPS), lambda i: (0, i))
     return pl.pallas_call(
         weights_kernel,
         grid=(STEPS,),
-        in_specs=[smem(), smem(), block, block, pl.BlockSpec(memory_space=pl.ANY)],
-        out_specs=[block] * 2,
-        out_shape=[jax.ShapeDtypeStruct(gate.shape, BF16)] * 2,
+        in_specs=[smem(), smem(), block, block] + [whole(small)] * 3 + [pl.BlockSpec(memory_space=pl.ANY)],
+        out_specs=[block] * 2 + [whole((3,) + small)],
+        out_shape=[jax.ShapeDtypeStruct(gate.shape, BF16)] * 2 + [jax.ShapeDtypeStruct((3,) + small, BF16)],
         compiler_params=params(),
         cost_estimate=pl.CostEstimate(
             flops=2 * width * hidden, bytes_accessed=8 * width * hidden, transcendentals=0
         ),
-    )(gate_scales, up_scales, gate, up, after)
+    )(gate_scales, up_scales, gate, up, *expands, after)
 
 
 def vmem_call(kernel, out_shape, *args, scratch=(), unread=0):
@@ -232,119 +251,145 @@
     return jnp.where(core == 0, first * 8 + z * 4 + second, second * 8 + z * 4 + first)
 
 
-def pack_kernel(where_ref, *refs):
-    keeps, received, outs = refs[:4], refs[4:8], refs[8:]
-    core, first, second = where_ref[0], where_ref[3], where_ref[4]
-    low = keeps[3][...].astype(F32) + received[3][...].astype(F32)
-    pair = 6 * keeps[0].shape[1]
-    for offset, out_ref in enumerate(outs):
-        there = lax.rem(first + offset, 4)
+def pack_rows(where_ref, keeps, received, offset, step):
+    there = lax.rem(where_ref[3] + offset, 4)
+    parts = []
+    for near in range(2):
+        chip = chip_of(where_ref[0], there, near, lax.rem(where_ref[4] + step, 4))
+        parts += [keep[chip].astype(F32) + got[chip].astype(F32) for keep, got in zip(keeps, received)]
+    return jnp.concatenate(parts, axis=0)
+
+
+def pack_low(keep_ref, received_ref, rows):
+    blocks = keep_ref.shape[0] - 2
+    return jnp.concatenate(
+        [keep_ref[blocks + i, :rows].astype(F32) + received_ref[blocks + i, :rows].astype(F32) for i in range(2)],
+        axis=0,
+    )
+
+
+def stage_kernel(kinds, offsets, where_ref, *refs):
+    keeps, received, outs = refs[:kinds], refs[kinds : 2 * kinds], refs[-len(offsets) :]
+    pair = 2 * kinds * keeps[0].shape[1]
+    for offset, out_ref in zip(offsets, outs):
         for step in range(4):
-            parts = []
-            for near in range(2):
-                chip = chip_of(core, there, near, lax.rem(second + step, 4))
-                parts += [keeps[k][chip].astype(F32) + received[k][chip].astype(F32) for k in range(3)]
-            out_ref[step * pair : (step + 1) * pair] = jnp.concatenate(parts, axis=0).astype(out_ref.dtype)
-        out_ref[4 * pair :] = low.astype(out_ref.dtype)
-
-
-def pack(where, keeps, received):
-    _, piece, tokens = keeps[0].shape
-    rows = 24 * piece + keeps[3].shape[0]
+            rows = pack_rows(where_ref, keeps, received, offset, step)
+            out_ref[step * pair : (step + 1) * pair] = rows.astype(out_ref.dtype)
+        low_rows = out_ref.shape[0] - 4 * pair
+        if low_rows:
+            out_ref[4 * pair :] = pack_low(keeps[-1], received[-1], low_rows // 2).astype(out_ref.dtype)
+
+
+def stage(offsets, where, keeps, received, low_rows=0, after=()):
+    chips, piece, tokens = keeps[0].shape
+    rows = 8 * len(keeps) * piece + low_rows
+    out_shape = [jax.ShapeDtypeStruct((rows, tokens), BF16 if offset else F32) for offset in offsets]
+    kernel = functools.partial(stage_kernel, len(keeps), offsets)
+    return vmem_call(kernel, out_shape, where, *keeps, *received, *after, unread=len(after))
+
+
+def second_kernel(where_ref, *refs):
+    wide, tall, outs = refs[:4], refs[4:8], refs[-4:]
+    down = tall[0].shape[0] // 4
+    pair = 2 * down
+
+    def add(refs, first, count):
+        rows = slice(first, first + count)
+        total = refs[0][rows]
+        for ref in refs[1:]:
+            total = total + ref[rows].astype(F32)
+        return total
+
+    low = add(wide, 4 * pair, wide[0].shape[0] - 4 * pair)
+    for step, out_ref in enumerate(outs):
+        out_ref[:pair] = add(wide, step * pair, pair).astype(out_ref.dtype)
+        out_ref[pair : pair + down] = add(tall, step * down, down).astype(out_ref.dtype)
+        out_ref[pair + down :] = low.astype(out_ref.dtype)
+
+
+def second(where, wide, tall, piece, ready):
+    rows, tokens = wide[0].shape
+    rows -= 10 * piece
     out_shape = [jax.ShapeDtypeStruct((rows, tokens), F32 if i == 0 else BF16) for i in range(4)]
-    return vmem_call(pack_kernel, out_shape, where, *keeps, *received)
-
-
-def second_kernel(where_ref, own_ref, one_ref, two_ref, three_ref, gate_ref, up_ref, *outs):
-    pair = (own_ref.shape[0] - outs[0].shape[0]) // 3
-
-    def add(first, count):
-        rows = slice(first, first + count)
-        arrived = one_ref[rows].astype(F32) + two_ref[rows].astype(F32) + three_ref[rows].astype(F32)
-        return own_ref[rows] + arrived
-
-    low = add(4 * pair, own_ref.shape[0] - 4 * pair)
-    for step, out_ref in enumerate(outs):
-        out_ref[:pair] = add(step * pair, pair).astype(out_ref.dtype)
-        out_ref[pair:] = low.astype(out_ref.dtype)
-
-
-def second(where, own, arrived, piece, ready):
-    rows, tokens = own.shape
-    rows -= 18 * piece
-    out_shape = [jax.ShapeDtypeStruct((rows, tokens), F32 if i == 0 else BF16) for i in range(4)]
-    return vmem_call(second_kernel, out_shape, where, own, *arrived, *ready, unread=2)
-
-
-def third_kernel(
-    where_ref, own_ref, one_ref, two_ref, three_ref, gate_expand_ref, up_expand_ref, down_reduce_ref, keep_ref, send_ref
-):
+    return vmem_call(second_kernel, out_shape, where, *wide, *tall, *ready, unread=len(ready))
+
+
+def third_kernel(where_ref, own_ref, one_ref, two_ref, three_ref, expand_ref, keep_ref, send_ref):
     rows, count = keep_ref.shape
     arrived = one_ref[...].astype(F32) + two_ref[...].astype(F32) + three_ref[...].astype(F32)
     everything = own_ref[...] + arrived
     keep_ref[...] = everything
     send_ref[:rows] = everything.astype(BF16)
-    rank, piece = gate_expand_ref.shape
-    for kind, ref in enumerate((gate_expand_ref, up_expand_ref, down_reduce_ref)):
+    _, rank, piece = expand_ref.shape
+    for kind in range(3):
         place = slice(rows + kind * rank, rows + (kind + 1) * rank)
-        send_ref[place, :piece] = ref[...]
+        send_ref[place, :piece] = expand_ref[kind]
         send_ref[place, piece:] = jnp.zeros((rank, count - piece), BF16)
 
 
-def third(where, own, arrived, expands):
+def third(where, own, arrived, expand):
     rows, count = own.shape
-    far_rows = rows + 3 * expands[0].shape[0]
+    far_rows = rows + 3 * expand.shape[1]
     out_shape = [jax.ShapeDtypeStruct(own.shape, F32), jax.ShapeDtypeStruct((far_rows, count), BF16)]
-    return vmem_call(third_kernel, out_shape, where, own, *arrived, *expands)
+    return vmem_call(third_kernel, out_shape, where, own, *arrived, expand)
 
 
 def middle_kernel(
-    where_ref, own_ref, arrived_ref, gate_expand_ref, up_expand_ref, down_reduce_ref,
-    send_ref, keep_ref, gate_out, up_out, down_out, expands_ref, grads_ref,
+    where_ref, own_ref, arrived_ref, expand_ref,
+    send_ref, keep_ref, gate_out, up_out, down_out, expands_ref, grads_ref, ranks_ref,
 ):
     core, z = where_ref[0], where_ref[2]
-    rank, piece = gate_expand_ref.shape
+    _, rank, piece = expand_ref.shape
+    half = rank // 2
     rows = own_ref.shape[0]
     sums = own_ref[...] + arrived_ref[:rows].astype(F32)
-    for kind, ref in enumerate((gate_expand_ref, up_expand_ref, down_reduce_ref)):
-        expands_ref[z, kind] = ref[...]
+    expands_ref[z] = expand_ref[...]
+    for kind in range(3):
         expands_ref[1 - z, kind] = arrived_ref[rows + kind * rank : rows + (kind + 1) * rank, :piece]
     lows = [sums[6 * piece + k * rank : 6 * piece + (k + 1) * rank].astype(BF16) for k in range(3)]
     keeps, sends, ranks = [], [], [0.0] * 3
-    first = core == 0
     for chip in range(2):
-        start = 3 * piece * chip
+        starts = (2 * piece * chip, 2 * piece * chip + piece, 4 * piece + piece * chip)
         gate, upper, back = [
-            sums[start + kind * piece : start + (kind + 1) * piece]
-            + SCALE * dot(expands_ref[chip, kind], lows[kind], 0, 0)
-            for kind in range(3)
+            sums[start : start + piece] + SCALE * dot(expands_ref[chip, kind], lows[kind], 0, 0)
+            for kind, start in enumerate(starts)
         ]
         sigma = jax.nn.sigmoid(gate)
         activated = gate * sigma
         hidden = activated * upper
         grad_gate = back * upper * sigma * (1.0 + gate * (1.0 - sigma))
         grad_upper = back * activated
-        keeps.append(jnp.where(first, grad_gate, grad_upper))
-        sends.append(jnp.where(first, grad_upper, grad_gate))
+        keeps.append(jnp.where(core == 0, grad_gate, grad_upper))
+        sends.append(jnp.where(core == 0, grad_upper, grad_gate))
         for kind, grad in enumerate((grad_gate, grad_upper, hidden)):
             grads_ref[chip, kind] = grad.astype(BF16)
             ranks[kind] = ranks[kind] + dot(expands_ref[chip, kind], grads_ref[chip, kind], 1, 0)
-    keep_ref[...] = jnp.concatenate([*keeps, *ranks], axis=0)
-    send_ref[...] = jnp.concatenate([*sends, *ranks], axis=0).astype(BF16)
+    for kind in range(3):
+        ranks_ref[kind] = ranks[kind]
+    mine = pl.multiple_of(core * half, half)
+    theirs = pl.multiple_of((1 - core) * half, half)
+    keeps += [ranks_ref[kind, pl.ds(mine, half), :] for kind in range(3)]
+    sends += [ranks_ref[kind, pl.ds(theirs, half), :] for kind in range(3)]
+    keep_ref[...] = jnp.concatenate(keeps, axis=0)
+    send_ref[...] = jnp.concatenate(sends, axis=0).astype(BF16)
     for kind, out_ref in enumerate((gate_out, up_out, down_out)):
         out_ref[...] = SCALE * dot(lows[kind], grads_ref[z, kind], 1, 1)
 
 
-def middle(where, own, arrived, expands):
-    rank, piece = expands[0].shape
+def middle(where, own, arrived, expand):
+    _, rank, piece = expand.shape
     tokens = own.shape[1]
-    rows = 2 * piece + 3 * rank
+    rows = 2 * piece + 3 * rank // 2
     out_shape = [
         jax.ShapeDtypeStruct((rows, tokens), BF16),
         jax.ShapeDtypeStruct((rows, tokens), F32),
     ] + [jax.ShapeDtypeStruct((rank, piece), F32)] * 3
-    scratch = [pltpu.VMEM((2, 3, rank, piece), BF16), pltpu.VMEM((2, 3, piece, tokens), BF16)]
-    return vmem_call(middle_kernel, out_shape, where, own, arrived, *expands, scratch=scratch)
+    scratch = [
+        pltpu.VMEM((2, 3, rank, piece), BF16),
+        pltpu.VMEM((2, 3, piece, tokens), BF16),
+        pltpu.VMEM((3, rank, tokens), F32),
+    ]
+    return vmem_call(middle_kernel, out_shape, where, own, arrived, expand, scratch=scratch)
 
 
 def pair_kernel(piece, where_ref, keep_ref, arrived_ref, out_ref):
@@ -371,7 +416,7 @@
     unit = (out_ref.shape[0] - own_ref.shape[0]) // (count - 1)
     place = where_ref[slot]
     rank = own_ref[unit:].astype(F32)
-    for offset, ref in enumerate([own_ref, *arrived]):
+    for offset, ref in zip(PIECES, [own_ref, *arrived]):
         start = pl.multiple_of(lax.rem(place + count - offset, count) * unit, 16)
         out_ref[pl.ds(start, unit), :] = ref[:unit]
         if offset:
@@ -395,7 +440,7 @@
     place = where_ref[4] if last else where_ref[3]
     part = grads_ref.shape[0] // 4
     unit = part // 8
-    for offset, ref in enumerate(pieces):
+    for offset, ref in zip(PIECES, pieces):
         there = lax.rem(place + 4 - offset, 4)
         for other in range(4):
             for z in range(2):
@@ -410,18 +455,24 @@
             product = dot(weight_ref[...], grads_ref[...], 1, 0)
             total_ref[...] = product + before_ref[...] if last else product
 
+    rank = pieces[0][part:].astype(F32)
+    for ref in pieces[1:]:
+        rank = rank + ref[part:].astype(F32)
     if last:
+        half = rank.shape[0] // 3
+        ranks = []
+        for kind in range(3):
+            rows = slice(kind * half, (kind + 1) * half)
+            ranks.append(jnp.where(core == 0, rank[rows], rank_ref[rows]))
+            ranks.append(jnp.where(core == 0, rank_ref[rows], rank[rows]))
         turned_ref[...] = total_ref[...].T
         share = turned_ref.shape[0] // 4
         for offset, out_ref in enumerate([own_ref, to_one, to_two, to_three]):
             start = pl.multiple_of(lax.rem(where_ref[1] + offset, 4) * share, share)
             piece = turned_ref[pl.ds(start, share), :]
-            block = jnp.concatenate([piece[:, :BLOCK], piece[:, BLOCK:], rank_ref[...]], axis=0)
+            block = jnp.concatenate([piece[:, :BLOCK], piece[:, BLOCK:], *ranks], axis=0)
             out_ref[...] = block.astype(BF16)
     else:
-        rank = pieces[0][part:].astype(F32)
-        for ref in pieces[1:]:
-            rank = rank + ref[part:].astype(F32)
         rank_ref[...] = rank
 
 
@@ -431,7 +482,7 @@
     rank_rows = rows - hidden // 4
     scratch = [pltpu.VMEM((hidden, tokens), BF16)]
     if last:
-        out_shape = [jax.ShapeDtypeStruct((tokens // 4 * width // BLOCK + rank_rows, tokens), BF16)] * 4
+        out_shape = [jax.ShapeDtypeStruct((tokens // 4 * width // BLOCK + 2 * rank_rows, tokens), BF16)] * 4
         scratch += [pltpu.VMEM((width, tokens), F32), pltpu.VMEM((tokens, width), F32)]
     else:
         out_shape = [
@@ -507,36 +558,43 @@
     def along_z(value):
         return lax.ppermute(value, "row", [(i, i ^ 8) for i in range(64)])
 
-    def along(second_axis, values):
-        out = [None] * 3
-        for offset in (2, 1, 3):
-            pairs = []
-            for i in range(64):
-                if (i % 2 == 0) != second_axis:
-                    pairs.append((i, (i + 16 * offset) % 64))
-                else:
-                    pairs.append((i, i - (i // 2 % 4) * 2 + ((i // 2 + offset) % 4) * 2))
-            out[offset - 1] = lax.ppermute(values[offset - 1], "row", pairs)
-        return out
-
-    expands = (gate_expand, up_expand, down_reduce)
-    *wide, low = wide_sums(
+    def along(second_axis, offset, value):
+        pairs = []
+        for i in range(64):
+            if (i % 2 == 0) != second_axis:
+                pairs.append((i, (i + 16 * offset) % 64))
+            else:
+                pairs.append((i, i - (i // 2 % 4) * 2 + ((i // 2 + offset) % 4) * 2))
+        return lax.ppermute(value, "row", pairs)
+
+    def along_all(second_axis, values, order=(2, 1, 3)):
+        return [along(second_axis, offset, values[offset - 1]) for offset in order]
+
+    low_rows = 3 * gate_expand.shape[0]
+    gate_send, gate_keep, up_send, up_keep = wide_sums(
         where, gate_scales, up_scales, tokens, output_gradient, gate_reduce_factor, up_reduce_factor, down_expand,
         gate_values, up_values, piece,
     )
-    tall = tall_sums(where, down_scales.T, output_gradient, down_values, piece, low)
-    sends = [wide[0], wide[2], tall[0], low]
-    own, *out = pack(where, [wide[1], wide[3], tall[1], low], [exchange(send) for send in sends])
-    gate_weight, up_weight = weights(gate_scales, up_scales, gate_values, up_values, own)
-    own, *out = second(where, own, along(False, out), piece, (gate_weight, up_weight))
-    own, out = third(where, own, along(True, out), expands)
+    down_send, down_keep = tall_sums(where, down_scales.T, output_gradient, down_values, piece, gate_keep)
+    keeps, received = [gate_keep, up_keep], [exchange(gate_send), exchange(up_send)]
+    own, *out = stage((0, 1, 2, 3), where, keeps, received, low_rows)
+    wide = [own, *along_all(False, out, (1, 2, 3))]
+    keeps, received = [down_keep], [exchange(down_send)]
+    own, one, two = stage((0, 1, 2), where, keeps, received, after=(own,))
+    (three,) = stage((3,), where, keeps, received, after=(wide[1],))
+    tall = [own, along(False, 1, one), along(False, 2, two), along(False, 3, three)]
+    gate_weight, up_weight, expand = weights(
+        gate_scales, up_scales, gate_values, up_values, (gate_expand, up_expand, down_reduce), own
+    )
+    own, *out = second(where, wide, tall, piece, (gate_weight, up_weight))
+    own, out = third(where, own, along_all(True, out), expand)
     send, keep, gate_expand_gradient, up_expand_gradient, down_reduce_gradient = middle(
-        where, own, along_z(out), expands
-    )
-    rank_rows = low.shape[0]
+        where, own, along_z(out), expand
+    )
+    rank_rows = low_rows // 2
     block = pair_block(where, keep, exchange(send), piece)
-    block = join(4, where, block, along(True, [block] * 3), rank_rows)
-    mine = [block, *along(False, [block] * 3)]
+    block = join(4, where, block, along_all(True, [block] * 3, PIECES[1:]), rank_rows)
+    mine = [block, *along_all(False, [block] * 3, PIECES[1:])]
     theirs = [exchange(value) for value in mine]
     begun = back(False, where, mine, gate_weight, up_weight)
     own, *out = back(True, where, theirs, gate_weight, up_weight, begun)

time: 109 us -> 103 us (0.945)
  waiting for transfers between devices: 46 us -> 36.2 us
  starting transfers between devices: 38.9 us -> 42.2 us
    ppermute x12 -> x15, waiting for transfers between devices: 33.6 us -> 25.1 us  [along(): return lax.ppermute(value, 'row', pairs)]
    ppermute x12 -> x15, starting transfers between devices: 12.8 us -> 15.4 us  [along(): return lax.ppermute(value, 'row', pairs)]
    ppermute x9 -> x8, waiting for transfers between devices: 2.93 us -> 0.99 us  [exchange(): return lax.ppermute(value, 'row', [(i, i ^ 1) for i in range(64)])]
    ppermute x3, starting transfers between devices: 9.09 us -> 10.4 us  [per_device(): lax.ppermute(value, 'col', [(i, (i + offset) % 4) for i in range(4)])]
    pallas_call x8 -> x10, Pallas kernels: 9.34 us -> 10.5 us  [vmem_call(): pl.pallas_call(kernel, in_specs=[smem()] + [vmem] * (len(args) - 1 - unre...]
    ppermute x9 -> x8, starting transfers between devices: 16.3 us -> 16.2 us  [exchange(): return lax.ppermute(value, 'row', [(i, i ^ 1) for i in range(64)])]
  transfers between devices with their start and end apart: 25 -> 27, of which waited for: 14 -> 15; matrix products, arithmetic and copies ran while one was open for 0% -> 0% of each run, Pallas kernels for 8% -> 10%
where the time goes in v3:
time: 103 us
  starting transfers between devices  42.2 us (41%)
  waiting for transfers between devices  36.2 us (35%)
  Pallas kernels  23.6 us (23%)
    ppermute x15, waiting for transfers between devices, along(): return lax.ppermute(value, 'row', pairs)  25.1 us
    ppermute x8, starting transfers between devices, exchange(): return lax.ppermute(value, 'row', [(i, i ^ 1) for i in range(64)])  16.2 us
    ppermute x15, starting transfers between devices, along(): return lax.ppermute(value, 'row', pairs)  15.4 us
    pallas_call x10, Pallas kernels, vmem_call(): pl.pallas_call(kernel, in_specs=[smem()] + [vmem] * (len(args) - 1 - unre...  10.5 us
    ppermute x3, starting transfers between devices, per_device(): lax.ppermute(value, 'col', [(i, (i + offset) % 4) for i in range(4)])  10.4 us
    pallas_call x1, Pallas kernels, wide_sums(): pl.pallas_call(wide_kernel, in_specs=[smem()] + [hbm] * 9, out_specs=[vme...  5.29 us
    ppermute x1, waiting for transfers between devices, along_z(): return lax.ppermute(value, 'row', [(i, i ^ 8) for i in range(64)])  5.09 us
    ppermute x3, waiting for transfers between devices, per_device(): lax.ppermute(value, 'col', [(i, (i + offset) % 4) for i in range(4)])  5.05 us
  transfers between devices with their start and end apart: 27, of which 15 were waited for; matrix products, arithmetic and copies ran while one was open for 0% of the time, Pallas kernels for 10%

profile of v3, /device:TPU:1, one launch (start us, length us, event | category | flops | bytes accessed | tf_op | source)
XLA Modules:
  0.0 103.1 jit_solution(7582960795395318609)
XLA Ops:
  0.7 5.3 %shard_map.189 = (bf16[32,104,128]{2,1,0:T(8,128)(2,1)S(1)}, bf16[32,104,128]{2,1,0:T(8,128)(2,1)S(1)}, bf16[34,104,128]{2,1,0:T(8,128)(2,1)S(1)}, bf16[34,104,128]{2,1,0:T(8,128)(2,1)S(1)}) custom-call(s32[5]{0:T(128)S(1)} %stack.23.where_ref.refs_0_, f32[2,52]{1,0:T(2,128)} %gate_scales.1, f32[2,52]{1,0:T(2,128)} %up_scales.1, ...), custom_call_target="tpu_custom_call" | custom-call | tf_op jit(solution)/shard_map/pallas_call | solution.py:170
  6.0 3.3 %collective-permute-start.1 = (bf16[34,104,128]{2,1,0:T(8,128)(2,1)S(1)}, bf16[34,104,128]{2,1,0:T(8,128)(2,1)S(1)}, u32[]{:S(2)}, u32[]{:S(2)}) collective-permute-start(bf16[34,104,128]{2,1,0:T(8,128)(2,1)S(1)} %get-tuple-element.47), channel_id=1, source_target_pairs={{0,1},{1,0},{2,3},{3,2},{4,5},{5,4},{6,7},{7,6},{8,9},{9,8},{10,11... | collective-permute-start | bytes 2715656 | tf_op jit(solution)/shard_map/ppermute | solution.py:556
  9.4 3.6 %shard_map.191 = (bf16[32,104,128]{2,1,0:T(8,128)(2,1)S(1)}, bf16[32,104,128]{2,1,0:T(8,128)(2,1)S(1)}) custom-call(s32[5]{0:T(128)S(1)} %stack.23.where_ref.refs_0_, f32[2,52]{1,0:T(2,128)} %bitcast.6, bf16[128,256]{1,0:T(8,128)(2,1)} %gradient_ref.1, bf16[6656,256]{1,0:T(8,128)(2,1)} %values_hbm.1, ...), custom_call_target="tpu_custom_call" | custom-call | tf_op jit(solution)/shard_map/pallas_call | solution.py:191
  14.7 2.2 %collective-permute-start.3 = (bf16[1856,128]{1,0:T(8,128)(2,1)S(1)}, bf16[1856,128]{1,0:T(8,128)(2,1)S(1)}, u32[]{:S(2)}, u32[]{:S(2)}) collective-permute-start(bf16[1856,128]{1,0:T(8,128)(2,1)S(1)} %get-tuple-element.50), channel_id=1, source_target_pairs={{0,32},{1,5},{2,34},{3,7},{4,36},{5,1},{6,38},{7,3},{8,40},{9,13},... | collective-permute-start | bytes 1425416 | tf_op jit(solution)/shard_map/ppermute | solution.py:568
  20.6 8.2 %collective-permute-done.2.refs_2_.refs_1_ = bf16[1856,128]{1,0:T(8,128)(2,1)S(1)} collective-permute-done((bf16[1856,128]{1,0:T(8,128)(2,1)S(1)}, bf16[1856,128]{1,0:T(8,128)(2,1)S(1)}, u32[]{:S(2)}, u32[]{:S(2)}) %collective-permute-start.2) | collective-permute-done | bytes 475168 | tf_op jit(solution)/shard_map/ppermute | solution.py:568
  29.6 2.8 %shard_map.194 = (bf16[256,6656]{1,0:T(8,128)(2,1)S(1)}, bf16[256,6656]{1,0:T(8,128)(2,1)S(1)}, bf16[3,64,104]{2,1,0:T(8,128)(2,1)S(1)}) custom-call(f32[2,52]{1,0:T(2,128)S(1)} %copy-done.9, f32[2,52]{1,0:T(2,128)S(1)} %copy-done.10, bf16[256,6656]{1,0:T(8,128)(2,1)S(1)} %copy-done, bf16[256,6656]{1,0:T(8,128)(2,1)S(1)} %copy-done.1, ...), custom_call_target="tpu_custom_call" | custom-call | flops 3407872 | bytes 13631488 | tf_op jit(solution)/shard_map/pallas_call | solution.py:225
  36.8 2.4 %collective-permute-start.11 = (bf16[816,128]{1,0:T(8,128)(2,1)S(1)}, bf16[816,128]{1,0:T(8,128)(2,1)S(1)}, u32[]{:S(2)}, u32[]{:S(2)}) collective-permute-start(bf16[816,128]{1,0:T(8,128)(2,1)S(1)} %get-tuple-element.62), channel_id=1, source_target_pairs={{0,6},{1,49},{2,0},{3,51},{4,2},{5,53},{6,4},{7,55},{8,14},{9,57},... | collective-permute-start | bytes 626696 | tf_op jit(solution)/shard_map/ppermute | solution.py:568
  39.2 2.7 %collective-permute-done.9.one_ref = bf16[816,128]{1,0:T(8,128)(2,1)S(1)} collective-permute-done((bf16[816,128]{1,0:T(8,128)(2,1)S(1)}, bf16[816,128]{1,0:T(8,128)(2,1)S(1)}, u32[]{:S(2)}, u32[]{:S(2)}) %collective-permute-start.9) | collective-permute-done | bytes 208928 | tf_op jit(solution)/shard_map/ppermute | solution.py:568
  41.8 2.4 %collective-permute-done.10.two_ref = bf16[816,128]{1,0:T(8,128)(2,1)S(1)} collective-permute-done((bf16[816,128]{1,0:T(8,128)(2,1)S(1)}, bf16[816,128]{1,0:T(8,128)(2,1)S(1)}, u32[]{:S(2)}, u32[]{:S(2)}) %collective-permute-start.10) | collective-permute-done | bytes 208928 | tf_op jit(solution)/shard_map/ppermute | solution.py:568
  45.1 5.1 %collective-permute-done.12.arrived_ref = bf16[1008,128]{1,0:T(8,128)(2,1)S(1)} collective-permute-done((bf16[1008,128]{1,0:T(8,128)(2,1)S(1)}, bf16[1008,128]{1,0:T(8,128)(2,1)S(1)}, u32[]{:S(2)}, u32[]{:S(2)}) %collective-permute-start.12) | collective-permute-done | bytes 258080 | tf_op jit(solution)/shard_map/ppermute | solution.py:559
  51.9 3.8 %collective-permute-start.13 = (bf16[304,128]{1,0:T(8,128)(2,1)S(1)}, bf16[304,128]{1,0:T(8,128)(2,1)S(1)}, u32[]{:S(2)}, u32[]{:S(2)}) collective-permute-start(bf16[304,128]{1,0:T(8,128)(2,1)S(1)} %get-tuple-element.67), channel_id=1, source_target_pairs={{0,1},{1,0},{2,3},{3,2},{4,5},{5,4},{6,7},{7,6},{8,9},{9,8},{10,11... | collective-permute-start | bytes 233480 | tf_op jit(solution)/shard_map/ppermute | solution.py:556
  59.5 3.5 %collective-permute-done.16.refs_2_ = bf16[512,128]{1,0:T(8,128)(2,1)S(1)} collective-permute-done((bf16[512,128]{1,0:T(8,128)(2,1)S(1)}, bf16[512,128]{1,0:T(8,128)(2,1)S(1)}, u32[]{:S(2)}, u32[]{:S(2)}) %collective-permute-start.16) | collective-permute-done | bytes 131104 | tf_op jit(solution)/shard_map/ppermute | solution.py:568
  64.9 2.3 %collective-permute-start.22 = (bf16[1760,128]{1,0:T(8,128)(2,1)S(1)}, bf16[1760,128]{1,0:T(8,128)(2,1)S(1)}, u32[]{:S(2)}, u32[]{:S(2)}) collective-permute-start(bf16[1760,128]{1,0:T(8,128)(2,1)S(1)} %shard_map.199.refs_1_), channel_id=1, source_target_pairs={{0,32},{1,5},{2,34},{3,7},{4,36},{5,1},{6,38},{7,3},{8,40},{9,13},... | collective-permute-start | bytes 1351688 | tf_op jit(solution)/shard_map/ppermute | solution.py:568
  68.9 2.6 %collective-permute-start.17 = (bf16[1760,128]{1,0:T(8,128)(2,1)S(1)}, bf16[1760,128]{1,0:T(8,128)(2,1)S(1)}, u32[]{:S(2)}, u32[]{:S(2)}) collective-permute-start(bf16[1760,128]{1,0:T(8,128)(2,1)S(1)} %shard_map.199.refs_1_), channel_id=1, source_target_pairs={{0,1},{1,0},{2,3},{3,2},{4,5},{5,4},{6,7},{7,6},{8,9},{9,8},{10,11... | collective-permute-start | bytes 1351688 | tf_op jit(solution)/shard_map/ppermute | solution.py:556
  71.5 2.5 %collective-permute-done.22.refs_4_ = bf16[1760,128]{1,0:T(8,128)(2,1)S(1)} collective-permute-done((bf16[1760,128]{1,0:T(8,128)(2,1)S(1)}, bf16[1760,128]{1,0:T(8,128)(2,1)S(1)}, u32[]{:S(2)}, u32[]{:S(2)}) %collective-permute-start.22) | collective-permute-done | bytes 450592 | tf_op jit(solution)/shard_map/ppermute | solution.py:568
  74.0 3.1 %collective-permute-start.23 = (bf16[1760,128]{1,0:T(8,128)(2,1)S(1)}, bf16[1760,128]{1,0:T(8,128)(2,1)S(1)}, u32[]{:S(2)}, u32[]{:S(2)}) collective-permute-start(bf16[1760,128]{1,0:T(8,128)(2,1)S(1)} %collective-permute-done.22.refs_4_), channel_id=1, source_target_pairs={{0,1},{1,0},{2,3},{3,2},{4,5},{5,4},{6,7},{7,6},{8,9},{9,8},{10,11... | collective-permute-start | bytes 1351688 | tf_op jit(solution)/shard_map/ppermute | solution.py:556
  77.2 2.3 %collective-permute-done.20.refs_3_ = bf16[1760,128]{1,0:T(8,128)(2,1)S(1)} collective-permute-done((bf16[1760,128]{1,0:T(8,128)(2,1)S(1)}, bf16[1760,128]{1,0:T(8,128)(2,1)S(1)}, u32[]{:S(2)}, u32[]{:S(2)}) %collective-permute-start.20) | collective-permute-done | bytes 450592 | tf_op jit(solution)/shard_map/ppermute | solution.py:568
  79.5 2.8 %collective-permute-start.21 = (bf16[1760,128]{1,0:T(8,128)(2,1)S(1)}, bf16[1760,128]{1,0:T(8,128)(2,1)S(1)}, u32[]{:S(2)}, u32[]{:S(2)}) collective-permute-start(bf16[1760,128]{1,0:T(8,128)(2,1)S(1)} %collective-permute-done.20.refs_3_), channel_id=1, source_target_pairs={{0,1},{1,0},{2,3},{3,2},{4,5},{5,4},{6,7},{7,6},{8,9},{9,8},{10,11... | collective-permute-start | bytes 1351688 | tf_op jit(solution)/shard_map/ppermute | solution.py:556
  82.2 2.0 %shard_map.200 = (f32[256,128]{1,0:T(8,128)S(1)}, f32[96,128]{1,0:T(8,128)S(1)}) custom-call(s32[5]{0:T(128)S(1)} %stack.23.where_ref.refs_0_, bf16[1760,128]{1,0:T(8,128)(2,1)S(1)} %shard_map.199.refs_1_, bf16[1760,128]{1,0:T(8,128)(2,1)S(1)} %collective-permute-done.18.refs_2_, bf16[1760,128]{1,0:T(8,128)(2,1)S(1)} %collective-permute-done.20.refs_3_, ...), custom_call_target="tpu_custom_call" | custom-call | tf_op jit(solution)/shard_map/pallas_call | solution.py:240
  84.3 1.9 %shard_map.201 = (bf16[256,128]{1,0:T(8,128)(2,1)S(1)}, bf16[256,128]{1,0:T(8,128)(2,1)S(1)}, bf16[256,128]{1,0:T(8,128)(2,1)S(1)}, bf16[256,128]{1,0:T(8,128)(2,1)S(1)}) custom-call(s32[5]{0:T(128)S(1)} %stack.23.where_ref.refs_0_, bf16[1760,128]{1,0:T(8,128)(2,1)S(1)} %collective-permute-done.17.refs_1_, ...), custom_call_target="tpu_custom_call" | custom-call | tf_op jit(solution)/shard_map/pallas_call | solution.py:240
  86.2 3.1 %collective-permute-start.24 = (bf16[256,128]{1,0:T(8,128)(2,1)S(1)}, bf16[256,128]{1,0:T(8,128)(2,1)S(1)}, u32[]{:S(2)}, u32[]{:S(2)}) collective-permute-start(bf16[256,128]{1,0:T(8,128)(2,1)S(1)} %get-tuple-element.71), channel_id=1, source_target_pairs={{0,64},{64,128},{128,192},{192,0},{1,65},{65,129},{129,193},{193,1... | collective-permute-start | bytes 196616 | tf_op jit(solution)/shard_map/ppermute | solution.py:602
  89.3 4.9 %collective-permute-start.25 = (bf16[256,128]{1,0:T(8,128)(2,1)S(1)}, bf16[256,128]{1,0:T(8,128)(2,1)S(1)}, u32[]{:S(2)}, u32[]{:S(2)}) collective-permute-start(bf16[256,128]{1,0:T(8,128)(2,1)S(1)} %get-tuple-element.72), channel_id=1, source_target_pairs={{0,128},{64,192},{128,0},{192,64},{1,129},{65,193},{129,1},{193,65... | collective-permute-start | bytes 196616 | tf_op jit(solution)/shard_map/ppermute | solution.py:602
  94.2 2.4 %collective-permute-start.26 = (bf16[256,128]{1,0:T(8,128)(2,1)S(1)}, bf16[256,128]{1,0:T(8,128)(2,1)S(1)}, u32[]{:S(2)}, u32[]{:S(2)}) collective-permute-start(bf16[256,128]{1,0:T(8,128)(2,1)S(1)} %get-tuple-element.73), channel_id=1, source_target_pairs={{0,192},{64,0},{128,64},{192,128},{1,193},{65,1},{129,65},{193,129... | collective-permute-start | bytes 196616 | tf_op jit(solution)/shard_map/ppermute | solution.py:602
  97.8 3.8 %collective-permute-done.26.three_ref = bf16[256,128]{1,0:T(8,128)(2,1)S(1)} collective-permute-done((bf16[256,128]{1,0:T(8,128)(2,1)S(1)}, bf16[256,128]{1,0:T(8,128)(2,1)S(1)}, u32[]{:S(2)}, u32[]{:S(2)}) %collective-permute-start.26) | collective-permute-done | bytes 65568 | tf_op jit(solution)/shard_map/ppermute | solution.py:602
  (67 shorter events, 23.3 us)
Async XLA Ops:
  6.0 7.5 %collective-permute-start.1 = (bf16[34,104,128]{2,1,0:T(8,128)(2,1)S(1)}, bf16[34,104,128]{2,1,0:T(8,128)(2,1)S(1)}, u32[]{:S(2)}, u32[]{:S(2)}) collective-permute-start(bf16[34,104,128]{2,1,0:T(8,128)(2,1)S(1)} %get-tuple-element.47), channel_id=1, source_target_pairs={{0,1},{1,0},{2,3},{3,2},{4,5},{5,4},{6,7},{7,6},{8,9},{9,8},{10,11... | collective-permute-start | bytes 2715656 | tf_op jit(solution)/shard_map/ppermute | solution.py:556
  13.0 4.9 %collective-permute-start.5 = (bf16[32,104,128]{2,1,0:T(8,128)(2,1)S(1)}, bf16[32,104,128]{2,1,0:T(8,128)(2,1)S(1)}, u32[]{:S(2)}, u32[]{:S(2)}) collective-permute-start(bf16[32,104,128]{2,1,0:T(8,128)(2,1)S(1)} %get-tuple-element.53), channel_id=1, source_target_pairs={{0,1},{1,0},{2,3},{3,2},{4,5},{5,4},{6,7},{7,6},{8,9},{9,8},{10,11... | collective-permute-start | bytes 2555912 | tf_op jit(solution)/shard_map/ppermute | solution.py:556
  14.6 14.2 %collective-permute-start.2 = (bf16[1856,128]{1,0:T(8,128)(2,1)S(1)}, bf16[1856,128]{1,0:T(8,128)(2,1)S(1)}, u32[]{:S(2)}, u32[]{:S(2)}) collective-permute-start(bf16[1856,128]{1,0:T(8,128)(2,1)S(1)} %get-tuple-element.49), channel_id=1, source_target_pairs={{0,16},{1,3},{2,18},{3,5},{4,20},{5,7},{6,22},{7,1},{8,24},{9,11},... | collective-permute-start | bytes 1425416 | tf_op jit(solution)/shard_map/ppermute | solution.py:568
  14.7 18.7 %collective-permute-start.3 = (bf16[1856,128]{1,0:T(8,128)(2,1)S(1)}, bf16[1856,128]{1,0:T(8,128)(2,1)S(1)}, u32[]{:S(2)}, u32[]{:S(2)}) collective-permute-start(bf16[1856,128]{1,0:T(8,128)(2,1)S(1)} %get-tuple-element.50), channel_id=1, source_target_pairs={{0,32},{1,5},{2,34},{3,7},{4,36},{5,1},{6,38},{7,3},{8,40},{9,13},... | collective-permute-start | bytes 1425416 | tf_op jit(solution)/shard_map/ppermute | solution.py:568
  16.9 16.5 %collective-permute-start.4 = (bf16[1856,128]{1,0:T(8,128)(2,1)S(1)}, bf16[1856,128]{1,0:T(8,128)(2,1)S(1)}, u32[]{:S(2)}, u32[]{:S(2)}) collective-permute-start(bf16[1856,128]{1,0:T(8,128)(2,1)S(1)} %get-tuple-element.51), channel_id=1, source_target_pairs={{0,48},{1,7},{2,50},{3,1},{4,52},{5,3},{6,54},{7,5},{8,56},{9,15},... | collective-permute-start | bytes 1425416 | tf_op jit(solution)/shard_map/ppermute | solution.py:568
  18.6 14.7 %collective-permute-start.6 = (bf16[832,128]{1,0:T(8,128)(2,1)S(1)}, bf16[832,128]{1,0:T(8,128)(2,1)S(1)}, u32[]{:S(2)}, u32[]{:S(2)}) collective-permute-start(bf16[832,128]{1,0:T(8,128)(2,1)S(1)} %get-tuple-element.55), channel_id=1, source_target_pairs={{0,16},{1,3},{2,18},{3,5},{4,20},{5,7},{6,22},{7,1},{8,24},{9,11},... | collective-permute-start | bytes 638984 | tf_op jit(solution)/shard_map/ppermute | solution.py:568
  19.1 14.2 %collective-permute-start.7 = (bf16[832,128]{1,0:T(8,128)(2,1)S(1)}, bf16[832,128]{1,0:T(8,128)(2,1)S(1)}, u32[]{:S(2)}, u32[]{:S(2)}) collective-permute-start(bf16[832,128]{1,0:T(8,128)(2,1)S(1)} %get-tuple-element.56), channel_id=1, source_target_pairs={{0,32},{1,5},{2,34},{3,7},{4,36},{5,1},{6,38},{7,3},{8,40},{9,13},... | collective-permute-start | bytes 638984 | tf_op jit(solution)/shard_map/ppermute | solution.py:568
  29.4 5.1 %collective-permute-start.8 = (bf16[832,128]{1,0:T(8,128)(2,1)S(1)}, bf16[832,128]{1,0:T(8,128)(2,1)S(1)}, u32[]{:S(2)}, u32[]{:S(2)}) collective-permute-start(bf16[832,128]{1,0:T(8,128)(2,1)S(1)} %shard_map.193), channel_id=1, source_target_pairs={{0,48},{1,7},{2,50},{3,1},{4,52},{5,3},{6,54},{7,5},{8,56},{9,15},... | collective-permute-start | bytes 638984 | tf_op jit(solution)/shard_map/ppermute | solution.py:568
  35.3 6.5 %collective-permute-start.9 = (bf16[816,128]{1,0:T(8,128)(2,1)S(1)}, bf16[816,128]{1,0:T(8,128)(2,1)S(1)}, u32[]{:S(2)}, u32[]{:S(2)}) collective-permute-start(bf16[816,128]{1,0:T(8,128)(2,1)S(1)} %get-tuple-element.60), channel_id=1, source_target_pairs={{0,4},{1,33},{2,6},{3,35},{4,0},{5,37},{6,2},{7,39},{8,12},{9,41},... | collective-permute-start | bytes 626696 | tf_op jit(solution)/shard_map/ppermute | solution.py:568
  36.5 7.8 %collective-permute-start.10 = (bf16[816,128]{1,0:T(8,128)(2,1)S(1)}, bf16[816,128]{1,0:T(8,128)(2,1)S(1)}, u32[]{:S(2)}, u32[]{:S(2)}) collective-permute-start(bf16[816,128]{1,0:T(8,128)(2,1)S(1)} %get-tuple-element.61), channel_id=1, source_target_pairs={{0,2},{1,17},{2,4},{3,19},{4,6},{5,21},{6,0},{7,23},{8,10},{9,25},... | collective-permute-start | bytes 626696 | tf_op jit(solution)/shard_map/ppermute | solution.py:568
  36.8 7.5 %collective-permute-start.11 = (bf16[816,128]{1,0:T(8,128)(2,1)S(1)}, bf16[816,128]{1,0:T(8,128)(2,1)S(1)}, u32[]{:S(2)}, u32[]{:S(2)}) collective-permute-start(bf16[816,128]{1,0:T(8,128)(2,1)S(1)} %get-tuple-element.62), channel_id=1, source_target_pairs={{0,6},{1,49},{2,0},{3,51},{4,2},{5,53},{6,4},{7,55},{8,14},{9,57},... | collective-permute-start | bytes 626696 | tf_op jit(solution)/shard_map/ppermute | solution.py:568
  45.0 5.3 %collective-permute-start.12 = (bf16[1008,128]{1,0:T(8,128)(2,1)S(1)}, bf16[1008,128]{1,0:T(8,128)(2,1)S(1)}, u32[]{:S(2)}, u32[]{:S(2)}) collective-permute-start(bf16[1008,128]{1,0:T(8,128)(2,1)S(1)} %get-tuple-element.65), channel_id=1, source_target_pairs={{0,8},{1,9},{2,10},{3,11},{4,12},{5,13},{6,14},{7,15},{8,0},{9,1},... | collective-permute-start | bytes 774152 | tf_op jit(solution)/shard_map/ppermute | solution.py:559
  57.2 5.7 %collective-permute-start.16 = (bf16[512,128]{1,0:T(8,128)(2,1)S(1)}, bf16[512,128]{1,0:T(8,128)(2,1)S(1)}, u32[]{:S(2)}, u32[]{:S(2)}) collective-permute-start(bf16[512,128]{1,0:T(8,128)(2,1)S(1)} %shard_map.198.own_ref), channel_id=1, source_target_pairs={{0,4},{1,33},{2,6},{3,35},{4,0},{5,37},{6,2},{7,39},{8,12},{9,41},... | collective-permute-start | bytes 393224 | tf_op jit(solution)/shard_map/ppermute | solution.py:568
  58.0 5.3 %collective-permute-start.15 = (bf16[512,128]{1,0:T(8,128)(2,1)S(1)}, bf16[512,128]{1,0:T(8,128)(2,1)S(1)}, u32[]{:S(2)}, u32[]{:S(2)}) collective-permute-start(bf16[512,128]{1,0:T(8,128)(2,1)S(1)} %shard_map.198.own_ref), channel_id=1, source_target_pairs={{0,6},{1,49},{2,0},{3,51},{4,2},{5,53},{6,4},{7,55},{8,14},{9,57},... | collective-permute-start | bytes 393224 | tf_op jit(solution)/shard_map/ppermute | solution.py:568
  59.3 5.0 %collective-permute-start.14 = (bf16[512,128]{1,0:T(8,128)(2,1)S(1)}, bf16[512,128]{1,0:T(8,128)(2,1)S(1)}, u32[]{:S(2)}, u32[]{:S(2)}) collective-permute-start(bf16[512,128]{1,0:T(8,128)(2,1)S(1)} %shard_map.198.own_ref), channel_id=1, source_target_pairs={{0,2},{1,17},{2,4},{3,19},{4,6},{5,21},{6,0},{7,23},{8,10},{9,25},... | collective-permute-start | bytes 393224 | tf_op jit(solution)/shard_map/ppermute | solution.py:568
  64.9 9.1 %collective-permute-start.22 = (bf16[1760,128]{1,0:T(8,128)(2,1)S(1)}, bf16[1760,128]{1,0:T(8,128)(2,1)S(1)}, u32[]{:S(2)}, u32[]{:S(2)}) collective-permute-start(bf16[1760,128]{1,0:T(8,128)(2,1)S(1)} %shard_map.199.refs_1_), channel_id=1, source_target_pairs={{0,32},{1,5},{2,34},{3,7},{4,36},{5,1},{6,38},{7,3},{8,40},{9,13},... | collective-permute-start | bytes 1351688 | tf_op jit(solution)/shard_map/ppermute | solution.py:568
  67.2 12.2 %collective-permute-start.20 = (bf16[1760,128]{1,0:T(8,128)(2,1)S(1)}, bf16[1760,128]{1,0:T(8,128)(2,1)S(1)}, u32[]{:S(2)}, u32[]{:S(2)}) collective-permute-start(bf16[1760,128]{1,0:T(8,128)(2,1)S(1)} %shard_map.199.refs_1_), channel_id=1, source_target_pairs={{0,48},{1,7},{2,50},{3,1},{4,52},{5,3},{6,54},{7,5},{8,56},{9,15},... | collective-permute-start | bytes 1351688 | tf_op jit(solution)/shard_map/ppermute | solution.py:568
  68.9 13.3 %collective-permute-start.18 = (bf16[1760,128]{1,0:T(8,128)(2,1)S(1)}, bf16[1760,128]{1,0:T(8,128)(2,1)S(1)}, u32[]{:S(2)}, u32[]{:S(2)}) collective-permute-start(bf16[1760,128]{1,0:T(8,128)(2,1)S(1)} %shard_map.199.refs_1_), channel_id=1, source_target_pairs={{0,16},{1,3},{2,18},{3,5},{4,20},{5,7},{6,22},{7,1},{8,24},{9,11},... | collective-permute-start | bytes 1351688 | tf_op jit(solution)/shard_map/ppermute | solution.py:568
  68.9 15.3 %collective-permute-start.17 = (bf16[1760,128]{1,0:T(8,128)(2,1)S(1)}, bf16[1760,128]{1,0:T(8,128)(2,1)S(1)}, u32[]{:S(2)}, u32[]{:S(2)}) collective-permute-start(bf16[1760,128]{1,0:T(8,128)(2,1)S(1)} %shard_map.199.refs_1_), channel_id=1, source_target_pairs={{0,1},{1,0},{2,3},{3,2},{4,5},{5,4},{6,7},{7,6},{8,9},{9,8},{10,11... | collective-permute-start | bytes 1351688 | tf_op jit(solution)/shard_map/ppermute | solution.py:556
  74.0 10.2 %collective-permute-start.23 = (bf16[1760,128]{1,0:T(8,128)(2,1)S(1)}, bf16[1760,128]{1,0:T(8,128)(2,1)S(1)}, u32[]{:S(2)}, u32[]{:S(2)}) collective-permute-start(bf16[1760,128]{1,0:T(8,128)(2,1)S(1)} %collective-permute-done.22.refs_4_), channel_id=1, source_target_pairs={{0,1},{1,0},{2,3},{3,2},{4,5},{5,4},{6,7},{7,6},{8,9},{9,8},{10,11... | collective-permute-start | bytes 1351688 | tf_op jit(solution)/shard_map/ppermute | solution.py:556
  79.5 4.8 %collective-permute-start.21 = (bf16[1760,128]{1,0:T(8,128)(2,1)S(1)}, bf16[1760,128]{1,0:T(8,128)(2,1)S(1)}, u32[]{:S(2)}, u32[]{:S(2)}) collective-permute-start(bf16[1760,128]{1,0:T(8,128)(2,1)S(1)} %collective-permute-done.20.refs_3_), channel_id=1, source_target_pairs={{0,1},{1,0},{2,3},{3,2},{4,5},{5,4},{6,7},{7,6},{8,9},{9,8},{10,11... | collective-permute-start | bytes 1351688 | tf_op jit(solution)/shard_map/ppermute | solution.py:556
  86.2 10.4 %collective-permute-start.24 = (bf16[256,128]{1,0:T(8,128)(2,1)S(1)}, bf16[256,128]{1,0:T(8,128)(2,1)S(1)}, u32[]{:S(2)}, u32[]{:S(2)}) collective-permute-start(bf16[256,128]{1,0:T(8,128)(2,1)S(1)} %get-tuple-element.71), channel_id=1, source_target_pairs={{0,64},{64,128},{128,192},{192,0},{1,65},{65,129},{129,193},{193,1... | collective-permute-start | bytes 196616 | tf_op jit(solution)/shard_map/ppermute | solution.py:602
  89.3 8.6 %collective-permute-start.25 = (bf16[256,128]{1,0:T(8,128)(2,1)S(1)}, bf16[256,128]{1,0:T(8,128)(2,1)S(1)}, u32[]{:S(2)}, u32[]{:S(2)}) collective-permute-start(bf16[256,128]{1,0:T(8,128)(2,1)S(1)} %get-tuple-element.72), channel_id=1, source_target_pairs={{0,128},{64,192},{128,0},{192,64},{1,129},{65,193},{129,1},{193,65... | collective-permute-start | bytes 196616 | tf_op jit(solution)/shard_map/ppermute | solution.py:602
  94.2 7.4 %collective-permute-start.26 = (bf16[256,128]{1,0:T(8,128)(2,1)S(1)}, bf16[256,128]{1,0:T(8,128)(2,1)S(1)}, u32[]{:S(2)}, u32[]{:S(2)}) collective-permute-start(bf16[256,128]{1,0:T(8,128)(2,1)S(1)} %get-tuple-element.73), channel_id=1, source_target_pairs={{0,192},{64,0},{128,64},{192,128},{1,193},{65,1},{129,65},{193,129... | collective-permute-start | bytes 196616 | tf_op jit(solution)/shard_map/ppermute | solution.py:602
  (14 other events, 186.0 us)

commit v4 on v3

--- a/solution.py
+++ b/solution.py
@@ -289,7 +289,8 @@
 
 
 def second_kernel(where_ref, *refs):
-    wide, tall, outs = refs[:4], refs[4:8], refs[-4:]
+    wide, tall, expand_ref, outs, expand_out = refs[:4], refs[4:8], refs[8], refs[-5:-1], refs[-1]
+    expand_out[...] = expand_ref[...]
     down = tall[0].shape[0] // 4
     pair = 2 * down
 
@@ -307,45 +308,36 @@
         out_ref[pair + down :] = low.astype(out_ref.dtype)
 
 
-def second(where, wide, tall, piece, ready):
+def second(where, wide, tall, expand, piece, ready):
     rows, tokens = wide[0].shape
     rows -= 10 * piece
     out_shape = [jax.ShapeDtypeStruct((rows, tokens), F32 if i == 0 else BF16) for i in range(4)]
-    return vmem_call(second_kernel, out_shape, where, *wide, *tall, *ready, unread=len(ready))
-
-
-def third_kernel(where_ref, own_ref, one_ref, two_ref, three_ref, expand_ref, keep_ref, send_ref):
-    rows, count = keep_ref.shape
+    out_shape.append(jax.ShapeDtypeStruct(expand.shape, BF16))
+    return vmem_call(second_kernel, out_shape, where, *wide, *tall, expand, *ready, unread=len(ready))
+
+
+def third_kernel(where_ref, own_ref, one_ref, two_ref, three_ref, after_ref, keep_ref, send_ref):
     arrived = one_ref[...].astype(F32) + two_ref[...].astype(F32) + three_ref[...].astype(F32)
     everything = own_ref[...] + arrived
     keep_ref[...] = everything
-    send_ref[:rows] = everything.astype(BF16)
-    _, rank, piece = expand_ref.shape
-    for kind in range(3):
-        place = slice(rows + kind * rank, rows + (kind + 1) * rank)
-        send_ref[place, :piece] = expand_ref[kind]
-        send_ref[place, piece:] = jnp.zeros((rank, count - piece), BF16)
-
-
-def third(where, own, arrived, expand):
-    rows, count = own.shape
-    far_rows = rows + 3 * expand.shape[1]
-    out_shape = [jax.ShapeDtypeStruct(own.shape, F32), jax.ShapeDtypeStruct((far_rows, count), BF16)]
-    return vmem_call(third_kernel, out_shape, where, own, *arrived, expand)
+    send_ref[...] = everything.astype(BF16)
+
+
+def third(where, own, arrived, after):
+    out_shape = [jax.ShapeDtypeStruct(own.shape, F32), jax.ShapeDtypeStruct(own.shape, BF16)]
+    return vmem_call(third_kernel, out_shape, where, own, *arrived, after, unread=1)
 
 
 def middle_kernel(
-    where_ref, own_ref, arrived_ref, expand_ref,
+    where_ref, own_ref, arrived_ref, expand_ref, far_expand_ref,
     send_ref, keep_ref, gate_out, up_out, down_out, expands_ref, grads_ref, ranks_ref,
 ):
     core, z = where_ref[0], where_ref[2]
     _, rank, piece = expand_ref.shape
     half = rank // 2
-    rows = own_ref.shape[0]
-    sums = own_ref[...] + arrived_ref[:rows].astype(F32)
+    sums = own_ref[...] + arrived_ref[...].astype(F32)
     expands_ref[z] = expand_ref[...]
-    for kind in range(3):
-        expands_ref[1 - z, kind] = arrived_ref[rows + kind * rank : rows + (kind + 1) * rank, :piece]
+    expands_ref[1 - z] = far_expand_ref[...]
     lows = [sums[6 * piece + k * rank : 6 * piece + (k + 1) * rank].astype(BF16) for k in range(3)]
     keeps, sends, ranks = [], [], [0.0] * 3
     for chip in range(2):
@@ -376,7 +368,7 @@
         out_ref[...] = SCALE * dot(lows[kind], grads_ref[z, kind], 1, 1)
 
 
-def middle(where, own, arrived, expand):
+def middle(where, own, arrived, expand, far_expand):
     _, rank, piece = expand.shape
     tokens = own.shape[1]
     rows = 2 * piece + 3 * rank // 2
@@ -389,7 +381,7 @@
         pltpu.VMEM((2, 3, piece, tokens), BF16),
         pltpu.VMEM((3, rank, tokens), F32),
     ]
-    return vmem_call(middle_kernel, out_shape, where, own, arrived, expand, scratch=scratch)
+    return vmem_call(middle_kernel, out_shape, where, own, arrived, expand, far_expand, scratch=scratch)
 
 
 def pair_kernel(piece, where_ref, keep_ref, arrived_ref, out_ref):
@@ -433,7 +425,7 @@
 def back_kernel(last, *refs):
     if last:
         (where_ref, *pieces, gate_ref, up_ref, before_ref, rank_ref,
-         own_ref, to_one, to_two, to_three, grads_ref, total_ref, turned_ref) = refs
+         keep_ref, send_ref, grads_ref, total_ref, turned_ref) = refs
     else:
         where_ref, *pieces, gate_ref, up_ref, total_ref, rank_ref, grads_ref = refs
     core = 1 - where_ref[0] if last else where_ref[0]
@@ -467,11 +459,13 @@
             ranks.append(jnp.where(core == 0, rank_ref[rows], rank[rows]))
         turned_ref[...] = total_ref[...].T
         share = turned_ref.shape[0] // 4
-        for offset, out_ref in enumerate([own_ref, to_one, to_two, to_three]):
-            start = pl.multiple_of(lax.rem(where_ref[1] + offset, 4) * share, share)
-            piece = turned_ref[pl.ds(start, share), :]
-            block = jnp.concatenate([piece[:, :BLOCK], piece[:, BLOCK:], *ranks], axis=0)
-            out_ref[...] = block.astype(BF16)
+        column = where_ref[1]
+        for base, out_ref in ((column, keep_ref), (column ^ 1, send_ref)):
+            rows = []
+            for place in (base, 3 - base):
+                piece = turned_ref[pl.ds(pl.multiple_of(place * share, share), share), :]
+                rows += [piece[:, :BLOCK], piece[:, BLOCK:]]
+            out_ref[...] = jnp.concatenate([*rows, *ranks], axis=0).astype(BF16)
     else:
         rank_ref[...] = rank
 
@@ -482,7 +476,7 @@
     rank_rows = rows - hidden // 4
     scratch = [pltpu.VMEM((hidden, tokens), BF16)]
     if last:
-        out_shape = [jax.ShapeDtypeStruct((tokens // 4 * width // BLOCK + 2 * rank_rows, tokens), BF16)] * 4
+        out_shape = [jax.ShapeDtypeStruct((tokens // 2 * width // BLOCK + 2 * rank_rows, tokens), BF16)] * 2
         scratch += [pltpu.VMEM((width, tokens), F32), pltpu.VMEM((tokens, width), F32)]
     else:
         out_shape = [
@@ -495,39 +489,48 @@
     )
 
 
+def halfway_kernel(where_ref, own_ref, arrived_ref, main_ref, send_ref):
+    rows = main_ref.shape[0]
+    summed = own_ref[...].astype(F32) + arrived_ref[...].astype(F32)
+    main_ref[...] = summed[:rows]
+    send_ref[...] = summed[rows:].astype(BF16)
+
+
+def halfway(where, own, arrived, main_rows):
+    rows, tokens = own.shape
+    out_shape = [
+        jax.ShapeDtypeStruct((main_rows, tokens), F32),
+        jax.ShapeDtypeStruct((rows - main_rows, tokens), BF16),
+    ]
+    return vmem_call(halfway_kernel, out_shape, where, own, arrived)
+
+
 def last_kernel(
-    where_ref, own_ref, one_ref, two_ref, three_ref, tokens_ref, gradient_ref, gate_reduce_ref, up_reduce_ref,
-    input_out, gate_out, up_out, down_out, parts_ref, wide_ref,
+    where_ref, main_ref, own_ref, arrived_ref, tokens_ref, gradient_ref, gate_reduce_ref, up_reduce_ref,
+    input_out, gate_out, up_out, down_out, wide_ref,
 ):
-    column = where_ref[1]
-    for offset, ref in enumerate([own_ref, one_ref, two_ref, three_ref]):
-        parts_ref[lax.rem(column + 4 - offset, 4)] = ref[...].astype(F32)
-    summed = parts_ref[0] + parts_ref[1] + parts_ref[2] + parts_ref[3]
     share = input_out.shape[0]
     rank = gate_out.shape[0]
-    sums = [summed[2 * share + k * rank : 2 * share + (k + 1) * rank].astype(BF16) for k in range(3)]
+    main = main_ref[...] + arrived_ref[: 2 * share].astype(F32)
+    summed = own_ref[2 * share :].astype(F32) + arrived_ref[2 * share :].astype(F32)
+    sums = [summed[k * rank : (k + 1) * rank].astype(BF16) for k in range(3)]
     wide_ref[...] = dot(sums[0], gate_reduce_ref[...], 0, 0) + dot(sums[1], up_reduce_ref[...], 0, 0)
-    start = pl.multiple_of(column * share, share)
-    main = jnp.concatenate([summed[:share], summed[share : 2 * share]], axis=1)
+    start = pl.multiple_of(where_ref[1] * share, share)
+    main = jnp.concatenate([main[:share], main[share:]], axis=1)
     input_out[...] = (main + SCALE * wide_ref[pl.ds(start, share), :]).astype(BF16)
     gate_out[...] = SCALE * dot(sums[0], tokens_ref[...], 1, 0)
     up_out[...] = SCALE * dot(sums[1], tokens_ref[...], 1, 0)
     down_out[...] = SCALE * dot(sums[2], gradient_ref[...], 1, 0)
 
 
-def finish(where, own, others, tokens, gradient, gate_reduce, up_reduce):
+def finish(where, main, own, arrived, tokens, gradient, gate_reduce, up_reduce):
     rank, width = gate_reduce.shape
     count = tokens.shape[0]
-    vmem = pl.BlockSpec(memory_space=pltpu.VMEM)
-    return pl.pallas_call(
-        last_kernel,
-        in_specs=[smem()] + [vmem] * 8,
-        out_specs=[vmem] * 4,
-        out_shape=[jax.ShapeDtypeStruct((count // 4, width), BF16)]
-        + [jax.ShapeDtypeStruct((rank, width), F32)] * 3,
-        scratch_shapes=[pltpu.VMEM((4,) + own.shape, F32), pltpu.VMEM((count, width), F32)],
-        compiler_params=params(),
-    )(where, own, *others, tokens, gradient, gate_reduce, up_reduce)
+    out_shape = [jax.ShapeDtypeStruct((count // 4, width), BF16)] + [jax.ShapeDtypeStruct((rank, width), F32)] * 3
+    return vmem_call(
+        last_kernel, out_shape, where, main, own, arrived, tokens, gradient, gate_reduce, up_reduce,
+        scratch=[pltpu.VMEM((count, width), F32)],
+    )
 
 
 def per_device(
@@ -586,10 +589,11 @@
     gate_weight, up_weight, expand = weights(
         gate_scales, up_scales, gate_values, up_values, (gate_expand, up_expand, down_reduce), own
     )
-    own, *out = second(where, wide, tall, piece, (gate_weight, up_weight))
-    own, out = third(where, own, along_all(True, out), expand)
+    own, *out, leaving = second(where, wide, tall, expand, piece, (gate_weight, up_weight))
+    far_expand = along_z(leaving)
+    own, out = third(where, own, along_all(True, out), far_expand)
     send, keep, gate_expand_gradient, up_expand_gradient, down_reduce_gradient = middle(
-        where, own, along_z(out), expand
+        where, own, along_z(out), expand, far_expand
     )
     rank_rows = low_rows // 2
     block = pair_block(where, keep, exchange(send), piece)
@@ -597,13 +601,13 @@
     mine = [block, *along_all(False, [block] * 3, PIECES[1:])]
     theirs = [exchange(value) for value in mine]
     begun = back(False, where, mine, gate_weight, up_weight)
-    own, *out = back(True, where, theirs, gate_weight, up_weight, begun)
-    others = [
-        lax.ppermute(value, "col", [(i, (i + offset) % 4) for i in range(4)])
-        for offset, value in zip((1, 2, 3), out)
-    ]
+    own, out = back(True, where, theirs, gate_weight, up_weight, begun)
+    main, out = halfway(
+        where, own, lax.ppermute(out, "col", [(i, i ^ 1) for i in range(4)]), tokens.size // 4 // BLOCK
+    )
+    arrived = lax.ppermute(out, "col", [(i, 3 - i) for i in range(4)])
     input_gradient, gate_reduce_gradient, up_reduce_gradient, down_expand_gradient = finish(
-        where, own, others, tokens, output_gradient, gate_reduce_factor, up_reduce_factor
+        where, main, out, arrived, tokens, output_gradient, gate_reduce_factor, up_reduce_factor
     )
     return (
         input_gradient,

time: 103 us -> 101 us (0.981); the launches traced: 103 us -> 99.3 us
  starting transfers between devices: 42.2 us -> 39.4 us
  waiting for transfers between devices: 36.2 us -> 34.6 us
    ppermute x3 -> x2, starting transfers between devices: 10.4 us -> 8.02 us  [the longest x1 4.98 us: per_device(): arrived = lax.ppermute(out, 'col', [(i, 3 - i) for i in range(4)])]
    pallas_call x10 -> x12, Pallas kernels: 10.5 us -> 12.5 us  [vmem_call(): pl.pallas_call(kernel, in_specs=[smem()] + [vmem] * (len(args) - 1 - unre...]
    ppermute x15, waiting for transfers between devices: 25.1 us -> 23.1 us  [along(): return lax.ppermute(value, 'row', pairs)]
    ppermute x1 -> x2, starting transfers between devices: 0.18 us -> 1.73 us  [along_z(): return lax.ppermute(value, 'row', [(i, i ^ 8) for i in range(64)])]
    pallas_call x1 -> x0, Pallas kernels: 1.43 us -> none  [finish(): pl.pallas_call(last_kernel, in_specs=[smem()] + [vmem] * 8, out_specs=[vm...]
    ppermute x1 -> x2, waiting for transfers between devices: 5.09 us -> 6.41 us  [along_z(): return lax.ppermute(value, 'row', [(i, i ^ 8) for i in range(64)])]
    ppermute x15, starting transfers between devices: 15.4 us -> 14.4 us  [along(): return lax.ppermute(value, 'row', pairs)]
    ppermute x3 -> x2, waiting for transfers between devices: 5.05 us -> 4.15 us  [the longest x1 2.5 us: per_device(): lax.ppermute(out, 'col', [(i, i ^ 1) for i in range(4)])]
  transfers between devices with their start and end apart: 27 -> 27, of which waited for: 15 -> 14; matrix products, arithmetic and copies ran while one was open for 0% -> 0% of each run, Pallas kernels for 10% -> 11%
where the time goes in v4:
time: 101 us; the launch traced here: 99.3 us
  starting transfers between devices  39.4 us (39%)
  waiting for transfers between devices  34.6 us (34%)
  Pallas kernels  24.1 us (24%)
    ppermute x15, waiting for transfers between devices, along(): return lax.ppermute(value, 'row', pairs)  23.1 us
    ppermute x8, starting transfers between devices, exchange(): return lax.ppermute(value, 'row', [(i, i ^ 1) for i in range(64)])  15.3 us
    ppermute x15, starting transfers between devices, along(): return lax.ppermute(value, 'row', pairs)  14.4 us
    pallas_call x12, Pallas kernels, vmem_call(): pl.pallas_call(kernel, in_specs=[smem()] + [vmem] * (len(args) - 1 - unre...  12.5 us
    ppermute x2, waiting for transfers between devices, along_z(): return lax.ppermute(value, 'row', [(i, i ^ 8) for i in range(64)])  6.41 us
    pallas_call x1, Pallas kernels, wide_sums(): pl.pallas_call(wide_kernel, in_specs=[smem()] + [hbm] * 9, out_specs=[vme...  5.29 us
    ppermute x1, starting transfers between devices, per_device(): arrived = lax.ppermute(out, 'col', [(i, 3 - i) for i in range(4)])  4.98 us
    pallas_call x1, Pallas kernels, tall_sums(): pl.pallas_call(tall_kernel, in_specs=[smem(), hbm, hbm, hbm, pl.BlockSpec...  3.58 us
  transfers between devices with their start and end apart: 27, of which 14 were waited for; matrix products, arithmetic and copies ran while one was open for 0% of the time, Pallas kernels for 11%

profile of v4, /device:TPU:1, one launch (start us, length us, event | category | flops | bytes accessed | tf_op | source)
XLA Modules:
  0.0 99.3 jit_solution(12721512604831330821)
XLA Ops:
  0.7 5.3 %shard_map.189 = (bf16[32,104,128]{2,1,0:T(8,128)(2,1)S(1)}, bf16[32,104,128]{2,1,0:T(8,128)(2,1)S(1)}, bf16[34,104,128]{2,1,0:T(8,128)(2,1)S(1)}, bf16[34,104,128]{2,1,0:T(8,128)(2,1)S(1)}) custom-call(s32[5]{0:T(128)S(1)} %stack.23.where_ref.refs_0_, f32[2,52]{1,0:T(2,128)} %gate_scales.1, f32[2,52]{1,0:T(2,128)} %up_scales.1, ...), custom_call_target="tpu_custom_call" | custom-call | tf_op jit(solution)/shard_map/pallas_call | solution.py:170
  6.0 3.3 %collective-permute-start.1 = (bf16[34,104,128]{2,1,0:T(8,128)(2,1)S(1)}, bf16[34,104,128]{2,1,0:T(8,128)(2,1)S(1)}, u32[]{:S(2)}, u32[]{:S(2)}) collective-permute-start(bf16[34,104,128]{2,1,0:T(8,128)(2,1)S(1)} %get-tuple-element.48), channel_id=1, source_target_pairs={{0,1},{1,0},{2,3},{3,2},{4,5},{5,4},{6,7},{7,6},{8,9},{9,8},{10,11... | collective-permute-start | bytes 2715656 | tf_op jit(solution)/shard_map/ppermute | solution.py:559
  9.4 3.6 %shard_map.191 = (bf16[32,104,128]{2,1,0:T(8,128)(2,1)S(1)}, bf16[32,104,128]{2,1,0:T(8,128)(2,1)S(1)}) custom-call(s32[5]{0:T(128)S(1)} %stack.23.where_ref.refs_0_, f32[2,52]{1,0:T(2,128)} %bitcast.6, bf16[128,256]{1,0:T(8,128)(2,1)} %gradient_ref.1, bf16[6656,256]{1,0:T(8,128)(2,1)} %values_hbm.1, ...), custom_call_target="tpu_custom_call" | custom-call | tf_op jit(solution)/shard_map/pallas_call | solution.py:191
  14.7 2.2 %collective-permute-start.3 = (bf16[1856,128]{1,0:T(8,128)(2,1)S(1)}, bf16[1856,128]{1,0:T(8,128)(2,1)S(1)}, u32[]{:S(2)}, u32[]{:S(2)}) collective-permute-start(bf16[1856,128]{1,0:T(8,128)(2,1)S(1)} %get-tuple-element.51), channel_id=1, source_target_pairs={{0,32},{1,5},{2,34},{3,7},{4,36},{5,1},{6,38},{7,3},{8,40},{9,13},... | collective-permute-start | bytes 1425416 | tf_op jit(solution)/shard_map/ppermute | solution.py:571
  20.6 8.2 %collective-permute-done.2.refs_2_.refs_1_ = bf16[1856,128]{1,0:T(8,128)(2,1)S(1)} collective-permute-done((bf16[1856,128]{1,0:T(8,128)(2,1)S(1)}, bf16[1856,128]{1,0:T(8,128)(2,1)S(1)}, u32[]{:S(2)}, u32[]{:S(2)}) %collective-permute-start.2) | collective-permute-done | bytes 475168 | tf_op jit(solution)/shard_map/ppermute | solution.py:571
  29.7 2.8 %shard_map.194 = (bf16[256,6656]{1,0:T(8,128)(2,1)S(1)}, bf16[256,6656]{1,0:T(8,128)(2,1)S(1)}, bf16[3,64,104]{2,1,0:T(8,128)(2,1)S(1)}) custom-call(f32[2,52]{1,0:T(2,128)S(1)} %copy-done.9, f32[2,52]{1,0:T(2,128)S(1)} %copy-done.10, bf16[256,6656]{1,0:T(8,128)(2,1)S(1)} %copy-done, bf16[256,6656]{1,0:T(8,128)(2,1)S(1)} %copy-done.1, ...), custom_call_target="tpu_custom_call" | custom-call | flops 3407872 | bytes 13631488 | tf_op jit(solution)/shard_map/pallas_call | solution.py:225
  36.6 2.4 %collective-permute-start.11 = (bf16[816,128]{1,0:T(8,128)(2,1)S(1)}, bf16[816,128]{1,0:T(8,128)(2,1)S(1)}, u32[]{:S(2)}, u32[]{:S(2)}) collective-permute-start(bf16[816,128]{1,0:T(8,128)(2,1)S(1)} %get-tuple-element.64), channel_id=1, source_target_pairs={{0,6},{1,49},{2,0},{3,51},{4,2},{5,53},{6,4},{7,55},{8,14},{9,57},... | collective-permute-start | bytes 626696 | tf_op jit(solution)/shard_map/ppermute | solution.py:571
  40.6 1.8 %collective-permute-done.12.after_ref.far_expand_ref = bf16[3,64,104]{2,1,0:T(8,128)(2,1)S(1)} collective-permute-done((bf16[3,64,104]{2,1,0:T(8,128)(2,1)S(1)}, bf16[3,64,104]{2,1,0:T(8,128)(2,1)S(1)}, u32[]{:S(2)}, u32[]{:S(2)}) %collective-permute-start.12) | collective-permute-done | bytes 39968 | tf_op jit(solution)/shard_map/ppermute | solution.py:562
  42.4 1.9 %collective-permute-done.10.two_ref = bf16[816,128]{1,0:T(8,128)(2,1)S(1)} collective-permute-done((bf16[816,128]{1,0:T(8,128)(2,1)S(1)}, bf16[816,128]{1,0:T(8,128)(2,1)S(1)}, u32[]{:S(2)}, u32[]{:S(2)}) %collective-permute-start.10) | collective-permute-done | bytes 208928 | tf_op jit(solution)/shard_map/ppermute | solution.py:571
  45.1 4.6 %collective-permute-done.13.arrived_ref = bf16[816,128]{1,0:T(8,128)(2,1)S(1)} collective-permute-done((bf16[816,128]{1,0:T(8,128)(2,1)S(1)}, bf16[816,128]{1,0:T(8,128)(2,1)S(1)}, u32[]{:S(2)}, u32[]{:S(2)}) %collective-permute-start.13) | collective-permute-done | bytes 208928 | tf_op jit(solution)/shard_map/ppermute | solution.py:562
  49.7 1.7 %shard_map.197 = (bf16[304,128]{1,0:T(8,128)(2,1)S(1)}, f32[304,128]{1,0:T(8,128)S(1)}, f32[64,104]{1,0:T(8,128)}, f32[64,104]{1,0:T(8,128)}, f32[64,104]{1,0:T(8,128)}) custom-call(s32[5]{0:T(128)S(1)} %stack.23.where_ref.refs_0_, f32[816,128]{1,0:T(8,128)S(1)} %get-tuple-element.66.own_ref, bf16[816,128]{1,0:T(8,128)(2,1)S(1)} %collective-permute-done.13.arrived_ref, ...), custom_call_target="tpu_custom_call" | custom-call | tf_op jit(solution)/shard_map/pallas_call | solution.py:240
  51.4 3.8 %collective-permute-start.14 = (bf16[304,128]{1,0:T(8,128)(2,1)S(1)}, bf16[304,128]{1,0:T(8,128)(2,1)S(1)}, u32[]{:S(2)}, u32[]{:S(2)}) collective-permute-start(bf16[304,128]{1,0:T(8,128)(2,1)S(1)} %get-tuple-element.69), channel_id=1, source_target_pairs={{0,1},{1,0},{2,3},{3,2},{4,5},{5,4},{6,7},{7,6},{8,9},{9,8},{10,11... | collective-permute-start | bytes 233480 | tf_op jit(solution)/shard_map/ppermute | solution.py:559
  59.1 3.4 %collective-permute-done.17.refs_2_ = bf16[512,128]{1,0:T(8,128)(2,1)S(1)} collective-permute-done((bf16[512,128]{1,0:T(8,128)(2,1)S(1)}, bf16[512,128]{1,0:T(8,128)(2,1)S(1)}, u32[]{:S(2)}, u32[]{:S(2)}) %collective-permute-start.17) | collective-permute-done | bytes 131104 | tf_op jit(solution)/shard_map/ppermute | solution.py:571
  66.0 1.7 %collective-permute-start.21 = (bf16[1760,128]{1,0:T(8,128)(2,1)S(1)}, bf16[1760,128]{1,0:T(8,128)(2,1)S(1)}, u32[]{:S(2)}, u32[]{:S(2)}) collective-permute-start(bf16[1760,128]{1,0:T(8,128)(2,1)S(1)} %shard_map.199.refs_1_), channel_id=1, source_target_pairs={{0,48},{1,7},{2,50},{3,1},{4,52},{5,3},{6,54},{7,5},{8,56},{9,15},... | collective-permute-start | bytes 1351688 | tf_op jit(solution)/shard_map/ppermute | solution.py:571
  67.8 2.7 %collective-permute-start.18 = (bf16[1760,128]{1,0:T(8,128)(2,1)S(1)}, bf16[1760,128]{1,0:T(8,128)(2,1)S(1)}, u32[]{:S(2)}, u32[]{:S(2)}) collective-permute-start(bf16[1760,128]{1,0:T(8,128)(2,1)S(1)} %shard_map.199.refs_1_), channel_id=1, source_target_pairs={{0,1},{1,0},{2,3},{3,2},{4,5},{5,4},{6,7},{7,6},{8,9},{9,8},{10,11... | collective-permute-start | bytes 1351688 | tf_op jit(solution)/shard_map/ppermute | solution.py:559
  70.5 3.5 %collective-permute-done.23.refs_4_ = bf16[1760,128]{1,0:T(8,128)(2,1)S(1)} collective-permute-done((bf16[1760,128]{1,0:T(8,128)(2,1)S(1)}, bf16[1760,128]{1,0:T(8,128)(2,1)S(1)}, u32[]{:S(2)}, u32[]{:S(2)}) %collective-permute-start.23) | collective-permute-done | bytes 450592 | tf_op jit(solution)/shard_map/ppermute | solution.py:571
  74.0 2.4 %collective-permute-start.24 = (bf16[1760,128]{1,0:T(8,128)(2,1)S(1)}, bf16[1760,128]{1,0:T(8,128)(2,1)S(1)}, u32[]{:S(2)}, u32[]{:S(2)}) collective-permute-start(bf16[1760,128]{1,0:T(8,128)(2,1)S(1)} %collective-permute-done.23.refs_4_), channel_id=1, source_target_pairs={{0,1},{1,0},{2,3},{3,2},{4,5},{5,4},{6,7},{7,6},{8,9},{9,8},{10,11... | collective-permute-start | bytes 1351688 | tf_op jit(solution)/shard_map/ppermute | solution.py:559
  76.4 2.3 %collective-permute-done.21.refs_3_ = bf16[1760,128]{1,0:T(8,128)(2,1)S(1)} collective-permute-done((bf16[1760,128]{1,0:T(8,128)(2,1)S(1)}, bf16[1760,128]{1,0:T(8,128)(2,1)S(1)}, u32[]{:S(2)}, u32[]{:S(2)}) %collective-permute-start.21) | collective-permute-done | bytes 450592 | tf_op jit(solution)/shard_map/ppermute | solution.py:571
  78.8 2.2 %collective-permute-start.22 = (bf16[1760,128]{1,0:T(8,128)(2,1)S(1)}, bf16[1760,128]{1,0:T(8,128)(2,1)S(1)}, u32[]{:S(2)}, u32[]{:S(2)}) collective-permute-start(bf16[1760,128]{1,0:T(8,128)(2,1)S(1)} %collective-permute-done.21.refs_3_), channel_id=1, source_target_pairs={{0,1},{1,0},{2,3},{3,2},{4,5},{5,4},{6,7},{7,6},{8,9},{9,8},{10,11... | collective-permute-start | bytes 1351688 | tf_op jit(solution)/shard_map/ppermute | solution.py:559
  81.2 2.0 %shard_map.200 = (f32[256,128]{1,0:T(8,128)S(1)}, f32[96,128]{1,0:T(8,128)S(1)}) custom-call(s32[5]{0:T(128)S(1)} %stack.23.where_ref.refs_0_, bf16[1760,128]{1,0:T(8,128)(2,1)S(1)} %shard_map.199.refs_1_, bf16[1760,128]{1,0:T(8,128)(2,1)S(1)} %collective-permute-done.19.refs_2_, bf16[1760,128]{1,0:T(8,128)(2,1)S(1)} %collective-permute-done.21.refs_3_, ...), custom_call_target="tpu_custom_call" | custom-call | tf_op jit(solution)/shard_map/pallas_call | solution.py:240
  83.2 1.9 %shard_map.201 = (bf16[320,128]{1,0:T(8,128)(2,1)S(1)}, bf16[320,128]{1,0:T(8,128)(2,1)S(1)}) custom-call(s32[5]{0:T(128)S(1)} %stack.23.where_ref.refs_0_, bf16[1760,128]{1,0:T(8,128)(2,1)S(1)} %collective-permute-done.18.refs_1_, bf16[1760,128]{1,0:T(8,128)(2,1)S(1)} %collective-permute-done.20.refs_2_, ...), custom_call_target="tpu_custom_call" | custom-call | tf_op jit(solution)/shard_map/pallas_call | solution.py:240
  85.1 3.0 %collective-permute-start.25 = (bf16[320,128]{1,0:T(8,128)(2,1)S(1)}, bf16[320,128]{1,0:T(8,128)(2,1)S(1)}, u32[]{:S(2)}, u32[]{:S(2)}) collective-permute-start(bf16[320,128]{1,0:T(8,128)(2,1)S(1)} %get-tuple-element.73), channel_id=1, source_target_pairs={{0,64},{64,0},{128,192},{192,128},{1,65},{65,1},{129,193},{193,129... | collective-permute-start | bytes 245768 | tf_op jit(solution)/shard_map/ppermute | solution.py:606
  88.1 2.5 %collective-permute-done.25.arrived_ref = bf16[320,128]{1,0:T(8,128)(2,1)S(1)} collective-permute-done((bf16[320,128]{1,0:T(8,128)(2,1)S(1)}, bf16[320,128]{1,0:T(8,128)(2,1)S(1)}, u32[]{:S(2)}, u32[]{:S(2)}) %collective-permute-start.25) | collective-permute-done | bytes 81952 | tf_op jit(solution)/shard_map/ppermute | solution.py:606
  91.2 5.0 %collective-permute-start.26 = (bf16[256,128]{1,0:T(8,128)(2,1)S(1)}, bf16[256,128]{1,0:T(8,128)(2,1)S(1)}, u32[]{:S(2)}, u32[]{:S(2)}) collective-permute-start(bf16[256,128]{1,0:T(8,128)(2,1)S(1)} %get-tuple-element.75.own_ref), channel_id=1, source_target_pairs={{0,192},{64,128},{128,64},{192,0},{1,193},{65,129},{129,65},{193,1... | collective-permute-start | bytes 196616 | tf_op jit(solution)/shard_map/ppermute | solution.py:608
  (68 shorter events, 24.2 us)
Async XLA Ops:
  6.0 7.5 %collective-permute-start.1 = (bf16[34,104,128]{2,1,0:T(8,128)(2,1)S(1)}, bf16[34,104,128]{2,1,0:T(8,128)(2,1)S(1)}, u32[]{:S(2)}, u32[]{:S(2)}) collective-permute-start(bf16[34,104,128]{2,1,0:T(8,128)(2,1)S(1)} %get-tuple-element.48), channel_id=1, source_target_pairs={{0,1},{1,0},{2,3},{3,2},{4,5},{5,4},{6,7},{7,6},{8,9},{9,8},{10,11... | collective-permute-start | bytes 2715656 | tf_op jit(solution)/shard_map/ppermute | solution.py:559
  13.0 4.9 %collective-permute-start.5 = (bf16[32,104,128]{2,1,0:T(8,128)(2,1)S(1)}, bf16[32,104,128]{2,1,0:T(8,128)(2,1)S(1)}, u32[]{:S(2)}, u32[]{:S(2)}) collective-permute-start(bf16[32,104,128]{2,1,0:T(8,128)(2,1)S(1)} %get-tuple-element.54), channel_id=1, source_target_pairs={{0,1},{1,0},{2,3},{3,2},{4,5},{5,4},{6,7},{7,6},{8,9},{9,8},{10,11... | collective-permute-start | bytes 2555912 | tf_op jit(solution)/shard_map/ppermute | solution.py:559
  14.6 14.2 %collective-permute-start.2 = (bf16[1856,128]{1,0:T(8,128)(2,1)S(1)}, bf16[1856,128]{1,0:T(8,128)(2,1)S(1)}, u32[]{:S(2)}, u32[]{:S(2)}) collective-permute-start(bf16[1856,128]{1,0:T(8,128)(2,1)S(1)} %get-tuple-element.50), channel_id=1, source_target_pairs={{0,16},{1,3},{2,18},{3,5},{4,20},{5,7},{6,22},{7,1},{8,24},{9,11},... | collective-permute-start | bytes 1425416 | tf_op jit(solution)/shard_map/ppermute | solution.py:571
  14.7 18.7 %collective-permute-start.3 = (bf16[1856,128]{1,0:T(8,128)(2,1)S(1)}, bf16[1856,128]{1,0:T(8,128)(2,1)S(1)}, u32[]{:S(2)}, u32[]{:S(2)}) collective-permute-start(bf16[1856,128]{1,0:T(8,128)(2,1)S(1)} %get-tuple-element.51), channel_id=1, source_target_pairs={{0,32},{1,5},{2,34},{3,7},{4,36},{5,1},{6,38},{7,3},{8,40},{9,13},... | collective-permute-start | bytes 1425416 | tf_op jit(solution)/shard_map/ppermute | solution.py:571
  16.9 16.5 %collective-permute-start.4 = (bf16[1856,128]{1,0:T(8,128)(2,1)S(1)}, bf16[1856,128]{1,0:T(8,128)(2,1)S(1)}, u32[]{:S(2)}, u32[]{:S(2)}) collective-permute-start(bf16[1856,128]{1,0:T(8,128)(2,1)S(1)} %get-tuple-element.52), channel_id=1, source_target_pairs={{0,48},{1,7},{2,50},{3,1},{4,52},{5,3},{6,54},{7,5},{8,56},{9,15},... | collective-permute-start | bytes 1425416 | tf_op jit(solution)/shard_map/ppermute | solution.py:571
  18.6 14.7 %collective-permute-start.6 = (bf16[832,128]{1,0:T(8,128)(2,1)S(1)}, bf16[832,128]{1,0:T(8,128)(2,1)S(1)}, u32[]{:S(2)}, u32[]{:S(2)}) collective-permute-start(bf16[832,128]{1,0:T(8,128)(2,1)S(1)} %get-tuple-element.56), channel_id=1, source_target_pairs={{0,16},{1,3},{2,18},{3,5},{4,20},{5,7},{6,22},{7,1},{8,24},{9,11},... | collective-permute-start | bytes 638984 | tf_op jit(solution)/shard_map/ppermute | solution.py:571
  19.1 14.2 %collective-permute-start.7 = (bf16[832,128]{1,0:T(8,128)(2,1)S(1)}, bf16[832,128]{1,0:T(8,128)(2,1)S(1)}, u32[]{:S(2)}, u32[]{:S(2)}) collective-permute-start(bf16[832,128]{1,0:T(8,128)(2,1)S(1)} %get-tuple-element.57), channel_id=1, source_target_pairs={{0,32},{1,5},{2,34},{3,7},{4,36},{5,1},{6,38},{7,3},{8,40},{9,13},... | collective-permute-start | bytes 638984 | tf_op jit(solution)/shard_map/ppermute | solution.py:571
  29.4 5.2 %collective-permute-start.8 = (bf16[832,128]{1,0:T(8,128)(2,1)S(1)}, bf16[832,128]{1,0:T(8,128)(2,1)S(1)}, u32[]{:S(2)}, u32[]{:S(2)}) collective-permute-start(bf16[832,128]{1,0:T(8,128)(2,1)S(1)} %shard_map.193), channel_id=1, source_target_pairs={{0,48},{1,7},{2,50},{3,1},{4,52},{5,3},{6,54},{7,5},{8,56},{9,15},... | collective-permute-start | bytes 638984 | tf_op jit(solution)/shard_map/ppermute | solution.py:571
  35.5 6.9 %collective-permute-start.9 = (bf16[816,128]{1,0:T(8,128)(2,1)S(1)}, bf16[816,128]{1,0:T(8,128)(2,1)S(1)}, u32[]{:S(2)}, u32[]{:S(2)}) collective-permute-start(bf16[816,128]{1,0:T(8,128)(2,1)S(1)} %get-tuple-element.62), channel_id=1, source_target_pairs={{0,4},{1,33},{2,6},{3,35},{4,0},{5,37},{6,2},{7,39},{8,12},{9,41},... | collective-permute-start | bytes 626696 | tf_op jit(solution)/shard_map/ppermute | solution.py:571
  36.3 8.0 %collective-permute-start.10 = (bf16[816,128]{1,0:T(8,128)(2,1)S(1)}, bf16[816,128]{1,0:T(8,128)(2,1)S(1)}, u32[]{:S(2)}, u32[]{:S(2)}) collective-permute-start(bf16[816,128]{1,0:T(8,128)(2,1)S(1)} %get-tuple-element.63), channel_id=1, source_target_pairs={{0,2},{1,17},{2,4},{3,19},{4,6},{5,21},{6,0},{7,23},{8,10},{9,25},... | collective-permute-start | bytes 626696 | tf_op jit(solution)/shard_map/ppermute | solution.py:571
  36.6 7.7 %collective-permute-start.11 = (bf16[816,128]{1,0:T(8,128)(2,1)S(1)}, bf16[816,128]{1,0:T(8,128)(2,1)S(1)}, u32[]{:S(2)}, u32[]{:S(2)}) collective-permute-start(bf16[816,128]{1,0:T(8,128)(2,1)S(1)} %get-tuple-element.64), channel_id=1, source_target_pairs={{0,6},{1,49},{2,0},{3,51},{4,2},{5,53},{6,4},{7,55},{8,14},{9,57},... | collective-permute-start | bytes 626696 | tf_op jit(solution)/shard_map/ppermute | solution.py:571
  45.0 4.7 %collective-permute-start.13 = (bf16[816,128]{1,0:T(8,128)(2,1)S(1)}, bf16[816,128]{1,0:T(8,128)(2,1)S(1)}, u32[]{:S(2)}, u32[]{:S(2)}) collective-permute-start(bf16[816,128]{1,0:T(8,128)(2,1)S(1)} %get-tuple-element.67), channel_id=1, source_target_pairs={{0,8},{1,9},{2,10},{3,11},{4,12},{5,13},{6,14},{7,15},{8,0},{9,1},... | collective-permute-start | bytes 626696 | tf_op jit(solution)/shard_map/ppermute | solution.py:562
  51.4 4.8 %collective-permute-start.14 = (bf16[304,128]{1,0:T(8,128)(2,1)S(1)}, bf16[304,128]{1,0:T(8,128)(2,1)S(1)}, u32[]{:S(2)}, u32[]{:S(2)}) collective-permute-start(bf16[304,128]{1,0:T(8,128)(2,1)S(1)} %get-tuple-element.69), channel_id=1, source_target_pairs={{0,1},{1,0},{2,3},{3,2},{4,5},{5,4},{6,7},{7,6},{8,9},{9,8},{10,11... | collective-permute-start | bytes 233480 | tf_op jit(solution)/shard_map/ppermute | solution.py:559
  56.7 5.7 %collective-permute-start.17 = (bf16[512,128]{1,0:T(8,128)(2,1)S(1)}, bf16[512,128]{1,0:T(8,128)(2,1)S(1)}, u32[]{:S(2)}, u32[]{:S(2)}) collective-permute-start(bf16[512,128]{1,0:T(8,128)(2,1)S(1)} %shard_map.198.own_ref), channel_id=1, source_target_pairs={{0,4},{1,33},{2,6},{3,35},{4,0},{5,37},{6,2},{7,39},{8,12},{9,41},... | collective-permute-start | bytes 393224 | tf_op jit(solution)/shard_map/ppermute | solution.py:571
  57.6 5.0 %collective-permute-start.16 = (bf16[512,128]{1,0:T(8,128)(2,1)S(1)}, bf16[512,128]{1,0:T(8,128)(2,1)S(1)}, u32[]{:S(2)}, u32[]{:S(2)}) collective-permute-start(bf16[512,128]{1,0:T(8,128)(2,1)S(1)} %shard_map.198.own_ref), channel_id=1, source_target_pairs={{0,6},{1,49},{2,0},{3,51},{4,2},{5,53},{6,4},{7,55},{8,14},{9,57},... | collective-permute-start | bytes 393224 | tf_op jit(solution)/shard_map/ppermute | solution.py:571
  58.9 5.3 %collective-permute-start.15 = (bf16[512,128]{1,0:T(8,128)(2,1)S(1)}, bf16[512,128]{1,0:T(8,128)(2,1)S(1)}, u32[]{:S(2)}, u32[]{:S(2)}) collective-permute-start(bf16[512,128]{1,0:T(8,128)(2,1)S(1)} %shard_map.198.own_ref), channel_id=1, source_target_pairs={{0,2},{1,17},{2,4},{3,19},{4,6},{5,21},{6,0},{7,23},{8,10},{9,25},... | collective-permute-start | bytes 393224 | tf_op jit(solution)/shard_map/ppermute | solution.py:571
  64.8 9.2 %collective-permute-start.23 = (bf16[1760,128]{1,0:T(8,128)(2,1)S(1)}, bf16[1760,128]{1,0:T(8,128)(2,1)S(1)}, u32[]{:S(2)}, u32[]{:S(2)}) collective-permute-start(bf16[1760,128]{1,0:T(8,128)(2,1)S(1)} %shard_map.199.refs_1_), channel_id=1, source_target_pairs={{0,32},{1,5},{2,34},{3,7},{4,36},{5,1},{6,38},{7,3},{8,40},{9,13},... | collective-permute-start | bytes 1351688 | tf_op jit(solution)/shard_map/ppermute | solution.py:571
  66.0 12.8 %collective-permute-start.21 = (bf16[1760,128]{1,0:T(8,128)(2,1)S(1)}, bf16[1760,128]{1,0:T(8,128)(2,1)S(1)}, u32[]{:S(2)}, u32[]{:S(2)}) collective-permute-start(bf16[1760,128]{1,0:T(8,128)(2,1)S(1)} %shard_map.199.refs_1_), channel_id=1, source_target_pairs={{0,48},{1,7},{2,50},{3,1},{4,52},{5,3},{6,54},{7,5},{8,56},{9,15},... | collective-permute-start | bytes 1351688 | tf_op jit(solution)/shard_map/ppermute | solution.py:571
  67.7 13.3 %collective-permute-start.19 = (bf16[1760,128]{1,0:T(8,128)(2,1)S(1)}, bf16[1760,128]{1,0:T(8,128)(2,1)S(1)}, u32[]{:S(2)}, u32[]{:S(2)}) collective-permute-start(bf16[1760,128]{1,0:T(8,128)(2,1)S(1)} %shard_map.199.refs_1_), channel_id=1, source_target_pairs={{0,16},{1,3},{2,18},{3,5},{4,20},{5,7},{6,22},{7,1},{8,24},{9,11},... | collective-permute-start | bytes 1351688 | tf_op jit(solution)/shard_map/ppermute | solution.py:571
  67.8 15.3 %collective-permute-start.18 = (bf16[1760,128]{1,0:T(8,128)(2,1)S(1)}, bf16[1760,128]{1,0:T(8,128)(2,1)S(1)}, u32[]{:S(2)}, u32[]{:S(2)}) collective-permute-start(bf16[1760,128]{1,0:T(8,128)(2,1)S(1)} %shard_map.199.refs_1_), channel_id=1, source_target_pairs={{0,1},{1,0},{2,3},{3,2},{4,5},{5,4},{6,7},{7,6},{8,9},{9,8},{10,11... | collective-permute-start | bytes 1351688 | tf_op jit(solution)/shard_map/ppermute | solution.py:559
  74.0 9.2 %collective-permute-start.24 = (bf16[1760,128]{1,0:T(8,128)(2,1)S(1)}, bf16[1760,128]{1,0:T(8,128)(2,1)S(1)}, u32[]{:S(2)}, u32[]{:S(2)}) collective-permute-start(bf16[1760,128]{1,0:T(8,128)(2,1)S(1)} %collective-permute-done.23.refs_4_), channel_id=1, source_target_pairs={{0,1},{1,0},{2,3},{3,2},{4,5},{5,4},{6,7},{7,6},{8,9},{9,8},{10,11... | collective-permute-start | bytes 1351688 | tf_op jit(solution)/shard_map/ppermute | solution.py:559
  78.8 4.4 %collective-permute-start.22 = (bf16[1760,128]{1,0:T(8,128)(2,1)S(1)}, bf16[1760,128]{1,0:T(8,128)(2,1)S(1)}, u32[]{:S(2)}, u32[]{:S(2)}) collective-permute-start(bf16[1760,128]{1,0:T(8,128)(2,1)S(1)} %collective-permute-done.21.refs_3_), channel_id=1, source_target_pairs={{0,1},{1,0},{2,3},{3,2},{4,5},{5,4},{6,7},{7,6},{8,9},{9,8},{10,11... | collective-permute-start | bytes 1351688 | tf_op jit(solution)/shard_map/ppermute | solution.py:559
  85.1 5.5 %collective-permute-start.25 = (bf16[320,128]{1,0:T(8,128)(2,1)S(1)}, bf16[320,128]{1,0:T(8,128)(2,1)S(1)}, u32[]{:S(2)}, u32[]{:S(2)}) collective-permute-start(bf16[320,128]{1,0:T(8,128)(2,1)S(1)} %get-tuple-element.73), channel_id=1, source_target_pairs={{0,64},{64,0},{128,192},{192,128},{1,65},{65,1},{129,193},{193,129... | collective-permute-start | bytes 245768 | tf_op jit(solution)/shard_map/ppermute | solution.py:606
  91.2 6.6 %collective-permute-start.26 = (bf16[256,128]{1,0:T(8,128)(2,1)S(1)}, bf16[256,128]{1,0:T(8,128)(2,1)S(1)}, u32[]{:S(2)}, u32[]{:S(2)}) collective-permute-start(bf16[256,128]{1,0:T(8,128)(2,1)S(1)} %get-tuple-element.75.own_ref), channel_id=1, source_target_pairs={{0,192},{64,128},{128,64},{192,0},{1,193},{65,129},{129,65},{193,1... | collective-permute-start | bytes 196616 | tf_op jit(solution)/shard_map/ppermute | solution.py:608
  (14 other events, 175.3 us)

commit v5 on v4

--- a/solution.py
+++ b/solution.py
@@ -251,8 +251,7 @@
     return jnp.where(core == 0, first * 8 + z * 4 + second, second * 8 + z * 4 + first)
 
 
-def pack_rows(where_ref, keeps, received, offset, step):
-    there = lax.rem(where_ref[3] + offset, 4)
+def pack_rows(where_ref, keeps, received, there, step):
     parts = []
     for near in range(2):
         chip = chip_of(where_ref[0], there, near, lax.rem(where_ref[4] + step, 4))
@@ -268,49 +267,82 @@
     )
 
 
-def stage_kernel(kinds, offsets, where_ref, *refs):
-    keeps, received, outs = refs[:kinds], refs[kinds : 2 * kinds], refs[-len(offsets) :]
+def halves_kernel(kinds, where_ref, *refs):
+    keeps, received, outs = refs[:kinds], refs[kinds : 2 * kinds], refs[-4:]
+    place = where_ref[3]
+    near, far = place ^ 1, 3 - place
     pair = 2 * kinds * keeps[0].shape[1]
-    for offset, out_ref in zip(offsets, outs):
-        for step in range(4):
-            rows = pack_rows(where_ref, keeps, received, offset, step)
-            out_ref[step * pair : (step + 1) * pair] = rows.astype(out_ref.dtype)
+    for out_ref, places, steps in (
+        (outs[0], (near, 3 - near), (0, 1)),
+        (outs[1], (far, far ^ 1), (2, 3)),
+        (outs[2], (place, far), (0, 1)),
+        (outs[3], (place, near), (2, 3)),
+    ):
+        for i, there in enumerate(places):
+            for j, step in enumerate(steps):
+                rows = pack_rows(where_ref, keeps, received, there, step)
+                first = (2 * i + j) * pair
+                out_ref[first : first + pair] = rows.astype(out_ref.dtype)
         low_rows = out_ref.shape[0] - 4 * pair
         if low_rows:
             out_ref[4 * pair :] = pack_low(keeps[-1], received[-1], low_rows // 2).astype(out_ref.dtype)
 
 
-def stage(offsets, where, keeps, received, low_rows=0, after=()):
+def halves(where, keeps, received, low_rows=0, after=()):
     chips, piece, tokens = keeps[0].shape
-    rows = 8 * len(keeps) * piece + low_rows
-    out_shape = [jax.ShapeDtypeStruct((rows, tokens), BF16 if offset else F32) for offset in offsets]
-    kernel = functools.partial(stage_kernel, len(keeps), offsets)
+    rows = 8 * len(keeps) * piece
+    out_shape = [
+        jax.ShapeDtypeStruct((rows + low_rows, tokens), BF16),
+        jax.ShapeDtypeStruct((rows, tokens), BF16),
+        jax.ShapeDtypeStruct((rows + low_rows, tokens), F32),
+        jax.ShapeDtypeStruct((rows, tokens), F32),
+    ]
+    kernel = functools.partial(halves_kernel, len(keeps))
     return vmem_call(kernel, out_shape, where, *keeps, *received, *after, unread=len(after))
+
+
+def add_kernel(low_rows, where_ref, one_own, two_own, one_got, two_got, one_send, two_send, one_keep, two_keep):
+    for own, got, send, keep, low in (
+        (one_own, one_got, one_send, one_keep, low_rows),
+        (two_own, two_got, two_send, two_keep, 0),
+    ):
+        half = keep.shape[0] - low
+        summed = own[...] + got[...].astype(F32)
+        keep[:half] = summed[:half]
+        send[:half] = summed[half : 2 * half].astype(BF16)
+        if low:
+            keep[half:] = summed[2 * half :]
+            send[half:] = summed[2 * half :].astype(BF16)
+
+
+def add(where, own, got, low_rows=0):
+    rows, tokens = own[1].shape
+    out_shape = [jax.ShapeDtypeStruct((rows // 2 + low, tokens), BF16) for low in (low_rows, 0)]
+    out_shape += [jax.ShapeDtypeStruct((rows // 2 + low, tokens), F32) for low in (low_rows, 0)]
+    return vmem_call(functools.partial(add_kernel, low_rows), out_shape, where, *own, *got)
 
 
 def second_kernel(where_ref, *refs):
     wide, tall, expand_ref, outs, expand_out = refs[:4], refs[4:8], refs[8], refs[-5:-1], refs[-1]
     expand_out[...] = expand_ref[...]
-    down = tall[0].shape[0] // 4
+    down = tall[0].shape[0] // 2
     pair = 2 * down
 
-    def add(refs, first, count):
+    def summed(refs, half, first, count):
         rows = slice(first, first + count)
-        total = refs[0][rows]
-        for ref in refs[1:]:
-            total = total + ref[rows].astype(F32)
-        return total
-
-    low = add(wide, 4 * pair, wide[0].shape[0] - 4 * pair)
+        return refs[half][rows] + refs[2 + half][rows].astype(F32)
+
+    low = summed(wide, 0, 2 * pair, wide[0].shape[0] - 2 * pair)
     for step, out_ref in enumerate(outs):
-        out_ref[:pair] = add(wide, step * pair, pair).astype(out_ref.dtype)
-        out_ref[pair : pair + down] = add(tall, step * down, down).astype(out_ref.dtype)
+        half, place = step // 2, step % 2
+        out_ref[:pair] = summed(wide, half, place * pair, pair).astype(out_ref.dtype)
+        out_ref[pair : pair + down] = summed(tall, half, place * down, down).astype(out_ref.dtype)
         out_ref[pair + down :] = low.astype(out_ref.dtype)
 
 
-def second(where, wide, tall, expand, piece, ready):
-    rows, tokens = wide[0].shape
-    rows -= 10 * piece
+def second(where, wide, tall, expand, piece, low_rows, ready):
+    tokens = wide[0].shape[1]
+    rows = 6 * piece + low_rows
     out_shape = [jax.ShapeDtypeStruct((rows, tokens), F32 if i == 0 else BF16) for i in range(4)]
     out_shape.append(jax.ShapeDtypeStruct(expand.shape, BF16))
     return vmem_call(second_kernel, out_shape, where, *wide, *tall, expand, *ready, unread=len(ready))
@@ -570,6 +602,9 @@
                 pairs.append((i, i - (i // 2 % 4) * 2 + ((i // 2 + offset) % 4) * 2))
         return lax.ppermute(value, "row", pairs)
 
+    def across(other, value):
+        return lax.ppermute(value, "row", [(i, i ^ (other * (16 if i % 2 == 0 else 2))) for i in range(64)])
+
     def along_all(second_axis, values, order=(2, 1, 3)):
         return [along(second_axis, offset, values[offset - 1]) for offset in order]
 
@@ -580,16 +615,19 @@
     )
     down_send, down_keep = tall_sums(where, down_scales.T, output_gradient, down_values, piece, gate_keep)
     keeps, received = [gate_keep, up_keep], [exchange(gate_send), exchange(up_send)]
-    own, *out = stage((0, 1, 2, 3), where, keeps, received, low_rows)
-    wide = [own, *along_all(False, out, (1, 2, 3))]
+    one, two, *wide = halves(where, keeps, received, low_rows)
+    wide_got = [across(1, one), across(3, two)]
     keeps, received = [down_keep], [exchange(down_send)]
-    own, one, two = stage((0, 1, 2), where, keeps, received, after=(own,))
-    (three,) = stage((3,), where, keeps, received, after=(wide[1],))
-    tall = [own, along(False, 1, one), along(False, 2, two), along(False, 3, three)]
+    one, two, *tall = halves(where, keeps, received, after=wide[:1])
+    tall_got = [across(1, one), across(3, two)]
     gate_weight, up_weight, expand = weights(
-        gate_scales, up_scales, gate_values, up_values, (gate_expand, up_expand, down_reduce), own
-    )
-    own, *out, leaving = second(where, wide, tall, expand, piece, (gate_weight, up_weight))
+        gate_scales, up_scales, gate_values, up_values, (gate_expand, up_expand, down_reduce), tall[0]
+    )
+    one, two, *wide = add(where, wide, wide_got, low_rows)
+    wide += [across(3, one), across(1, two)]
+    one, two, *tall = add(where, tall, tall_got)
+    tall += [across(3, one), across(1, two)]
+    own, *out, leaving = second(where, wide, tall, expand, piece, low_rows, (gate_weight, up_weight))
     far_expand = along_z(leaving)
     own, out = third(where, own, along_all(True, out), far_expand)
     send, keep, gate_expand_gradient, up_expand_gradient, down_reduce_gradient = middle(

time: 101 us -> 100 us (0.990)
  waiting for transfers between devices: 34.6 us -> 27.6 us
  starting transfers between devices: 39.4 us -> 45.7 us
    ppermute x15 -> x9, waiting for transfers between devices: 23.1 us -> 10.2 us  [along(): return lax.ppermute(value, 'row', pairs)]
    ppermute x0 -> x8, starting transfers between devices: none -> 7.33 us  [across(): lax.ppermute(value, 'row', [(i, i ^ other * (16 if i % 2 == 0 else 2)) fo...]
    ppermute x0 -> x8, waiting for transfers between devices: none -> 5.07 us  [across(): lax.ppermute(value, 'row', [(i, i ^ other * (16 if i % 2 == 0 else 2)) fo...]
    ppermute x15 -> x9, starting transfers between devices: 14.4 us -> 12 us  [along(): return lax.ppermute(value, 'row', pairs)]
    ppermute x1, waiting for transfers between devices: 2.5 us -> 4.57 us  [per_device(): lax.ppermute(out, 'col', [(i, i ^ 1) for i in range(4)])]
    ppermute x8, starting transfers between devices: 15.3 us -> 16.8 us  [exchange(): return lax.ppermute(value, 'row', [(i, i ^ 1) for i in range(64)])]
    ppermute x1, starting transfers between devices: 4.98 us -> 3.56 us  [per_device(): arrived = lax.ppermute(out, 'col', [(i, 3 - i) for i in range(4)])]
    ppermute x2, starting transfers between devices: 1.73 us -> 3.05 us  [along_z(): return lax.ppermute(value, 'row', [(i, i ^ 8) for i in range(64)])]
  transfers between devices with their start and end apart: 27 -> 29, of which waited for: 14 -> 14; matrix products, arithmetic and copies ran while one was open for 0% -> 0% of each run, Pallas kernels for 11% -> 12%
where the time goes in v5:
time: 100 us; the launch traced here: 99.2 us
  starting transfers between devices  45.7 us (46%)
  waiting for transfers between devices  27.6 us (28%)
  Pallas kernels  24.7 us (25%)
    ppermute x8, starting transfers between devices, exchange(): return lax.ppermute(value, 'row', [(i, i ^ 1) for i in range(64)])  16.8 us
    pallas_call x13, Pallas kernels, vmem_call(): pl.pallas_call(kernel, in_specs=[smem()] + [vmem] * (len(args) - 1 - unre...  13.1 us
    ppermute x9, starting transfers between devices, along(): return lax.ppermute(value, 'row', pairs)  12 us
    ppermute x9, waiting for transfers between devices, along(): return lax.ppermute(value, 'row', pairs)  10.2 us
    ppermute x8, starting transfers between devices, across(): lax.ppermute(value, 'row', [(i, i ^ other * (16 if i % 2 == 0 else 2)) fo...  7.33 us
    pallas_call x1, Pallas kernels, wide_sums(): pl.pallas_call(wide_kernel, in_specs=[smem()] + [hbm] * 9, out_specs=[vme...  5.29 us
    ppermute x2, waiting for transfers between devices, along_z(): return lax.ppermute(value, 'row', [(i, i ^ 8) for i in range(64)])  5.09 us
    ppermute x8, waiting for transfers between devices, across(): lax.ppermute(value, 'row', [(i, i ^ other * (16 if i % 2 == 0 else 2)) fo...  5.07 us
  transfers between devices with their start and end apart: 29, of which 14 were waited for; matrix products, arithmetic and copies ran while one was open for 0% of the time, Pallas kernels for 12%

profile of v5, /device:TPU:1, one launch (start us, length us, event | category | flops | bytes accessed | tf_op | source)
XLA Modules:
  0.0 99.2 jit_solution(10910991257371761253)
XLA Ops:
  0.7 5.3 %shard_map.189 = (bf16[32,104,128]{2,1,0:T(8,128)(2,1)S(1)}, bf16[32,104,128]{2,1,0:T(8,128)(2,1)S(1)}, bf16[34,104,128]{2,1,0:T(8,128)(2,1)S(1)}, bf16[34,104,128]{2,1,0:T(8,128)(2,1)S(1)}) custom-call(s32[5]{0:T(128)S(1)} %stack.23.where_ref.refs_0_, f32[2,52]{1,0:T(2,128)} %gate_scales.1, f32[2,52]{1,0:T(2,128)} %up_scales.1, ...), custom_call_target="tpu_custom_call" | custom-call | tf_op jit(solution)/shard_map/pallas_call | solution.py:170
  6.0 3.3 %collective-permute-start.1 = (bf16[34,104,128]{2,1,0:T(8,128)(2,1)S(1)}, bf16[34,104,128]{2,1,0:T(8,128)(2,1)S(1)}, u32[]{:S(2)}, u32[]{:S(2)}) collective-permute-start(bf16[34,104,128]{2,1,0:T(8,128)(2,1)S(1)} %get-tuple-element.57), channel_id=1, source_target_pairs={{0,1},{1,0},{2,3},{3,2},{4,5},{5,4},{6,7},{7,6},{8,9},{9,8},{10,11... | collective-permute-start | bytes 2715656 | tf_op jit(solution)/shard_map/ppermute | solution.py:591
  9.4 3.6 %shard_map.192 = (bf16[32,104,128]{2,1,0:T(8,128)(2,1)S(1)}, bf16[32,104,128]{2,1,0:T(8,128)(2,1)S(1)}) custom-call(s32[5]{0:T(128)S(1)} %stack.23.where_ref.refs_0_, f32[2,52]{1,0:T(2,128)} %bitcast.6, bf16[128,256]{1,0:T(8,128)(2,1)} %gradient_ref.1, bf16[6656,256]{1,0:T(8,128)(2,1)} %values_hbm.1, ...), custom_call_target="tpu_custom_call" | custom-call | tf_op jit(solution)/shard_map/pallas_call | solution.py:191
  17.4 1.7 %collective-permute-start.8 = (bf16[832,128]{1,0:T(8,128)(2,1)S(1)}, bf16[832,128]{1,0:T(8,128)(2,1)S(1)}, u32[]{:S(2)}, u32[]{:S(2)}) collective-permute-start(bf16[832,128]{1,0:T(8,128)(2,1)S(1)} %get-tuple-element.71), channel_id=1, source_target_pairs={{0,48},{1,7},{2,50},{3,5},{4,52},{5,3},{6,54},{7,1},{8,56},{9,15},... | collective-permute-start | bytes 638984 | tf_op jit(solution)/shard_map/ppermute | solution.py:606
  19.0 4.2 %collective-permute-done.3.two_got = bf16[1664,128]{1,0:T(8,128)(2,1)S(1)} collective-permute-done((bf16[1664,128]{1,0:T(8,128)(2,1)S(1)}, bf16[1664,128]{1,0:T(8,128)(2,1)S(1)}, u32[]{:S(2)}, u32[]{:S(2)}) %collective-permute-start.3) | collective-permute-done | bytes 426016 | tf_op jit(solution)/shard_map/ppermute | solution.py:606
  28.4 2.8 %shard_map.195 = (bf16[256,6656]{1,0:T(8,128)(2,1)S(1)}, bf16[256,6656]{1,0:T(8,128)(2,1)S(1)}, bf16[3,64,104]{2,1,0:T(8,128)(2,1)S(1)}) custom-call(f32[2,52]{1,0:T(2,128)S(1)} %copy-done.9, f32[2,52]{1,0:T(2,128)S(1)} %copy-done.10, bf16[256,6656]{1,0:T(8,128)(2,1)S(1)} %copy-done, bf16[256,6656]{1,0:T(8,128)(2,1)S(1)} %copy-done.1, ...), custom_call_target="tpu_custom_call" | custom-call | flops 3407872 | bytes 13631488 | tf_op jit(solution)/shard_map/pallas_call | solution.py:225
  32.6 2.2 %collective-permute-start.11 = (bf16[816,128]{1,0:T(8,128)(2,1)S(1)}, bf16[816,128]{1,0:T(8,128)(2,1)S(1)}, u32[]{:S(2)}, u32[]{:S(2)}) collective-permute-start(bf16[816,128]{1,0:T(8,128)(2,1)S(1)} %get-tuple-element.80), channel_id=1, source_target_pairs={{0,4},{1,33},{2,6},{3,35},{4,0},{5,37},{6,2},{7,39},{8,12},{9,41},... | collective-permute-start | bytes 626696 | tf_op jit(solution)/shard_map/ppermute | solution.py:603
  35.4 2.1 %collective-permute-start.13 = (bf16[816,128]{1,0:T(8,128)(2,1)S(1)}, bf16[816,128]{1,0:T(8,128)(2,1)S(1)}, u32[]{:S(2)}, u32[]{:S(2)}) collective-permute-start(bf16[816,128]{1,0:T(8,128)(2,1)S(1)} %get-tuple-element.82), channel_id=1, source_target_pairs={{0,6},{1,49},{2,0},{3,51},{4,2},{5,53},{6,4},{7,55},{8,14},{9,57},... | collective-permute-start | bytes 626696 | tf_op jit(solution)/shard_map/ppermute | solution.py:603
  39.1 1.8 %collective-permute-done.14.after_ref.far_expand_ref = bf16[3,64,104]{2,1,0:T(8,128)(2,1)S(1)} collective-permute-done((bf16[3,64,104]{2,1,0:T(8,128)(2,1)S(1)}, bf16[3,64,104]{2,1,0:T(8,128)(2,1)S(1)}, u32[]{:S(2)}, u32[]{:S(2)}) %collective-permute-start.14) | collective-permute-done | bytes 39968 | tf_op jit(solution)/shard_map/ppermute | solution.py:594
  43.5 3.3 %collective-permute-done.15.arrived_ref = bf16[816,128]{1,0:T(8,128)(2,1)S(1)} collective-permute-done((bf16[816,128]{1,0:T(8,128)(2,1)S(1)}, bf16[816,128]{1,0:T(8,128)(2,1)S(1)}, u32[]{:S(2)}, u32[]{:S(2)}) %collective-permute-start.15) | collective-permute-done | bytes 208928 | tf_op jit(solution)/shard_map/ppermute | solution.py:594
  46.8 1.7 %shard_map.198 = (bf16[304,128]{1,0:T(8,128)(2,1)S(1)}, f32[304,128]{1,0:T(8,128)S(1)}, f32[64,104]{1,0:T(8,128)}, f32[64,104]{1,0:T(8,128)}, f32[64,104]{1,0:T(8,128)}) custom-call(s32[5]{0:T(128)S(1)} %stack.23.where_ref.refs_0_, f32[816,128]{1,0:T(8,128)S(1)} %get-tuple-element.84.own_ref, bf16[816,128]{1,0:T(8,128)(2,1)S(1)} %collective-permute-done.15.arrived_ref, ...), custom_call_target="tpu_custom_call" | custom-call | tf_op jit(solution)/shard_map/pallas_call | solution.py:240
  48.5 4.9 %collective-permute-start.16 = (bf16[304,128]{1,0:T(8,128)(2,1)S(1)}, bf16[304,128]{1,0:T(8,128)(2,1)S(1)}, u32[]{:S(2)}, u32[]{:S(2)}) collective-permute-start(bf16[304,128]{1,0:T(8,128)(2,1)S(1)} %get-tuple-element.87), channel_id=1, source_target_pairs={{0,1},{1,0},{2,3},{3,2},{4,5},{5,4},{6,7},{7,6},{8,9},{9,8},{10,11... | collective-permute-start | bytes 233480 | tf_op jit(solution)/shard_map/ppermute | solution.py:591
  54.9 2.7 %collective-permute-start.19 = (bf16[512,128]{1,0:T(8,128)(2,1)S(1)}, bf16[512,128]{1,0:T(8,128)(2,1)S(1)}, u32[]{:S(2)}, u32[]{:S(2)}) collective-permute-start(bf16[512,128]{1,0:T(8,128)(2,1)S(1)} %shard_map.199.own_ref), channel_id=1, source_target_pairs={{0,4},{1,33},{2,6},{3,35},{4,0},{5,37},{6,2},{7,39},{8,12},{9,41},... | collective-permute-start | bytes 393224 | tf_op jit(solution)/shard_map/ppermute | solution.py:603
  64.9 1.7 %collective-permute-start.23 = (bf16[1760,128]{1,0:T(8,128)(2,1)S(1)}, bf16[1760,128]{1,0:T(8,128)(2,1)S(1)}, u32[]{:S(2)}, u32[]{:S(2)}) collective-permute-start(bf16[1760,128]{1,0:T(8,128)(2,1)S(1)} %shard_map.200.refs_1_), channel_id=1, source_target_pairs={{0,48},{1,7},{2,50},{3,1},{4,52},{5,3},{6,54},{7,5},{8,56},{9,15},... | collective-permute-start | bytes 1351688 | tf_op jit(solution)/shard_map/ppermute | solution.py:603
  66.9 3.2 %collective-permute-start.20 = (bf16[1760,128]{1,0:T(8,128)(2,1)S(1)}, bf16[1760,128]{1,0:T(8,128)(2,1)S(1)}, u32[]{:S(2)}, u32[]{:S(2)}) collective-permute-start(bf16[1760,128]{1,0:T(8,128)(2,1)S(1)} %shard_map.200.refs_1_), channel_id=1, source_target_pairs={{0,1},{1,0},{2,3},{3,2},{4,5},{5,4},{6,7},{7,6},{8,9},{9,8},{10,11... | collective-permute-start | bytes 1351688 | tf_op jit(solution)/shard_map/ppermute | solution.py:591
  70.1 3.0 %collective-permute-done.25.refs_4_ = bf16[1760,128]{1,0:T(8,128)(2,1)S(1)} collective-permute-done((bf16[1760,128]{1,0:T(8,128)(2,1)S(1)}, bf16[1760,128]{1,0:T(8,128)(2,1)S(1)}, u32[]{:S(2)}, u32[]{:S(2)}) %collective-permute-start.25) | collective-permute-done | bytes 450592 | tf_op jit(solution)/shard_map/ppermute | solution.py:603
  73.1 2.4 %collective-permute-start.26 = (bf16[1760,128]{1,0:T(8,128)(2,1)S(1)}, bf16[1760,128]{1,0:T(8,128)(2,1)S(1)}, u32[]{:S(2)}, u32[]{:S(2)}) collective-permute-start(bf16[1760,128]{1,0:T(8,128)(2,1)S(1)} %collective-permute-done.25.refs_4_), channel_id=1, source_target_pairs={{0,1},{1,0},{2,3},{3,2},{4,5},{5,4},{6,7},{7,6},{8,9},{9,8},{10,11... | collective-permute-start | bytes 1351688 | tf_op jit(solution)/shard_map/ppermute | solution.py:591
  75.5 2.4 %collective-permute-done.23.refs_3_ = bf16[1760,128]{1,0:T(8,128)(2,1)S(1)} collective-permute-done((bf16[1760,128]{1,0:T(8,128)(2,1)S(1)}, bf16[1760,128]{1,0:T(8,128)(2,1)S(1)}, u32[]{:S(2)}, u32[]{:S(2)}) %collective-permute-start.23) | collective-permute-done | bytes 450592 | tf_op jit(solution)/shard_map/ppermute | solution.py:603
  80.3 2.0 %shard_map.201 = (f32[256,128]{1,0:T(8,128)S(1)}, f32[96,128]{1,0:T(8,128)S(1)}) custom-call(s32[5]{0:T(128)S(1)} %stack.23.where_ref.refs_0_, bf16[1760,128]{1,0:T(8,128)(2,1)S(1)} %shard_map.200.refs_1_, bf16[1760,128]{1,0:T(8,128)(2,1)S(1)} %collective-permute-done.21.refs_2_, bf16[1760,128]{1,0:T(8,128)(2,1)S(1)} %collective-permute-done.23.refs_3_, ...), custom_call_target="tpu_custom_call" | custom-call | tf_op jit(solution)/shard_map/pallas_call | solution.py:240
  82.3 1.9 %shard_map.202 = (bf16[320,128]{1,0:T(8,128)(2,1)S(1)}, bf16[320,128]{1,0:T(8,128)(2,1)S(1)}) custom-call(s32[5]{0:T(128)S(1)} %stack.23.where_ref.refs_0_, bf16[1760,128]{1,0:T(8,128)(2,1)S(1)} %collective-permute-done.20.refs_1_, bf16[1760,128]{1,0:T(8,128)(2,1)S(1)} %collective-permute-done.22.refs_2_, ...), custom_call_target="tpu_custom_call" | custom-call | tf_op jit(solution)/shard_map/pallas_call | solution.py:240
  84.2 3.1 %collective-permute-start.27 = (bf16[320,128]{1,0:T(8,128)(2,1)S(1)}, bf16[320,128]{1,0:T(8,128)(2,1)S(1)}, u32[]{:S(2)}, u32[]{:S(2)}) collective-permute-start(bf16[320,128]{1,0:T(8,128)(2,1)S(1)} %get-tuple-element.91), channel_id=1, source_target_pairs={{0,64},{64,0},{128,192},{192,128},{1,65},{65,1},{129,193},{193,129... | collective-permute-start | bytes 245768 | tf_op jit(solution)/shard_map/ppermute | solution.py:644
  87.3 4.6 %collective-permute-done.27.arrived_ref = bf16[320,128]{1,0:T(8,128)(2,1)S(1)} collective-permute-done((bf16[320,128]{1,0:T(8,128)(2,1)S(1)}, bf16[320,128]{1,0:T(8,128)(2,1)S(1)}, u32[]{:S(2)}, u32[]{:S(2)}) %collective-permute-start.27) | collective-permute-done | bytes 81952 | tf_op jit(solution)/shard_map/ppermute | solution.py:644
  92.4 3.6 %collective-permute-start.28 = (bf16[256,128]{1,0:T(8,128)(2,1)S(1)}, bf16[256,128]{1,0:T(8,128)(2,1)S(1)}, u32[]{:S(2)}, u32[]{:S(2)}) collective-permute-start(bf16[256,128]{1,0:T(8,128)(2,1)S(1)} %get-tuple-element.93.own_ref), channel_id=1, source_target_pairs={{0,192},{64,128},{128,64},{192,0},{1,193},{65,129},{129,65},{193,1... | collective-permute-start | bytes 196616 | tf_op jit(solution)/shard_map/ppermute | solution.py:646
  96.0 1.8 %collective-permute-done.28.arrived_ref = bf16[256,128]{1,0:T(8,128)(2,1)S(1)} collective-permute-done((bf16[256,128]{1,0:T(8,128)(2,1)S(1)}, bf16[256,128]{1,0:T(8,128)(2,1)S(1)}, u32[]{:S(2)}, u32[]{:S(2)}) %collective-permute-start.28) | collective-permute-done | bytes 65568 | tf_op jit(solution)/shard_map/ppermute | solution.py:646
  (73 shorter events, 29.3 us)
Async XLA Ops:
  6.0 7.5 %collective-permute-start.1 = (bf16[34,104,128]{2,1,0:T(8,128)(2,1)S(1)}, bf16[34,104,128]{2,1,0:T(8,128)(2,1)S(1)}, u32[]{:S(2)}, u32[]{:S(2)}) collective-permute-start(bf16[34,104,128]{2,1,0:T(8,128)(2,1)S(1)} %get-tuple-element.57), channel_id=1, source_target_pairs={{0,1},{1,0},{2,3},{3,2},{4,5},{5,4},{6,7},{7,6},{8,9},{9,8},{10,11... | collective-permute-start | bytes 2715656 | tf_op jit(solution)/shard_map/ppermute | solution.py:591
  14.6 8.7 %collective-permute-start.2 = (bf16[1856,128]{1,0:T(8,128)(2,1)S(1)}, bf16[1856,128]{1,0:T(8,128)(2,1)S(1)}, u32[]{:S(2)}, u32[]{:S(2)}) collective-permute-start(bf16[1856,128]{1,0:T(8,128)(2,1)S(1)} %get-tuple-element.60), channel_id=1, source_target_pairs={{0,16},{1,3},{2,18},{3,1},{4,20},{5,7},{6,22},{7,5},{8,24},{9,11},... | collective-permute-start | bytes 1425416 | tf_op jit(solution)/shard_map/ppermute | solution.py:606
  14.7 8.6 %collective-permute-start.3 = (bf16[1664,128]{1,0:T(8,128)(2,1)S(1)}, bf16[1664,128]{1,0:T(8,128)(2,1)S(1)}, u32[]{:S(2)}, u32[]{:S(2)}) collective-permute-start(bf16[1664,128]{1,0:T(8,128)(2,1)S(1)} %get-tuple-element.61), channel_id=1, source_target_pairs={{0,48},{1,7},{2,50},{3,5},{4,52},{5,3},{6,54},{7,1},{8,56},{9,15},... | collective-permute-start | bytes 1277960 | tf_op jit(solution)/shard_map/ppermute | solution.py:606
  16.9 8.6 %collective-permute-start.7 = (bf16[832,128]{1,0:T(8,128)(2,1)S(1)}, bf16[832,128]{1,0:T(8,128)(2,1)S(1)}, u32[]{:S(2)}, u32[]{:S(2)}) collective-permute-start(bf16[832,128]{1,0:T(8,128)(2,1)S(1)} %get-tuple-element.70), channel_id=1, source_target_pairs={{0,16},{1,3},{2,18},{3,1},{4,20},{5,7},{6,22},{7,5},{8,24},{9,11},... | collective-permute-start | bytes 638984 | tf_op jit(solution)/shard_map/ppermute | solution.py:606
  17.4 8.2 %collective-permute-start.8 = (bf16[832,128]{1,0:T(8,128)(2,1)S(1)}, bf16[832,128]{1,0:T(8,128)(2,1)S(1)}, u32[]{:S(2)}, u32[]{:S(2)}) collective-permute-start(bf16[832,128]{1,0:T(8,128)(2,1)S(1)} %get-tuple-element.71), channel_id=1, source_target_pairs={{0,48},{1,7},{2,50},{3,5},{4,52},{5,3},{6,54},{7,1},{8,56},{9,15},... | collective-permute-start | bytes 638984 | tf_op jit(solution)/shard_map/ppermute | solution.py:606
  24.0 8.0 %collective-permute-start.4 = (bf16[1024,128]{1,0:T(8,128)(2,1)S(1)}, bf16[1024,128]{1,0:T(8,128)(2,1)S(1)}, u32[]{:S(2)}, u32[]{:S(2)}) collective-permute-start(bf16[1024,128]{1,0:T(8,128)(2,1)S(1)} %get-tuple-element.64), channel_id=1, source_target_pairs={{0,48},{1,7},{2,50},{3,5},{4,52},{5,3},{6,54},{7,1},{8,56},{9,15},... | collective-permute-start | bytes 786440 | tf_op jit(solution)/shard_map/ppermute | solution.py:606
  25.4 6.5 %collective-permute-start.5 = (bf16[832,128]{1,0:T(8,128)(2,1)S(1)}, bf16[832,128]{1,0:T(8,128)(2,1)S(1)}, u32[]{:S(2)}, u32[]{:S(2)}) collective-permute-start(bf16[832,128]{1,0:T(8,128)(2,1)S(1)} %get-tuple-element.65), channel_id=1, source_target_pairs={{0,16},{1,3},{2,18},{3,1},{4,20},{5,7},{6,22},{7,5},{8,24},{9,11},... | collective-permute-start | bytes 638984 | tf_op jit(solution)/shard_map/ppermute | solution.py:606
  26.2 5.8 %collective-permute-start.9 = (bf16[416,128]{1,0:T(8,128)(2,1)S(1)}, bf16[416,128]{1,0:T(8,128)(2,1)S(1)}, u32[]{:S(2)}, u32[]{:S(2)}) collective-permute-start(bf16[416,128]{1,0:T(8,128)(2,1)S(1)} %get-tuple-element.74), channel_id=1, source_target_pairs={{0,48},{1,7},{2,50},{3,5},{4,52},{5,3},{6,54},{7,1},{8,56},{9,15},... | collective-permute-start | bytes 319496 | tf_op jit(solution)/shard_map/ppermute | solution.py:606
  27.6 4.3 %collective-permute-start.10 = (bf16[416,128]{1,0:T(8,128)(2,1)S(1)}, bf16[416,128]{1,0:T(8,128)(2,1)S(1)}, u32[]{:S(2)}, u32[]{:S(2)}) collective-permute-start(bf16[416,128]{1,0:T(8,128)(2,1)S(1)} %get-tuple-element.75), channel_id=1, source_target_pairs={{0,16},{1,3},{2,18},{3,1},{4,20},{5,7},{6,22},{7,5},{8,24},{9,11},... | collective-permute-start | bytes 319496 | tf_op jit(solution)/shard_map/ppermute | solution.py:606
  32.6 8.2 %collective-permute-start.11 = (bf16[816,128]{1,0:T(8,128)(2,1)S(1)}, bf16[816,128]{1,0:T(8,128)(2,1)S(1)}, u32[]{:S(2)}, u32[]{:S(2)}) collective-permute-start(bf16[816,128]{1,0:T(8,128)(2,1)S(1)} %get-tuple-element.80), channel_id=1, source_target_pairs={{0,4},{1,33},{2,6},{3,35},{4,0},{5,37},{6,2},{7,39},{8,12},{9,41},... | collective-permute-start | bytes 626696 | tf_op jit(solution)/shard_map/ppermute | solution.py:603
  34.8 6.6 %collective-permute-start.12 = (bf16[816,128]{1,0:T(8,128)(2,1)S(1)}, bf16[816,128]{1,0:T(8,128)(2,1)S(1)}, u32[]{:S(2)}, u32[]{:S(2)}) collective-permute-start(bf16[816,128]{1,0:T(8,128)(2,1)S(1)} %get-tuple-element.81), channel_id=1, source_target_pairs={{0,2},{1,17},{2,4},{3,19},{4,6},{5,21},{6,0},{7,23},{8,10},{9,25},... | collective-permute-start | bytes 626696 | tf_op jit(solution)/shard_map/ppermute | solution.py:603
  35.4 6.0 %collective-permute-start.13 = (bf16[816,128]{1,0:T(8,128)(2,1)S(1)}, bf16[816,128]{1,0:T(8,128)(2,1)S(1)}, u32[]{:S(2)}, u32[]{:S(2)}) collective-permute-start(bf16[816,128]{1,0:T(8,128)(2,1)S(1)} %get-tuple-element.82), channel_id=1, source_target_pairs={{0,6},{1,49},{2,0},{3,51},{4,2},{5,53},{6,4},{7,55},{8,14},{9,57},... | collective-permute-start | bytes 626696 | tf_op jit(solution)/shard_map/ppermute | solution.py:603
  42.1 4.7 %collective-permute-start.15 = (bf16[816,128]{1,0:T(8,128)(2,1)S(1)}, bf16[816,128]{1,0:T(8,128)(2,1)S(1)}, u32[]{:S(2)}, u32[]{:S(2)}) collective-permute-start(bf16[816,128]{1,0:T(8,128)(2,1)S(1)} %get-tuple-element.85), channel_id=1, source_target_pairs={{0,8},{1,9},{2,10},{3,11},{4,12},{5,13},{6,14},{7,15},{8,0},{9,1},... | collective-permute-start | bytes 626696 | tf_op jit(solution)/shard_map/ppermute | solution.py:594
  48.5 5.8 %collective-permute-start.16 = (bf16[304,128]{1,0:T(8,128)(2,1)S(1)}, bf16[304,128]{1,0:T(8,128)(2,1)S(1)}, u32[]{:S(2)}, u32[]{:S(2)}) collective-permute-start(bf16[304,128]{1,0:T(8,128)(2,1)S(1)} %get-tuple-element.87), channel_id=1, source_target_pairs={{0,1},{1,0},{2,3},{3,2},{4,5},{5,4},{6,7},{7,6},{8,9},{9,8},{10,11... | collective-permute-start | bytes 233480 | tf_op jit(solution)/shard_map/ppermute | solution.py:591
  54.9 5.7 %collective-permute-start.19 = (bf16[512,128]{1,0:T(8,128)(2,1)S(1)}, bf16[512,128]{1,0:T(8,128)(2,1)S(1)}, u32[]{:S(2)}, u32[]{:S(2)}) collective-permute-start(bf16[512,128]{1,0:T(8,128)(2,1)S(1)} %shard_map.199.own_ref), channel_id=1, source_target_pairs={{0,4},{1,33},{2,6},{3,35},{4,0},{5,37},{6,2},{7,39},{8,12},{9,41},... | collective-permute-start | bytes 393224 | tf_op jit(solution)/shard_map/ppermute | solution.py:603
  58.0 5.3 %collective-permute-start.17 = (bf16[512,128]{1,0:T(8,128)(2,1)S(1)}, bf16[512,128]{1,0:T(8,128)(2,1)S(1)}, u32[]{:S(2)}, u32[]{:S(2)}) collective-permute-start(bf16[512,128]{1,0:T(8,128)(2,1)S(1)} %shard_map.199.own_ref), channel_id=1, source_target_pairs={{0,2},{1,17},{2,4},{3,19},{4,6},{5,21},{6,0},{7,23},{8,10},{9,25},... | collective-permute-start | bytes 393224 | tf_op jit(solution)/shard_map/ppermute | solution.py:603
  63.9 9.2 %collective-permute-start.25 = (bf16[1760,128]{1,0:T(8,128)(2,1)S(1)}, bf16[1760,128]{1,0:T(8,128)(2,1)S(1)}, u32[]{:S(2)}, u32[]{:S(2)}) collective-permute-start(bf16[1760,128]{1,0:T(8,128)(2,1)S(1)} %shard_map.200.refs_1_), channel_id=1, source_target_pairs={{0,32},{1,5},{2,34},{3,7},{4,36},{5,1},{6,38},{7,3},{8,40},{9,13},... | collective-permute-start | bytes 1351688 | tf_op jit(solution)/shard_map/ppermute | solution.py:603
  64.9 13.0 %collective-permute-start.23 = (bf16[1760,128]{1,0:T(8,128)(2,1)S(1)}, bf16[1760,128]{1,0:T(8,128)(2,1)S(1)}, u32[]{:S(2)}, u32[]{:S(2)}) collective-permute-start(bf16[1760,128]{1,0:T(8,128)(2,1)S(1)} %shard_map.200.refs_1_), channel_id=1, source_target_pairs={{0,48},{1,7},{2,50},{3,1},{4,52},{5,3},{6,54},{7,5},{8,56},{9,15},... | collective-permute-start | bytes 1351688 | tf_op jit(solution)/shard_map/ppermute | solution.py:603
  66.6 12.8 %collective-permute-start.21 = (bf16[1760,128]{1,0:T(8,128)(2,1)S(1)}, bf16[1760,128]{1,0:T(8,128)(2,1)S(1)}, u32[]{:S(2)}, u32[]{:S(2)}) collective-permute-start(bf16[1760,128]{1,0:T(8,128)(2,1)S(1)} %shard_map.200.refs_1_), channel_id=1, source_target_pairs={{0,16},{1,3},{2,18},{3,5},{4,20},{5,7},{6,22},{7,1},{8,24},{9,11},... | collective-permute-start | bytes 1351688 | tf_op jit(solution)/shard_map/ppermute | solution.py:603
  66.9 15.3 %collective-permute-start.20 = (bf16[1760,128]{1,0:T(8,128)(2,1)S(1)}, bf16[1760,128]{1,0:T(8,128)(2,1)S(1)}, u32[]{:S(2)}, u32[]{:S(2)}) collective-permute-start(bf16[1760,128]{1,0:T(8,128)(2,1)S(1)} %shard_map.200.refs_1_), channel_id=1, source_target_pairs={{0,1},{1,0},{2,3},{3,2},{4,5},{5,4},{6,7},{7,6},{8,9},{9,8},{10,11... | collective-permute-start | bytes 1351688 | tf_op jit(solution)/shard_map/ppermute | solution.py:591
  73.1 9.1 %collective-permute-start.26 = (bf16[1760,128]{1,0:T(8,128)(2,1)S(1)}, bf16[1760,128]{1,0:T(8,128)(2,1)S(1)}, u32[]{:S(2)}, u32[]{:S(2)}) collective-permute-start(bf16[1760,128]{1,0:T(8,128)(2,1)S(1)} %collective-permute-done.25.refs_4_), channel_id=1, source_target_pairs={{0,1},{1,0},{2,3},{3,2},{4,5},{5,4},{6,7},{7,6},{8,9},{9,8},{10,11... | collective-permute-start | bytes 1351688 | tf_op jit(solution)/shard_map/ppermute | solution.py:591
  77.9 4.4 %collective-permute-start.24 = (bf16[1760,128]{1,0:T(8,128)(2,1)S(1)}, bf16[1760,128]{1,0:T(8,128)(2,1)S(1)}, u32[]{:S(2)}, u32[]{:S(2)}) collective-permute-start(bf16[1760,128]{1,0:T(8,128)(2,1)S(1)} %collective-permute-done.23.refs_3_), channel_id=1, source_target_pairs={{0,1},{1,0},{2,3},{3,2},{4,5},{5,4},{6,7},{7,6},{8,9},{9,8},{10,11... | collective-permute-start | bytes 1351688 | tf_op jit(solution)/shard_map/ppermute | solution.py:591
  84.2 7.7 %collective-permute-start.27 = (bf16[320,128]{1,0:T(8,128)(2,1)S(1)}, bf16[320,128]{1,0:T(8,128)(2,1)S(1)}, u32[]{:S(2)}, u32[]{:S(2)}) collective-permute-start(bf16[320,128]{1,0:T(8,128)(2,1)S(1)} %get-tuple-element.91), channel_id=1, source_target_pairs={{0,64},{64,0},{128,192},{192,128},{1,65},{65,1},{129,193},{193,129... | collective-permute-start | bytes 245768 | tf_op jit(solution)/shard_map/ppermute | solution.py:644
  92.4 5.3 %collective-permute-start.28 = (bf16[256,128]{1,0:T(8,128)(2,1)S(1)}, bf16[256,128]{1,0:T(8,128)(2,1)S(1)}, u32[]{:S(2)}, u32[]{:S(2)}) collective-permute-start(bf16[256,128]{1,0:T(8,128)(2,1)S(1)} %get-tuple-element.93.own_ref), channel_id=1, source_target_pairs={{0,192},{64,128},{128,64},{192,0},{1,193},{65,129},{129,65},{193,1... | collective-permute-start | bytes 196616 | tf_op jit(solution)/shard_map/ppermute | solution.py:646
  (16 other events, 177.2 us)

commit v6 on v5

--- a/solution.py
+++ b/solution.py
@@ -158,7 +158,7 @@
         for start in range(first, first + size, CHUNK):
             part = slice(start, start + CHUNK)
             weight = dequantize_tall(values_ref[part], scales_ref, start // BLOCK)
-            sums_ref[part] = dot(weight, gradient_ref[...], 1, 1)
+            sums_ref[part] = dot(gradient_ref[...], weight, 1, 1).T
     split_by_core(where_ref[0], sums_ref, send_ref, keep_ref)
 
 

time: 100 us -> 101 us (1.010)
  no operation moved by 1% of the time
where the time goes in v6:
time: 101 us; the launch traced here: 99.5 us
  starting transfers between devices  45.8 us (45%)
  waiting for transfers between devices  27.6 us (27%)
  Pallas kernels  25.1 us (25%)
    ppermute x8, starting transfers between devices, exchange(): return lax.ppermute(value, 'row', [(i, i ^ 1) for i in range(64)])  16.8 us
    pallas_call x13, Pallas kernels, vmem_call(): pl.pallas_call(kernel, in_specs=[smem()] + [vmem] * (len(args) - 1 - unre...  13.1 us
    ppermute x9, starting transfers between devices, along(): return lax.ppermute(value, 'row', pairs)  12 us
    ppermute x9, waiting for transfers between devices, along(): return lax.ppermute(value, 'row', pairs)  10.2 us
    ppermute x8, starting transfers between devices, across(): lax.ppermute(value, 'row', [(i, i ^ other * (16 if i % 2 == 0 else 2)) fo...  7.33 us
    pallas_call x1, Pallas kernels, wide_sums(): pl.pallas_call(wide_kernel, in_specs=[smem()] + [hbm] * 9, out_specs=[vme...  5.29 us
    ppermute x2, waiting for transfers between devices, along_z(): return lax.ppermute(value, 'row', [(i, i ^ 8) for i in range(64)])  5.09 us
    ppermute x8, waiting for transfers between devices, across(): lax.ppermute(value, 'row', [(i, i ^ other * (16 if i % 2 == 0 else 2)) fo...  5.07 us
  transfers between devices with their start and end apart: 29, of which 14 were waited for; matrix products, arithmetic and copies ran while one was open for 0% of the time, Pallas kernels for 12%

profile of v6, /device:TPU:1, one launch (start us, length us, event | category | flops | bytes accessed | tf_op | source)
XLA Modules:
  0.0 99.5 jit_solution(12239317865137514897)
XLA Ops:
  0.7 5.3 %shard_map.189 = (bf16[32,104,128]{2,1,0:T(8,128)(2,1)S(1)}, bf16[32,104,128]{2,1,0:T(8,128)(2,1)S(1)}, bf16[34,104,128]{2,1,0:T(8,128)(2,1)S(1)}, bf16[34,104,128]{2,1,0:T(8,128)(2,1)S(1)}) custom-call(s32[5]{0:T(128)S(1)} %stack.23.where_ref.refs_0_, f32[2,52]{1,0:T(2,128)} %gate_scales.1, f32[2,52]{1,0:T(2,128)} %up_scales.1, ...), custom_call_target="tpu_custom_call" | custom-call | tf_op jit(solution)/shard_map/pallas_call | solution.py:170
  6.0 3.3 %collective-permute-start.1 = (bf16[34,104,128]{2,1,0:T(8,128)(2,1)S(1)}, bf16[34,104,128]{2,1,0:T(8,128)(2,1)S(1)}, u32[]{:S(2)}, u32[]{:S(2)}) collective-permute-start(bf16[34,104,128]{2,1,0:T(8,128)(2,1)S(1)} %get-tuple-element.57), channel_id=1, source_target_pairs={{0,1},{1,0},{2,3},{3,2},{4,5},{5,4},{6,7},{7,6},{8,9},{9,8},{10,11... | collective-permute-start | bytes 2715656 | tf_op jit(solution)/shard_map/ppermute | solution.py:591
  9.4 3.9 %shard_map.192 = (bf16[32,104,128]{2,1,0:T(8,128)(2,1)S(1)}, bf16[32,104,128]{2,1,0:T(8,128)(2,1)S(1)}) custom-call(s32[5]{0:T(128)S(1)} %stack.23.where_ref.refs_0_, f32[2,52]{1,0:T(2,128)} %bitcast.6, bf16[128,256]{1,0:T(8,128)(2,1)} %gradient_ref.1, bf16[6656,256]{1,0:T(8,128)(2,1)} %values_hbm.1, ...), custom_call_target="tpu_custom_call" | custom-call | tf_op jit(solution)/shard_map/pallas_call | solution.py:191
  17.7 1.7 %collective-permute-start.8 = (bf16[832,128]{1,0:T(8,128)(2,1)S(1)}, bf16[832,128]{1,0:T(8,128)(2,1)S(1)}, u32[]{:S(2)}, u32[]{:S(2)}) collective-permute-start(bf16[832,128]{1,0:T(8,128)(2,1)S(1)} %get-tuple-element.71), channel_id=1, source_target_pairs={{0,48},{1,7},{2,50},{3,5},{4,52},{5,3},{6,54},{7,1},{8,56},{9,15},... | collective-permute-start | bytes 638984 | tf_op jit(solution)/shard_map/ppermute | solution.py:606
  19.4 4.2 %collective-permute-done.3.two_got = bf16[1664,128]{1,0:T(8,128)(2,1)S(1)} collective-permute-done((bf16[1664,128]{1,0:T(8,128)(2,1)S(1)}, bf16[1664,128]{1,0:T(8,128)(2,1)S(1)}, u32[]{:S(2)}, u32[]{:S(2)}) %collective-permute-start.3) | collective-permute-done | bytes 426016 | tf_op jit(solution)/shard_map/ppermute | solution.py:606
  28.7 2.8 %shard_map.195 = (bf16[256,6656]{1,0:T(8,128)(2,1)S(1)}, bf16[256,6656]{1,0:T(8,128)(2,1)S(1)}, bf16[3,64,104]{2,1,0:T(8,128)(2,1)S(1)}) custom-call(f32[2,52]{1,0:T(2,128)S(1)} %copy-done.9, f32[2,52]{1,0:T(2,128)S(1)} %copy-done.10, bf16[256,6656]{1,0:T(8,128)(2,1)S(1)} %copy-done, bf16[256,6656]{1,0:T(8,128)(2,1)S(1)} %copy-done.1, ...), custom_call_target="tpu_custom_call" | custom-call | flops 3407872 | bytes 13631488 | tf_op jit(solution)/shard_map/pallas_call | solution.py:225
  33.0 2.2 %collective-permute-start.11 = (bf16[816,128]{1,0:T(8,128)(2,1)S(1)}, bf16[816,128]{1,0:T(8,128)(2,1)S(1)}, u32[]{:S(2)}, u32[]{:S(2)}) collective-permute-start(bf16[816,128]{1,0:T(8,128)(2,1)S(1)} %get-tuple-element.80), channel_id=1, source_target_pairs={{0,4},{1,33},{2,6},{3,35},{4,0},{5,37},{6,2},{7,39},{8,12},{9,41},... | collective-permute-start | bytes 626696 | tf_op jit(solution)/shard_map/ppermute | solution.py:603
  35.7 2.1 %collective-permute-start.13 = (bf16[816,128]{1,0:T(8,128)(2,1)S(1)}, bf16[816,128]{1,0:T(8,128)(2,1)S(1)}, u32[]{:S(2)}, u32[]{:S(2)}) collective-permute-start(bf16[816,128]{1,0:T(8,128)(2,1)S(1)} %get-tuple-element.82), channel_id=1, source_target_pairs={{0,6},{1,49},{2,0},{3,51},{4,2},{5,53},{6,4},{7,55},{8,14},{9,57},... | collective-permute-start | bytes 626696 | tf_op jit(solution)/shard_map/ppermute | solution.py:603
  39.4 1.8 %collective-permute-done.14.after_ref.far_expand_ref = bf16[3,64,104]{2,1,0:T(8,128)(2,1)S(1)} collective-permute-done((bf16[3,64,104]{2,1,0:T(8,128)(2,1)S(1)}, bf16[3,64,104]{2,1,0:T(8,128)(2,1)S(1)}, u32[]{:S(2)}, u32[]{:S(2)}) %collective-permute-start.14) | collective-permute-done | bytes 39968 | tf_op jit(solution)/shard_map/ppermute | solution.py:594
  43.8 3.3 %collective-permute-done.15.arrived_ref = bf16[816,128]{1,0:T(8,128)(2,1)S(1)} collective-permute-done((bf16[816,128]{1,0:T(8,128)(2,1)S(1)}, bf16[816,128]{1,0:T(8,128)(2,1)S(1)}, u32[]{:S(2)}, u32[]{:S(2)}) %collective-permute-start.15) | collective-permute-done | bytes 208928 | tf_op jit(solution)/shard_map/ppermute | solution.py:594
  47.2 1.7 %shard_map.198 = (bf16[304,128]{1,0:T(8,128)(2,1)S(1)}, f32[304,128]{1,0:T(8,128)S(1)}, f32[64,104]{1,0:T(8,128)}, f32[64,104]{1,0:T(8,128)}, f32[64,104]{1,0:T(8,128)}) custom-call(s32[5]{0:T(128)S(1)} %stack.23.where_ref.refs_0_, f32[816,128]{1,0:T(8,128)S(1)} %get-tuple-element.84.own_ref, bf16[816,128]{1,0:T(8,128)(2,1)S(1)} %collective-permute-done.15.arrived_ref, ...), custom_call_target="tpu_custom_call" | custom-call | tf_op jit(solution)/shard_map/pallas_call | solution.py:240
  48.9 4.9 %collective-permute-start.16 = (bf16[304,128]{1,0:T(8,128)(2,1)S(1)}, bf16[304,128]{1,0:T(8,128)(2,1)S(1)}, u32[]{:S(2)}, u32[]{:S(2)}) collective-permute-start(bf16[304,128]{1,0:T(8,128)(2,1)S(1)} %get-tuple-element.87), channel_id=1, source_target_pairs={{0,1},{1,0},{2,3},{3,2},{4,5},{5,4},{6,7},{7,6},{8,9},{9,8},{10,11... | collective-permute-start | bytes 233480 | tf_op jit(solution)/shard_map/ppermute | solution.py:591
  55.3 2.7 %collective-permute-start.19 = (bf16[512,128]{1,0:T(8,128)(2,1)S(1)}, bf16[512,128]{1,0:T(8,128)(2,1)S(1)}, u32[]{:S(2)}, u32[]{:S(2)}) collective-permute-start(bf16[512,128]{1,0:T(8,128)(2,1)S(1)} %shard_map.199.own_ref), channel_id=1, source_target_pairs={{0,4},{1,33},{2,6},{3,35},{4,0},{5,37},{6,2},{7,39},{8,12},{9,41},... | collective-permute-start | bytes 393224 | tf_op jit(solution)/shard_map/ppermute | solution.py:603
  65.2 1.7 %collective-permute-start.23 = (bf16[1760,128]{1,0:T(8,128)(2,1)S(1)}, bf16[1760,128]{1,0:T(8,128)(2,1)S(1)}, u32[]{:S(2)}, u32[]{:S(2)}) collective-permute-start(bf16[1760,128]{1,0:T(8,128)(2,1)S(1)} %shard_map.200.refs_1_), channel_id=1, source_target_pairs={{0,48},{1,7},{2,50},{3,1},{4,52},{5,3},{6,54},{7,5},{8,56},{9,15},... | collective-permute-start | bytes 1351688 | tf_op jit(solution)/shard_map/ppermute | solution.py:603
  67.3 3.2 %collective-permute-start.20 = (bf16[1760,128]{1,0:T(8,128)(2,1)S(1)}, bf16[1760,128]{1,0:T(8,128)(2,1)S(1)}, u32[]{:S(2)}, u32[]{:S(2)}) collective-permute-start(bf16[1760,128]{1,0:T(8,128)(2,1)S(1)} %shard_map.200.refs_1_), channel_id=1, source_target_pairs={{0,1},{1,0},{2,3},{3,2},{4,5},{5,4},{6,7},{7,6},{8,9},{9,8},{10,11... | collective-permute-start | bytes 1351688 | tf_op jit(solution)/shard_map/ppermute | solution.py:591
  70.5 3.0 %collective-permute-done.25.refs_4_ = bf16[1760,128]{1,0:T(8,128)(2,1)S(1)} collective-permute-done((bf16[1760,128]{1,0:T(8,128)(2,1)S(1)}, bf16[1760,128]{1,0:T(8,128)(2,1)S(1)}, u32[]{:S(2)}, u32[]{:S(2)}) %collective-permute-start.25) | collective-permute-done | bytes 450592 | tf_op jit(solution)/shard_map/ppermute | solution.py:603
  73.5 2.4 %collective-permute-start.26 = (bf16[1760,128]{1,0:T(8,128)(2,1)S(1)}, bf16[1760,128]{1,0:T(8,128)(2,1)S(1)}, u32[]{:S(2)}, u32[]{:S(2)}) collective-permute-start(bf16[1760,128]{1,0:T(8,128)(2,1)S(1)} %collective-permute-done.25.refs_4_), channel_id=1, source_target_pairs={{0,1},{1,0},{2,3},{3,2},{4,5},{5,4},{6,7},{7,6},{8,9},{9,8},{10,11... | collective-permute-start | bytes 1351688 | tf_op jit(solution)/shard_map/ppermute | solution.py:591
  75.9 2.3 %collective-permute-done.23.refs_3_ = bf16[1760,128]{1,0:T(8,128)(2,1)S(1)} collective-permute-done((bf16[1760,128]{1,0:T(8,128)(2,1)S(1)}, bf16[1760,128]{1,0:T(8,128)(2,1)S(1)}, u32[]{:S(2)}, u32[]{:S(2)}) %collective-permute-start.23) | collective-permute-done | bytes 450592 | tf_op jit(solution)/shard_map/ppermute | solution.py:603
  80.6 2.0 %shard_map.201 = (f32[256,128]{1,0:T(8,128)S(1)}, f32[96,128]{1,0:T(8,128)S(1)}) custom-call(s32[5]{0:T(128)S(1)} %stack.23.where_ref.refs_0_, bf16[1760,128]{1,0:T(8,128)(2,1)S(1)} %shard_map.200.refs_1_, bf16[1760,128]{1,0:T(8,128)(2,1)S(1)} %collective-permute-done.21.refs_2_, bf16[1760,128]{1,0:T(8,128)(2,1)S(1)} %collective-permute-done.23.refs_3_, ...), custom_call_target="tpu_custom_call" | custom-call | tf_op jit(solution)/shard_map/pallas_call | solution.py:240
  82.7 1.9 %shard_map.202 = (bf16[320,128]{1,0:T(8,128)(2,1)S(1)}, bf16[320,128]{1,0:T(8,128)(2,1)S(1)}) custom-call(s32[5]{0:T(128)S(1)} %stack.23.where_ref.refs_0_, bf16[1760,128]{1,0:T(8,128)(2,1)S(1)} %collective-permute-done.20.refs_1_, bf16[1760,128]{1,0:T(8,128)(2,1)S(1)} %collective-permute-done.22.refs_2_, ...), custom_call_target="tpu_custom_call" | custom-call | tf_op jit(solution)/shard_map/pallas_call | solution.py:240
  84.6 3.1 %collective-permute-start.27 = (bf16[320,128]{1,0:T(8,128)(2,1)S(1)}, bf16[320,128]{1,0:T(8,128)(2,1)S(1)}, u32[]{:S(2)}, u32[]{:S(2)}) collective-permute-start(bf16[320,128]{1,0:T(8,128)(2,1)S(1)} %get-tuple-element.91), channel_id=1, source_target_pairs={{0,64},{64,0},{128,192},{192,128},{1,65},{65,1},{129,193},{193,129... | collective-permute-start | bytes 245768 | tf_op jit(solution)/shard_map/ppermute | solution.py:644
  87.6 4.6 %collective-permute-done.27.arrived_ref = bf16[320,128]{1,0:T(8,128)(2,1)S(1)} collective-permute-done((bf16[320,128]{1,0:T(8,128)(2,1)S(1)}, bf16[320,128]{1,0:T(8,128)(2,1)S(1)}, u32[]{:S(2)}, u32[]{:S(2)}) %collective-permute-start.27) | collective-permute-done | bytes 81952 | tf_op jit(solution)/shard_map/ppermute | solution.py:644
  92.8 3.6 %collective-permute-start.28 = (bf16[256,128]{1,0:T(8,128)(2,1)S(1)}, bf16[256,128]{1,0:T(8,128)(2,1)S(1)}, u32[]{:S(2)}, u32[]{:S(2)}) collective-permute-start(bf16[256,128]{1,0:T(8,128)(2,1)S(1)} %get-tuple-element.93.own_ref), channel_id=1, source_target_pairs={{0,192},{64,128},{128,64},{192,0},{1,193},{65,129},{129,65},{193,1... | collective-permute-start | bytes 196616 | tf_op jit(solution)/shard_map/ppermute | solution.py:646
  96.3 1.8 %collective-permute-done.28.arrived_ref = bf16[256,128]{1,0:T(8,128)(2,1)S(1)} collective-permute-done((bf16[256,128]{1,0:T(8,128)(2,1)S(1)}, bf16[256,128]{1,0:T(8,128)(2,1)S(1)}, u32[]{:S(2)}, u32[]{:S(2)}) %collective-permute-start.28) | collective-permute-done | bytes 65568 | tf_op jit(solution)/shard_map/ppermute | solution.py:646
  (73 shorter events, 29.3 us)
Async XLA Ops:
  6.0 7.8 %collective-permute-start.1 = (bf16[34,104,128]{2,1,0:T(8,128)(2,1)S(1)}, bf16[34,104,128]{2,1,0:T(8,128)(2,1)S(1)}, u32[]{:S(2)}, u32[]{:S(2)}) collective-permute-start(bf16[34,104,128]{2,1,0:T(8,128)(2,1)S(1)} %get-tuple-element.57), channel_id=1, source_target_pairs={{0,1},{1,0},{2,3},{3,2},{4,5},{5,4},{6,7},{7,6},{8,9},{9,8},{10,11... | collective-permute-start | bytes 2715656 | tf_op jit(solution)/shard_map/ppermute | solution.py:591
  9.3 4.5 %collective-permute-start = (bf16[32,104,128]{2,1,0:T(8,128)(2,1)S(1)}, bf16[32,104,128]{2,1,0:T(8,128)(2,1)S(1)}, u32[]{:S(2)}, u32[]{:S(2)}) collective-permute-start(bf16[32,104,128]{2,1,0:T(8,128)(2,1)S(1)} %get-tuple-element.56), channel_id=1, source_target_pairs={{0,1},{1,0},{2,3},{3,2},{4,5},{5,4},{6,7},{7,6},{8,9},{9,8},{10,11... | collective-permute-start | bytes 2555912 | tf_op jit(solution)/shard_map/ppermute | solution.py:591
  14.9 8.7 %collective-permute-start.2 = (bf16[1856,128]{1,0:T(8,128)(2,1)S(1)}, bf16[1856,128]{1,0:T(8,128)(2,1)S(1)}, u32[]{:S(2)}, u32[]{:S(2)}) collective-permute-start(bf16[1856,128]{1,0:T(8,128)(2,1)S(1)} %get-tuple-element.60), channel_id=1, source_target_pairs={{0,16},{1,3},{2,18},{3,1},{4,20},{5,7},{6,22},{7,5},{8,24},{9,11},... | collective-permute-start | bytes 1425416 | tf_op jit(solution)/shard_map/ppermute | solution.py:606
  15.0 8.6 %collective-permute-start.3 = (bf16[1664,128]{1,0:T(8,128)(2,1)S(1)}, bf16[1664,128]{1,0:T(8,128)(2,1)S(1)}, u32[]{:S(2)}, u32[]{:S(2)}) collective-permute-start(bf16[1664,128]{1,0:T(8,128)(2,1)S(1)} %get-tuple-element.61), channel_id=1, source_target_pairs={{0,48},{1,7},{2,50},{3,5},{4,52},{5,3},{6,54},{7,1},{8,56},{9,15},... | collective-permute-start | bytes 1277960 | tf_op jit(solution)/shard_map/ppermute | solution.py:606
  17.2 8.6 %collective-permute-start.7 = (bf16[832,128]{1,0:T(8,128)(2,1)S(1)}, bf16[832,128]{1,0:T(8,128)(2,1)S(1)}, u32[]{:S(2)}, u32[]{:S(2)}) collective-permute-start(bf16[832,128]{1,0:T(8,128)(2,1)S(1)} %get-tuple-element.70), channel_id=1, source_target_pairs={{0,16},{1,3},{2,18},{3,1},{4,20},{5,7},{6,22},{7,5},{8,24},{9,11},... | collective-permute-start | bytes 638984 | tf_op jit(solution)/shard_map/ppermute | solution.py:606
  17.7 8.2 %collective-permute-start.8 = (bf16[832,128]{1,0:T(8,128)(2,1)S(1)}, bf16[832,128]{1,0:T(8,128)(2,1)S(1)}, u32[]{:S(2)}, u32[]{:S(2)}) collective-permute-start(bf16[832,128]{1,0:T(8,128)(2,1)S(1)} %get-tuple-element.71), channel_id=1, source_target_pairs={{0,48},{1,7},{2,50},{3,5},{4,52},{5,3},{6,54},{7,1},{8,56},{9,15},... | collective-permute-start | bytes 638984 | tf_op jit(solution)/shard_map/ppermute | solution.py:606
  24.3 8.0 %collective-permute-start.4 = (bf16[1024,128]{1,0:T(8,128)(2,1)S(1)}, bf16[1024,128]{1,0:T(8,128)(2,1)S(1)}, u32[]{:S(2)}, u32[]{:S(2)}) collective-permute-start(bf16[1024,128]{1,0:T(8,128)(2,1)S(1)} %get-tuple-element.64), channel_id=1, source_target_pairs={{0,48},{1,7},{2,50},{3,5},{4,52},{5,3},{6,54},{7,1},{8,56},{9,15},... | collective-permute-start | bytes 786440 | tf_op jit(solution)/shard_map/ppermute | solution.py:606
  25.8 6.5 %collective-permute-start.5 = (bf16[832,128]{1,0:T(8,128)(2,1)S(1)}, bf16[832,128]{1,0:T(8,128)(2,1)S(1)}, u32[]{:S(2)}, u32[]{:S(2)}) collective-permute-start(bf16[832,128]{1,0:T(8,128)(2,1)S(1)} %get-tuple-element.65), channel_id=1, source_target_pairs={{0,16},{1,3},{2,18},{3,1},{4,20},{5,7},{6,22},{7,5},{8,24},{9,11},... | collective-permute-start | bytes 638984 | tf_op jit(solution)/shard_map/ppermute | solution.py:606
  26.5 5.8 %collective-permute-start.9 = (bf16[416,128]{1,0:T(8,128)(2,1)S(1)}, bf16[416,128]{1,0:T(8,128)(2,1)S(1)}, u32[]{:S(2)}, u32[]{:S(2)}) collective-permute-start(bf16[416,128]{1,0:T(8,128)(2,1)S(1)} %get-tuple-element.74), channel_id=1, source_target_pairs={{0,48},{1,7},{2,50},{3,5},{4,52},{5,3},{6,54},{7,1},{8,56},{9,15},... | collective-permute-start | bytes 319496 | tf_op jit(solution)/shard_map/ppermute | solution.py:606
  33.0 8.2 %collective-permute-start.11 = (bf16[816,128]{1,0:T(8,128)(2,1)S(1)}, bf16[816,128]{1,0:T(8,128)(2,1)S(1)}, u32[]{:S(2)}, u32[]{:S(2)}) collective-permute-start(bf16[816,128]{1,0:T(8,128)(2,1)S(1)} %get-tuple-element.80), channel_id=1, source_target_pairs={{0,4},{1,33},{2,6},{3,35},{4,0},{5,37},{6,2},{7,39},{8,12},{9,41},... | collective-permute-start | bytes 626696 | tf_op jit(solution)/shard_map/ppermute | solution.py:603
  35.1 6.6 %collective-permute-start.12 = (bf16[816,128]{1,0:T(8,128)(2,1)S(1)}, bf16[816,128]{1,0:T(8,128)(2,1)S(1)}, u32[]{:S(2)}, u32[]{:S(2)}) collective-permute-start(bf16[816,128]{1,0:T(8,128)(2,1)S(1)} %get-tuple-element.81), channel_id=1, source_target_pairs={{0,2},{1,17},{2,4},{3,19},{4,6},{5,21},{6,0},{7,23},{8,10},{9,25},... | collective-permute-start | bytes 626696 | tf_op jit(solution)/shard_map/ppermute | solution.py:603
  35.7 6.0 %collective-permute-start.13 = (bf16[816,128]{1,0:T(8,128)(2,1)S(1)}, bf16[816,128]{1,0:T(8,128)(2,1)S(1)}, u32[]{:S(2)}, u32[]{:S(2)}) collective-permute-start(bf16[816,128]{1,0:T(8,128)(2,1)S(1)} %get-tuple-element.82), channel_id=1, source_target_pairs={{0,6},{1,49},{2,0},{3,51},{4,2},{5,53},{6,4},{7,55},{8,14},{9,57},... | collective-permute-start | bytes 626696 | tf_op jit(solution)/shard_map/ppermute | solution.py:603
  42.4 4.7 %collective-permute-start.15 = (bf16[816,128]{1,0:T(8,128)(2,1)S(1)}, bf16[816,128]{1,0:T(8,128)(2,1)S(1)}, u32[]{:S(2)}, u32[]{:S(2)}) collective-permute-start(bf16[816,128]{1,0:T(8,128)(2,1)S(1)} %get-tuple-element.85), channel_id=1, source_target_pairs={{0,8},{1,9},{2,10},{3,11},{4,12},{5,13},{6,14},{7,15},{8,0},{9,1},... | collective-permute-start | bytes 626696 | tf_op jit(solution)/shard_map/ppermute | solution.py:594
  48.9 5.8 %collective-permute-start.16 = (bf16[304,128]{1,0:T(8,128)(2,1)S(1)}, bf16[304,128]{1,0:T(8,128)(2,1)S(1)}, u32[]{:S(2)}, u32[]{:S(2)}) collective-permute-start(bf16[304,128]{1,0:T(8,128)(2,1)S(1)} %get-tuple-element.87), channel_id=1, source_target_pairs={{0,1},{1,0},{2,3},{3,2},{4,5},{5,4},{6,7},{7,6},{8,9},{9,8},{10,11... | collective-permute-start | bytes 233480 | tf_op jit(solution)/shard_map/ppermute | solution.py:591
  55.3 5.7 %collective-permute-start.19 = (bf16[512,128]{1,0:T(8,128)(2,1)S(1)}, bf16[512,128]{1,0:T(8,128)(2,1)S(1)}, u32[]{:S(2)}, u32[]{:S(2)}) collective-permute-start(bf16[512,128]{1,0:T(8,128)(2,1)S(1)} %shard_map.199.own_ref), channel_id=1, source_target_pairs={{0,4},{1,33},{2,6},{3,35},{4,0},{5,37},{6,2},{7,39},{8,12},{9,41},... | collective-permute-start | bytes 393224 | tf_op jit(solution)/shard_map/ppermute | solution.py:603
  58.4 5.3 %collective-permute-start.17 = (bf16[512,128]{1,0:T(8,128)(2,1)S(1)}, bf16[512,128]{1,0:T(8,128)(2,1)S(1)}, u32[]{:S(2)}, u32[]{:S(2)}) collective-permute-start(bf16[512,128]{1,0:T(8,128)(2,1)S(1)} %shard_map.199.own_ref), channel_id=1, source_target_pairs={{0,2},{1,17},{2,4},{3,19},{4,6},{5,21},{6,0},{7,23},{8,10},{9,25},... | collective-permute-start | bytes 393224 | tf_op jit(solution)/shard_map/ppermute | solution.py:603
  64.3 9.2 %collective-permute-start.25 = (bf16[1760,128]{1,0:T(8,128)(2,1)S(1)}, bf16[1760,128]{1,0:T(8,128)(2,1)S(1)}, u32[]{:S(2)}, u32[]{:S(2)}) collective-permute-start(bf16[1760,128]{1,0:T(8,128)(2,1)S(1)} %shard_map.200.refs_1_), channel_id=1, source_target_pairs={{0,32},{1,5},{2,34},{3,7},{4,36},{5,1},{6,38},{7,3},{8,40},{9,13},... | collective-permute-start | bytes 1351688 | tf_op jit(solution)/shard_map/ppermute | solution.py:603
  65.2 13.0 %collective-permute-start.23 = (bf16[1760,128]{1,0:T(8,128)(2,1)S(1)}, bf16[1760,128]{1,0:T(8,128)(2,1)S(1)}, u32[]{:S(2)}, u32[]{:S(2)}) collective-permute-start(bf16[1760,128]{1,0:T(8,128)(2,1)S(1)} %shard_map.200.refs_1_), channel_id=1, source_target_pairs={{0,48},{1,7},{2,50},{3,1},{4,52},{5,3},{6,54},{7,5},{8,56},{9,15},... | collective-permute-start | bytes 1351688 | tf_op jit(solution)/shard_map/ppermute | solution.py:603
  67.0 12.8 %collective-permute-start.21 = (bf16[1760,128]{1,0:T(8,128)(2,1)S(1)}, bf16[1760,128]{1,0:T(8,128)(2,1)S(1)}, u32[]{:S(2)}, u32[]{:S(2)}) collective-permute-start(bf16[1760,128]{1,0:T(8,128)(2,1)S(1)} %shard_map.200.refs_1_), channel_id=1, source_target_pairs={{0,16},{1,3},{2,18},{3,5},{4,20},{5,7},{6,22},{7,1},{8,24},{9,11},... | collective-permute-start | bytes 1351688 | tf_op jit(solution)/shard_map/ppermute | solution.py:603
  67.3 15.3 %collective-permute-start.20 = (bf16[1760,128]{1,0:T(8,128)(2,1)S(1)}, bf16[1760,128]{1,0:T(8,128)(2,1)S(1)}, u32[]{:S(2)}, u32[]{:S(2)}) collective-permute-start(bf16[1760,128]{1,0:T(8,128)(2,1)S(1)} %shard_map.200.refs_1_), channel_id=1, source_target_pairs={{0,1},{1,0},{2,3},{3,2},{4,5},{5,4},{6,7},{7,6},{8,9},{9,8},{10,11... | collective-permute-start | bytes 1351688 | tf_op jit(solution)/shard_map/ppermute | solution.py:591
  73.5 9.1 %collective-permute-start.26 = (bf16[1760,128]{1,0:T(8,128)(2,1)S(1)}, bf16[1760,128]{1,0:T(8,128)(2,1)S(1)}, u32[]{:S(2)}, u32[]{:S(2)}) collective-permute-start(bf16[1760,128]{1,0:T(8,128)(2,1)S(1)} %collective-permute-done.25.refs_4_), channel_id=1, source_target_pairs={{0,1},{1,0},{2,3},{3,2},{4,5},{5,4},{6,7},{7,6},{8,9},{9,8},{10,11... | collective-permute-start | bytes 1351688 | tf_op jit(solution)/shard_map/ppermute | solution.py:591
  78.2 4.4 %collective-permute-start.24 = (bf16[1760,128]{1,0:T(8,128)(2,1)S(1)}, bf16[1760,128]{1,0:T(8,128)(2,1)S(1)}, u32[]{:S(2)}, u32[]{:S(2)}) collective-permute-start(bf16[1760,128]{1,0:T(8,128)(2,1)S(1)} %collective-permute-done.23.refs_3_), channel_id=1, source_target_pairs={{0,1},{1,0},{2,3},{3,2},{4,5},{5,4},{6,7},{7,6},{8,9},{9,8},{10,11... | collective-permute-start | bytes 1351688 | tf_op jit(solution)/shard_map/ppermute | solution.py:591
  84.6 7.6 %collective-permute-start.27 = (bf16[320,128]{1,0:T(8,128)(2,1)S(1)}, bf16[320,128]{1,0:T(8,128)(2,1)S(1)}, u32[]{:S(2)}, u32[]{:S(2)}) collective-permute-start(bf16[320,128]{1,0:T(8,128)(2,1)S(1)} %get-tuple-element.91), channel_id=1, source_target_pairs={{0,64},{64,0},{128,192},{192,128},{1,65},{65,1},{129,193},{193,129... | collective-permute-start | bytes 245768 | tf_op jit(solution)/shard_map/ppermute | solution.py:644
  92.8 5.3 %collective-permute-start.28 = (bf16[256,128]{1,0:T(8,128)(2,1)S(1)}, bf16[256,128]{1,0:T(8,128)(2,1)S(1)}, u32[]{:S(2)}, u32[]{:S(2)}) collective-permute-start(bf16[256,128]{1,0:T(8,128)(2,1)S(1)} %get-tuple-element.93.own_ref), channel_id=1, source_target_pairs={{0,192},{64,128},{128,64},{192,0},{1,193},{65,129},{129,65},{193,1... | collective-permute-start | bytes 196616 | tf_op jit(solution)/shard_map/ppermute | solution.py:646
  (16 other events, 177.3 us)
